TPU v7x, 32 devices: a whole 2x2x4 slice. The times are simulated.
32 devices in a mesh: dp: 4 (over y, x), fsdp: 8 (over z, core).
Axes of the slice: x: 2, y: 2, z: 4, core: 2. Of those that a mesh axis runs over, the one named last changes fastest.
Arguments:
- tokens: bfloat16 [64, 512, 768], P(('dp', 'fsdp')), may hold values from -6 to 6
- w_query: float32 [768, 768], P(('dp', 'fsdp')), may hold values from -0.21875 to 0.21875
- b_query: float32 [768], P(('dp', 'fsdp')), may hold values from -4 to 4
- w_key: float32 [768, 768], P(('dp', 'fsdp')), may hold values from -0.21875 to 0.21875
- w_value: float32 [768, 768], P(('dp', 'fsdp')), may hold values from -0.21875 to 0.21875
- b_value: float32 [768], P(('dp', 'fsdp')), may hold values from -4 to 4
- w_out: float32 [768, 768], P(('dp', 'fsdp')), may hold values from -1.75 to 1.75
- b_out: float32 [768], P(('dp', 'fsdp')), may hold values from -4 to 4
- gain_one: float32 [768], P(('dp', 'fsdp')), may hold values from 0.5 to 1.5
- shift_one: float32 [768], P(('dp', 'fsdp')), may hold values from -4 to 4
- w_up: float32 [768, 3072], P(('dp', 'fsdp')), may hold values from -0.21875 to 0.21875
- b_up: float32 [3072], P(('dp', 'fsdp')), may hold values from -4 to 4
- w_down: float32 [3072, 768], P(('dp', 'fsdp')), may hold values from -0.109375 to 0.109375
- b_down: float32 [768], P(('dp', 'fsdp')), may hold values from -4 to 4
- gain_two: float32 [768], P(('dp', 'fsdp')), may hold values from 0.5 to 1.5
- shift_two: float32 [768], P(('dp', 'fsdp')), may hold values from -4 to 4
- w_proj: float32 [768, 128], P(('dp', 'fsdp')), may hold values from -0.21875 to 0.21875
- segment_ids: int32 [64, 512], P(('dp', 'fsdp')), may hold values from 0 to 8, as said below
- row_lengths: int32 [64], P(('dp', 'fsdp')), may hold values from 490 to 512, as said below
- teacher_index: int32 [64, 8], P(('dp', 'fsdp')), may hold values from 0 to 1023
- teacher_table: float32 [1024], replicated, may hold values from -6 to 6
Outputs:
- losses: float32 [64], P(('dp', 'fsdp'))
- embeddings: float32 [64, 512, 128], P(('dp', 'fsdp'))
- grad_tokens: float32 [64, 512, 768], P(('dp', 'fsdp'))
- grad_w_query: float32 [768, 768], P(('dp', 'fsdp'))
- grad_b_query: float32 [768], P(('dp', 'fsdp'))
- grad_w_key: float32 [768, 768], P(('dp', 'fsdp'))
- grad_w_value: float32 [768, 768], P(('dp', 'fsdp'))
- grad_b_value: float32 [768], P(('dp', 'fsdp'))
- grad_w_out: float32 [768, 768], P(('dp', 'fsdp'))
- grad_b_out: float32 [768], P(('dp', 'fsdp'))
- grad_gain_one: float32 [768], P(('dp', 'fsdp'))
- grad_shift_one: float32 [768], P(('dp', 'fsdp'))
- grad_w_up: float32 [768, 3072], P(('dp', 'fsdp'))
- grad_b_up: float32 [3072], P(('dp', 'fsdp'))
- grad_w_down: float32 [3072, 768], P(('dp', 'fsdp'))
- grad_b_down: float32 [768], P(('dp', 'fsdp'))
- grad_gain_two: float32 [768], P(('dp', 'fsdp'))
- grad_shift_two: float32 [768], P(('dp', 'fsdp'))
- grad_w_proj: float32 [768, 128], P(('dp', 'fsdp'))
Inputs may be any that keep to these rules, and one draw needn't show every extreme that they name: `segment_ids`: positions below 32 hold 0, the query; the other positions hold the passage numbers 1 to 8 in rising order, each passage a run of consecutive positions. `row_lengths`: padding lies inside a row's last passage, which keeps at least half of its positions live; the first row has no padding.
All inputs are finite; a program needn't handle non-finite values.
Results may differ from a plain program's by a relative error of at most 0.024.
Values may be sent and summed in bfloat16 or wider, within the bound.
A program may use at most 192 MiB of HBM per device.

v0:
```python
import math

import jax
import jax.numpy as jnp
from jax import lax
from jax.sharding import PartitionSpec as P

HEADS = 12
HEAD = 64
SEQ = 512
QLEN = 32
NPASS = 8
TABLE = 1024


NORM_EPS = 1e-12
UNIT_EPS = 1e-12
SOFTNESS = 0.1
MASK_FILL = -1000000000.0
ROOT_HALF = 0.7071067811865476
DENSITY_SCALE = 0.3989422804014327


def matmul(left, right):
    return jnp.dot(left, right, preferred_element_type=jnp.float32)


def over_rows(left, right):
    return lax.dot_general(
        left, right, (((0,), (0,)), ((), ())), preferred_element_type=jnp.float32
    )


def against(left, right):
    return lax.dot_general(
        left, right, (((1,), (1,)), ((), ())), preferred_element_type=jnp.float32
    )


def normalise(mixed, gain, shift):
    centred = mixed - jnp.mean(mixed, -1, keepdims=True)
    scaled = lax.rsqrt(jnp.mean(centred * centred, -1, keepdims=True) + NORM_EPS)
    normed = centred * scaled
    return (normed * gain + shift, normed, scaled)


def normalise_back(grad_out, normed, scaled, gain):
    inner = grad_out * gain
    grad_in = scaled * (
        inner
        - jnp.mean(inner, -1, keepdims=True)
        - normed * jnp.mean(inner * normed, -1, keepdims=True)
    )
    return (grad_in, jnp.sum(grad_out * normed, 0), jnp.sum(grad_out, 0))


def gelu_exact(upward):
    return 0.5 * upward * (1.0 + lax.erf(upward * ROOT_HALF))


def gelu_slope(upward):
    return (
        0.5 * (1.0 + lax.erf(upward * ROOT_HALF))
        + upward * jnp.exp(-0.5 * upward * upward) * DENSITY_SCALE
    )


def split_heads(matrix, rows_dev):
    return (
        matrix.reshape(rows_dev, SEQ, HEADS, HEAD)
        .transpose(0, 2, 1, 3)
        .reshape(rows_dev * HEADS, SEQ, HEAD)
    )


def join_heads(stacked, rows_dev):
    return (
        stacked.reshape(rows_dev, HEADS, SEQ, HEAD)
        .transpose(0, 2, 1, 3)
        .reshape(rows_dev * SEQ, HEADS * HEAD)
    )


def collect(sent):
    return (
        lax.all_gather(sent[0], ("dp", "fsdp"), axis=0, tiled=True),
        lax.all_gather(sent[1], ("dp", "fsdp"), axis=0, tiled=True),
        lax.all_gather(sent[2], ("dp", "fsdp"), axis=0, tiled=True),
        lax.all_gather(sent[3], ("dp", "fsdp"), axis=0, tiled=True),
        lax.all_gather(sent[4], ("dp", "fsdp"), axis=0, tiled=True),
        lax.all_gather(sent[5], ("dp", "fsdp"), axis=0, tiled=True),
        lax.all_gather(sent[6], ("dp", "fsdp"), axis=0, tiled=True),
        lax.all_gather(sent[7], ("dp", "fsdp"), axis=0, tiled=True),
        lax.all_gather(sent[8], ("dp", "fsdp"), axis=0, tiled=True),
        lax.all_gather(sent[9], ("dp", "fsdp"), axis=0, tiled=True),
        lax.all_gather(sent[10], ("dp", "fsdp"), axis=0, tiled=True),
        lax.all_gather(sent[11], ("dp", "fsdp"), axis=0, tiled=True),
        lax.all_gather(sent[12], ("dp", "fsdp"), axis=0, tiled=True),
        lax.all_gather(sent[13], ("dp", "fsdp"), axis=0, tiled=True),
        lax.all_gather(sent[14], ("dp", "fsdp"), axis=0, tiled=True),
        lax.all_gather(sent[15], ("dp", "fsdp"), axis=0, tiled=True),
    )


def spread_grads(terms):
    return (
        lax.psum_scatter(terms[0], ("dp", "fsdp"), scatter_dimension=0, tiled=True),
        lax.psum_scatter(terms[1], ("dp", "fsdp"), scatter_dimension=0, tiled=True),
        lax.psum_scatter(terms[2], ("dp", "fsdp"), scatter_dimension=0, tiled=True),
        lax.psum_scatter(terms[3], ("dp", "fsdp"), scatter_dimension=0, tiled=True),
        lax.psum_scatter(terms[4], ("dp", "fsdp"), scatter_dimension=0, tiled=True),
        lax.psum_scatter(terms[5], ("dp", "fsdp"), scatter_dimension=0, tiled=True),
        lax.psum_scatter(terms[6], ("dp", "fsdp"), scatter_dimension=0, tiled=True),
        lax.psum_scatter(terms[7], ("dp", "fsdp"), scatter_dimension=0, tiled=True),
        lax.psum_scatter(terms[8], ("dp", "fsdp"), scatter_dimension=0, tiled=True),
        lax.psum_scatter(terms[9], ("dp", "fsdp"), scatter_dimension=0, tiled=True),
        lax.psum_scatter(terms[10], ("dp", "fsdp"), scatter_dimension=0, tiled=True),
        lax.psum_scatter(terms[11], ("dp", "fsdp"), scatter_dimension=0, tiled=True),
        lax.psum_scatter(terms[12], ("dp", "fsdp"), scatter_dimension=0, tiled=True),
        lax.psum_scatter(terms[13], ("dp", "fsdp"), scatter_dimension=0, tiled=True),
        lax.psum_scatter(terms[14], ("dp", "fsdp"), scatter_dimension=0, tiled=True),
        lax.psum_scatter(terms[15], ("dp", "fsdp"), scatter_dimension=0, tiled=True),
    )


def body(
    tokens,
    w_query,
    b_query,
    w_key,
    w_value,
    b_value,
    w_out,
    b_out,
    gain_one,
    shift_one,
    w_up,
    b_up,
    w_down,
    b_down,
    gain_two,
    shift_two,
    w_proj,
    segment_ids,
    row_lengths,
    teacher_index,
    teacher_table,
):
    rows_dev = tokens.shape[0]
    width = tokens.shape[2]
    scale = 1.0 / math.sqrt(HEAD)
    shards = (
        w_query,
        b_query,
        w_key,
        w_value,
        b_value,
        w_out,
        b_out,
        gain_one,
        shift_one,
        w_up,
        b_up,
        w_down,
        b_down,
        gain_two,
        shift_two,
        w_proj,
    )
    sent = tuple((member.astype(jnp.bfloat16) for member in shards))
    gathered = collect(sent)
    (
        query_mat,
        query_bias,
        key_mat,
        value_mat,
        value_bias,
        out_mat,
        out_bias,
        gain_first,
        shift_first,
        up_mat,
        up_bias,
        down_mat,
        down_bias,
        gain_second,
        shift_second,
        proj_mat,
    ) = gathered

    def visibility(item_index):
        row_index = item_index // HEADS
        segment_row = lax.dynamic_index_in_dim(segment_ids, row_index, 0, keepdims=False)
        length_row = lax.dynamic_index_in_dim(row_lengths, row_index, 0, keepdims=False)
        positions = jnp.arange(SEQ, dtype=jnp.int32)
        return (segment_row[:, None] == segment_row[None, :]) & (positions[None, :] < length_row)

    def attend(inputs):
        query_h, key_h, value_h, item_index = inputs
        scores = jnp.where(visibility(item_index), against(query_h, key_h) * scale, MASK_FILL)
        peak = jnp.max(scores, -1, keepdims=True)
        shifted = jnp.exp(scores - peak)
        totals = jnp.sum(shifted, -1, keepdims=True)
        chances = (shifted / totals).astype(jnp.bfloat16)
        context_h = matmul(chances, value_h).astype(jnp.bfloat16)
        return (context_h, (peak + jnp.log(totals))[:, 0])

    def attend_back(inputs):
        query_h, key_h, value_h, grad_h, logsum, item_index = inputs
        scores = jnp.where(visibility(item_index), against(query_h, key_h) * scale, MASK_FILL)
        chances = jnp.exp(scores - logsum[:, None])
        d_chances = against(grad_h, value_h)
        rowdot = jnp.sum(chances * d_chances, -1, keepdims=True)
        d_scores = (chances * (d_chances - rowdot)).astype(jnp.bfloat16)
        d_query_h = (matmul(d_scores, key_h) * scale).astype(jnp.bfloat16)
        d_key_h = (over_rows(d_scores, query_h) * scale).astype(jnp.bfloat16)
        d_value_h = over_rows(chances.astype(jnp.bfloat16), grad_h).astype(jnp.bfloat16)
        return (d_query_h, d_key_h, d_value_h)

    flat = tokens.reshape(rows_dev * SEQ, width)
    queries = (matmul(flat, query_mat) + query_bias.astype(jnp.float32)).astype(jnp.bfloat16)
    keys_all = matmul(flat, key_mat).astype(jnp.bfloat16)
    values = (matmul(flat, value_mat) + value_bias.astype(jnp.float32)).astype(jnp.bfloat16)
    query_heads = split_heads(queries, rows_dev)
    key_heads = split_heads(keys_all, rows_dev)
    value_heads = split_heads(values, rows_dev)
    items = jnp.arange(rows_dev * HEADS, dtype=jnp.int32)
    context_heads, logsums = lax.map(attend, (query_heads, key_heads, value_heads, items))
    context_low = join_heads(context_heads, rows_dev)
    branch_one = matmul(context_low, out_mat) + out_bias.astype(jnp.float32)
    mid_one = flat.astype(jnp.float32) + branch_one
    hidden_one, normed_one, scaled_one = normalise(
        mid_one, gain_first.astype(jnp.float32), shift_first.astype(jnp.float32)
    )
    hidden_one_low = hidden_one.astype(jnp.bfloat16)
    upward = matmul(hidden_one_low, up_mat) + up_bias.astype(jnp.float32)
    activated = gelu_exact(upward).astype(jnp.bfloat16)
    branch_two = matmul(activated, down_mat) + down_bias.astype(jnp.float32)
    hidden_two, normed_two, scaled_two = normalise(
        hidden_one + branch_two, gain_second.astype(jnp.float32), shift_second.astype(jnp.float32)
    )
    hidden_two_low = hidden_two.astype(jnp.bfloat16)
    raw_embed = matmul(hidden_two_low, proj_mat)
    inverse = lax.rsqrt(jnp.sum(raw_embed * raw_embed, -1, keepdims=True) + UNIT_EPS)
    embeddings = raw_embed * inverse
    embed_dim = embeddings.shape[1]
    embed_low = embeddings.astype(jnp.bfloat16).reshape(rows_dev, SEQ, embed_dim)
    query_low = embed_low[:, :QLEN]
    similar = jnp.einsum("rqc,rsc->rqs", query_low, embed_low, preferred_element_type=jnp.float32)
    positions = jnp.arange(SEQ, dtype=jnp.int32)
    live = positions[None, :] < row_lengths[:, None]
    passages = jnp.arange(1, NPASS + 1, dtype=jnp.int32)
    member = (segment_ids[:, None, :] == passages[None, :, None]) & live[:, None, :]
    masked = jnp.where(member[:, None], similar[:, :, None, :] / SOFTNESS, MASK_FILL)
    peak = jnp.max(masked, -1, keepdims=True)
    shifted = jnp.exp(masked - peak)
    totals = jnp.sum(shifted, -1, keepdims=True)
    student = SOFTNESS * jnp.sum(peak[..., 0] + jnp.log(totals[..., 0]), axis=1)
    choose = teacher_index[..., None] == jnp.arange(TABLE, dtype=jnp.int32)
    teacher = jnp.sum(jnp.where(choose, teacher_table, 0.0), -1)
    teacher_logp = jax.nn.log_softmax(teacher, axis=-1)
    student_logp = jax.nn.log_softmax(student, axis=-1)
    losses = jnp.sum(jnp.exp(teacher_logp) * (teacher_logp - student_logp), -1)
    again = collect(sent)
    (
        query_back,
        query_bias_back,
        key_back,
        value_back,
        value_bias_back,
        out_back,
        out_bias_back,
        gain_first_back,
        shift_first_back,
        up_back,
        up_bias_back,
        down_back,
        down_bias_back,
        gain_second_back,
        shift_second_back,
        proj_back,
    ) = again
    d_student = jnp.exp(student_logp) - jnp.exp(teacher_logp)
    spread_weights = shifted / totals
    d_similar = jnp.einsum("rp,rqps->rqs", d_student, spread_weights).astype(jnp.bfloat16)
    d_embed = jnp.einsum("rqs,rqc->rsc", d_similar, query_low, preferred_element_type=jnp.float32)
    d_query_part = jnp.einsum(
        "rqs,rsc->rqc", d_similar, embed_low, preferred_element_type=jnp.float32
    )
    d_embed = jnp.concatenate([d_embed[:, :QLEN] + d_query_part, d_embed[:, QLEN:]], 1).reshape(
        rows_dev * SEQ, embed_dim
    )
    d_raw = (
        inverse * (d_embed - embeddings * jnp.sum(d_embed * embeddings, -1, keepdims=True))
    ).astype(jnp.bfloat16)
    grad_proj = over_rows(hidden_two_low, d_raw)
    d_hidden_two = against(d_raw, proj_back)
    d_mid_two, grad_gain_second, grad_shift_second = normalise_back(
        d_hidden_two, normed_two, scaled_two, gain_second_back.astype(jnp.float32)
    )
    d_branch_two = d_mid_two.astype(jnp.bfloat16)
    grad_down = over_rows(activated, d_branch_two)
    grad_down_bias = jnp.sum(d_branch_two, 0, dtype=jnp.float32)
    d_upward = (against(d_branch_two, down_back) * gelu_slope(upward)).astype(jnp.bfloat16)
    grad_up = over_rows(hidden_one_low, d_upward)
    grad_up_bias = jnp.sum(d_upward, 0, dtype=jnp.float32)
    d_hidden_one = d_mid_two + against(d_upward, up_back)
    d_mid_one, grad_gain_first, grad_shift_first = normalise_back(
        d_hidden_one, normed_one, scaled_one, gain_first_back.astype(jnp.float32)
    )
    d_branch_one = d_mid_one.astype(jnp.bfloat16)
    grad_out = over_rows(context_low, d_branch_one)
    grad_out_bias = jnp.sum(d_branch_one, 0, dtype=jnp.float32)
    d_context = against(d_branch_one, out_back).astype(jnp.bfloat16)
    d_context_heads = split_heads(d_context, rows_dev)
    d_query_heads, d_key_heads, d_value_heads = lax.map(
        attend_back, (query_heads, key_heads, value_heads, d_context_heads, logsums, items)
    )
    d_queries = join_heads(d_query_heads, rows_dev)
    d_keys = join_heads(d_key_heads, rows_dev)
    d_values = join_heads(d_value_heads, rows_dev)
    grad_query = over_rows(flat, d_queries)
    grad_query_bias = jnp.sum(d_queries, 0, dtype=jnp.float32)
    grad_key = over_rows(flat, d_keys)
    grad_value = over_rows(flat, d_values)
    grad_value_bias = jnp.sum(d_values, 0, dtype=jnp.float32)
    grad_input = (
        d_mid_one
        + against(d_queries, query_back)
        + against(d_keys, key_back)
        + against(d_values, value_back)
    )
    terms = (
        grad_query,
        grad_query_bias,
        grad_key,
        grad_value,
        grad_value_bias,
        grad_out,
        grad_out_bias,
        grad_gain_first,
        grad_shift_first,
        grad_up,
        grad_up_bias,
        grad_down,
        grad_down_bias,
        grad_gain_second,
        grad_shift_second,
        grad_proj,
    )
    owned = spread_grads(terms)
    return (
        losses,
        embeddings.reshape(rows_dev, SEQ, embed_dim),
        grad_input.reshape(rows_dev, SEQ, width),
        owned[0],
        owned[1],
        owned[2],
        owned[3],
        owned[4],
        owned[5],
        owned[6],
        owned[7],
        owned[8],
        owned[9],
        owned[10],
        owned[11],
        owned[12],
        owned[13],
        owned[14],
        owned[15],
    )


def solution(mesh):
    in_specs = (
        P(("dp", "fsdp"), None, None),
        P(("dp", "fsdp"), None),
        P(("dp", "fsdp")),
        P(("dp", "fsdp"), None),
        P(("dp", "fsdp"), None),
        P(("dp", "fsdp")),
        P(("dp", "fsdp"), None),
        P(("dp", "fsdp")),
        P(("dp", "fsdp")),
        P(("dp", "fsdp")),
        P(("dp", "fsdp"), None),
        P(("dp", "fsdp")),
        P(("dp", "fsdp"), None),
        P(("dp", "fsdp")),
        P(("dp", "fsdp")),
        P(("dp", "fsdp")),
        P(("dp", "fsdp"), None),
        P(("dp", "fsdp"), None),
        P(("dp", "fsdp")),
        P(("dp", "fsdp"), None),
        P(),
    )
    out_specs = (
        P(("dp", "fsdp")),
        P(("dp", "fsdp"), None, None),
        P(("dp", "fsdp"), None, None),
        P(("dp", "fsdp"), None),
        P(("dp", "fsdp")),
        P(("dp", "fsdp"), None),
        P(("dp", "fsdp"), None),
        P(("dp", "fsdp")),
        P(("dp", "fsdp"), None),
        P(("dp", "fsdp")),
        P(("dp", "fsdp")),
        P(("dp", "fsdp")),
        P(("dp", "fsdp"), None),
        P(("dp", "fsdp")),
        P(("dp", "fsdp"), None),
        P(("dp", "fsdp")),
        P(("dp", "fsdp")),
        P(("dp", "fsdp")),
        P(("dp", "fsdp"), None),
    )
    return jax.shard_map(body, mesh=mesh, in_specs=in_specs, out_specs=out_specs, check_vma=False)
```

profile of v0, /device:TPU:0, one launch (start us, length us, event | category | flops | bytes accessed | tf_op | source)
XLA Modules:
  0.0 1398.7 jit_solution(7596296346658523675)
XLA Ops:
  24.8 42.6 %all-reduce.20 = (bf16[768]{0:T(1024)(128)(2,1)S(1)}, bf16[768]{0:T(1024)(128)(2,1)S(1)}, bf16[768]{0:T(1024)(128)(2,1)S(1)}, bf16[768]{0:T(1024)(128)(2,1)S(1)}...) all-reduce(bf16[768]{0:T(1024)(128)(2,1)S(1)} %dynamic-update-slice, ...), channel_id=1, replica_groups=mesh['dp'=4,'fsdp'=8] {'dp','fsdp'}, use_global_device_ids=true, to_apply=%add | all-reduce | flops 9216 | bytes 36864
  68.2 41.0 %all_gather.72 = bf16[768,128]{1,0:T(8,128)(2,1)S(1)} all-gather(bf16[24,128]{1,0:T(8,128)(2,1)S(1)} %convert_element_type.209), channel_id=1, replica_groups=mesh['dp'=4,'fsdp'=8] {'dp','fsdp'}, dimensions={0}, use_global_device_ids=true | all-gather | bytes 202752 | tf_op jit(solution)/shard_map/all_gather | solution.py:101
  121.8 3.8 all-gather.11.cloned.1.call-done
  130.3 3.4 copy.153
  133.7 48.7 %all-gather.9.cloned.1.call-done = bf16[768,768]{1,0:T(8,128)(2,1)} async-done(((bf16[24,768]{1,0:T(8,128)(2,1)}), bf16[768,768]{1,0:T(8,128)(2,1)}) %all-gather.9.cloned.1.call-update) | async-done | bytes 1179664 | tf_op jit(solution)/shard_map/all_gather | solution.py:88
  190.7 191.1 %while.30 = (s32[]{:T(128)}, bf16[24,512,64]{1,2,0:T(8,128)(2,1)S(1)}, f32[24,512]{1,0:T(8,128)}, s32[24]{0:T(128)S(1)}, s32[2,512]{1,0:T(2,128)S(1)}, /*index=5...) while((s32[]{:T(128)}, ...), condition=%wide.region_6.8_spmd, body=%wide.region_3.7_spmd.sunk | while | flops 69763088 | bytes 3636521 | solution.py:228
  385.0 3.9 fusion.82
  389.5 12.8 multiply_convert_fusion.1
  402.3 8.8 fusion.83
  429.8 3.7 convert_reduce_fusion.1
  433.5 13.1 convert_reduce_fusion
  446.6 6.0 multiply_reduce_fusion.2
  460.8 3.9 reshape.271
  464.7 5.4 copy.156
  470.1 5.1 fusion.69
  479.5 311.9 %while.31 = (s32[]{:T(128)}, bf16[24,512,64]{1,2,0:T(8,128)(2,1)}, bf16[24,512,64]{1,2,0:T(8,128)(2,1)}, bf16[24,512,64]{1,2,0:T(8,128)(2,1)}, s32[24]{0:T(128)S...) while((s32[]{:T(128)}, bf16[24,512,64]{1,2,0:T(8,128)(2,1)}, ...), condition=%wide.region_23.25_spmd, body=%wide.region_21.24_spmd.sunk | while | flops 170819584 | bytes 9003329 | solution.py:316
  823.8 10.7 fusion.76
  836.5 10.3 fusion.72
  850.9 4.1 convert_reduce_fusion.3
  855.1 40.3 %all-reduce.19 = (f32[768]{0:T(1024)S(1)}, f32[768]{0:T(1024)S(1)}, f32[768]{0:T(1024)S(1)}, f32[768]{0:T(1024)S(1)}, f32[768]{0:T(1024)S(1)}, /*index=5*/f32[30...) all-reduce(f32[768]{0:T(1024)S(1)} %reduce_sum.259, ...), channel_id=3, replica_groups=mesh['dp'=4,'fsdp'=8] {'dp','fsdp'}, use_global_device_ids=true, to_apply=%region_26.28.clone | all-reduce | flops 9216 | bytes 73728
  909.4 95.5 %reduce-scatter.24.cloned.1.call-done = f32[24,768]{1,0:T(8,128)} async-done(((f32[768,768]{1,0:T(8,128)}), f32[24,768]{1,0:T(8,128)}) %reduce-scatter.24.cloned.1.call-update) | async-done | bytes 73744
  1004.9 104.0 %reduce-scatter.26.cloned.1.call-done = f32[24,768]{1,0:T(8,128)} async-done(((f32[768,768]{1,0:T(8,128)}), f32[24,768]{1,0:T(8,128)}) %reduce-scatter.26.cloned.1.call-update) | async-done | bytes 73744
  1108.9 141.8 %reduce-scatter.18.cloned.1.call-done = f32[24,3072]{1,0:T(8,128)} async-done(((f32[768,3072]{1,0:T(8,128)}), f32[24,3072]{1,0:T(8,128)}) %reduce-scatter.18.cloned.1.call-update) | async-done | bytes 294928 | tf_op jit(solution)/shard_map/reduce_scatter | solution.py:116
  1250.8 141.2 %reduce-scatter.20.cloned.1.call-done = f32[96,768]{1,0:T(8,128)} async-done(((f32[3072,768]{1,0:T(8,128)}), f32[96,768]{1,0:T(8,128)}) %reduce-scatter.20.cloned.1.call-update) | async-done | bytes 294928 | tf_op jit(solution)/shard_map/reduce_scatter | solution.py:118
  (742 shorter events, 537.5 us)
Async XLA Ops:
  7.2 105.8 %all-gather.7.cloned.1.call-start = ((), (), s32[]{:S(2)}) async-start(), calls=%async_computation.7 | async-start | bytes 1216512 | tf_op jit(solution)/shard_map/all_gather | solution.py:86
  8.8 116.9 %all-gather.11.cloned.1.call-start = ((), (), s32[]{:S(2)}) async-start(), calls=%async_computation.9 | async-start | bytes 1216512 | tf_op jit(solution)/shard_map/all_gather | solution.py:89
  10.3 172.1 %all-gather.9.cloned.1.call-start = ((), (), s32[]{:S(2)}) async-start(), calls=%async_computation.8 | async-start | bytes 1216512 | tf_op jit(solution)/shard_map/all_gather | solution.py:88
  11.9 373.1 %all-gather.13.cloned.1.call-start = ((), (), s32[]{:S(2)}) async-start(), calls=%async_computation.10 | async-start | bytes 1216512 | tf_op jit(solution)/shard_map/all_gather | solution.py:91
  13.5 375.9 %all-gather.15.cloned.1.call-start = ((), (), s32[]{:S(2)}) async-start(), calls=%async_computation.11 | async-start | bytes 4866048 | tf_op jit(solution)/shard_map/all_gather | solution.py:95
  15.2 387.0 %all-gather.17.cloned.1.call-start = ((), (), s32[]{:S(2)}) async-start(), calls=%async_computation.12 | async-start | bytes 4866048 | tf_op jit(solution)/shard_map/all_gather | solution.py:97
  16.9 892.5 %reduce-scatter.28.cloned.1.call-start = ((), (), s32[]{:S(2)}) async-start(), calls=%async_computation.19 | async-start | bytes 405504
  67.4 334.9 %copy-start.22 = (f32[768]{0:T(1024)}, f32[768]{0:T(1024)S(1)}, u32[]{:S(2)}) copy-start(f32[768]{0:T(1024)S(1)} %convert_element_type.195) | copy-start | bytes 9220
  67.4 322.0 %copy-start.34 = (f32[3072]{0:T(1024)}, f32[3072]{0:T(1024)S(1)}, u32[]{:S(2)}) copy-start(f32[3072]{0:T(1024)S(1)} %convert_element_type.199) | copy-start | bytes 36868
  67.4 344.2 %copy-start.26 = (f32[768]{0:T(1024)}, f32[768]{0:T(1024)S(1)}, u32[]{:S(2)}) copy-start(f32[768]{0:T(1024)S(1)} %convert_element_type.205) | copy-start | bytes 9220
  109.2 303.0 %copy-start.18 = (bf16[768,128]{1,0:T(8,128)(2,1)}, bf16[768,128]{1,0:T(8,128)(2,1)S(1)}, u32[]{:S(2)}) copy-start(bf16[768,128]{1,0:T(8,128)(2,1)S(1)} %all_gather.72) | copy-start | bytes 589828
  118.4 7.2 copy-start.39
  130.3 52.2 %copy-start.40 = (bf16[2,512,768]{2,1,0:T(8,128)(2,1)S(1)}, bf16[2,512,768]{2,1,0:T(8,128)(2,1)}, u32[]{:S(2)}) copy-start(bf16[2,512,768]{2,1,0:T(8,128)(2,1)} %param.26) | copy-start | bytes 4718596
  429.7 479.7 %reduce-scatter.16.cloned.1.call-start = ((), (), s32[]{:S(2)}) async-start(), calls=%async_computation.13 | async-start | bytes 2433024 | tf_op jit(solution)/shard_map/reduce_scatter | solution.py:112
  429.8 16.8 %slice-start = ((s8[4718592]{0:T(1024)(128)(4,1)}), s8[4194304]{0:T(1024)(128)(4,1)S(1)}, s32[]{:S(2)}) async-start(s8[4718592]{0:T(1024)(128)(4,1)} %bitcast.270), calls=%async_computation.20 | async-start | bytes 8388608
  433.5 13.1 copy-start.11
  433.5 13.1 slice-start.1
  446.6 6.1 copy-start.7
  475.2 434.2 %reduce-scatter.22.cloned.1.call-start = ((), (), s32[]{:S(2)}) async-start(), calls=%async_computation.16 | async-start | bytes 2433024
  802.1 202.8 %reduce-scatter.24.cloned.1.call-start = ((), (), s32[]{:S(2)}) async-start(), calls=%async_computation.17 | async-start | bytes 2433024
  812.8 296.1 %reduce-scatter.26.cloned.1.call-start = ((), (), s32[]{:S(2)}) async-start(), calls=%async_computation.18 | async-start | bytes 2433024
  823.8 427.0 %reduce-scatter.18.cloned.1.call-start = ((), (), s32[]{:S(2)}) async-start(), calls=%async_computation.14 | async-start | bytes 9732096 | tf_op jit(solution)/shard_map/reduce_scatter | solution.py:116
  834.6 557.4 %reduce-scatter.20.cloned.1.call-start = ((), (), s32[]{:S(2)}) async-start(), calls=%async_computation.15 | async-start | bytes 9732096 | tf_op jit(solution)/shard_map/reduce_scatter | solution.py:118
  846.8 53.9 %copy-start.14 = (bf16[96,8,2,512]{3,1,2,0:T(8,128)(2,1)S(1)}, bf16[96,8,2,512]{3,1,2,0:T(8,128)(2,1)}, u32[]{:S(2)}) copy-start(bf16[96,8,2,512]{3,1,2,0:T(8,128)(2,1)} %copy-done.13) | copy-start | bytes 4718596
  (37 other events, 92.6 us)
Sparse Core Ops, SparseCore 0:
  11.6 56.9 all-gather.6
  72.2 53.3 all-gather.10
  129.2 53.1 all-gather.8
  185.3 53.1 all-gather.12
  241.9 62.5 all-gather.14
  308.0 62.4 all-gather.16
  429.8 93.8 reduce-scatter.27
  530.5 98.1 reduce-scatter.15
  802.2 97.9 reduce-scatter.21
  906.8 98.0 reduce-scatter.23
  1010.8 98.1 reduce-scatter.25
  1116.3 134.4 reduce-scatter.17
  1257.2 134.7 reduce-scatter.19
where the time goes:
time: 1410 us; the launch traced here: 1400 us
  waiting for transfers between devices  535 us (38%)
  matrix products  363 us (26%)
  local copies, waits for them, and re-layouts  184 us (13%)
  blocking collectives  124 us (9%)
  loops' own time  96 us (7%)
  other arithmetic  79.8 us (6%)
  between operations  15 us (1%)
    unnamed x17, waiting for transfers between devices  200 us
    reduce_scatter x1, waiting for transfers between devices, spread_grads(): lax.psum_scatter(terms[9], ('dp', 'fsdp'), scatter_dimension=0, tiled=True)  142 us
    reduce_scatter x1, waiting for transfers between devices, spread_grads(): lax.psum_scatter(terms[11], ('dp', 'fsdp'), scatter_dimension=0, tiled=True)  141 us
    dot_general x79, matrix products, against(): lax.dot_general(left, right, (((1,), (1,)), ((), ())), preferred_element_...  132 us
    dot_general x55, matrix products, over_rows(): lax.dot_general(left, right, (((0,), (0,)), ((), ())), preferred_element_...  123 us
    dot_general x55, matrix products, matmul(): return jnp.dot(left, right, preferred_element_type=jnp.float32)  106 us
    unnamed x2, blocking collectives  82.9 us
    all_gather x1, waiting for transfers between devices, collect(): lax.all_gather(sent[2], ('dp', 'fsdp'), axis=0, tiled=True)  48.7 us
  transfers between devices with their start and end apart: 13, of which 6 were waited for; matrix products, arithmetic and copies ran while one was open for 42% of the time, Pallas kernels for 0%

commit v1 on v0

--- a/solution.py
+++ b/solution.py
@@ -1,8 +1,11 @@
+import functools
 import math
 
 import jax
 import jax.numpy as jnp
 from jax import lax
+from jax.experimental import pallas as pl
+from jax.experimental.pallas import tpu as pltpu
 from jax.sharding import PartitionSpec as P
 
 HEADS = 12
@@ -123,7 +126,7 @@
     )
 
 
-def body(
+def body_whole(
     tokens,
     w_query,
     b_query,
@@ -372,6 +375,1318 @@
     )
 
 
+MESH = pl.DeviceIdType.MESH
+EXP2_SCALE = 1.4426950408889634 / math.sqrt(HEAD)
+SHARDS = 32
+CHIPS = 16
+WIDTH = 768
+HIDDEN = 3072
+EMBED = 128
+SMALL = 40
+PAIRS = HEADS // 2
+CHUNK = 256
+
+
+def fits(mesh):
+    return dict(mesh.shape) == {"dp": 4, "fsdp": 8}
+
+
+def dotted(left, right, left_dim, right_dim):
+    return lax.dot_general(
+        left,
+        right,
+        (((left_dim,), (right_dim,)), ((), ())),
+        preferred_element_type=jnp.float32,
+    )
+
+
+def part_of(start, size):
+    return pl.ds(pl.multiple_of(start * size, size), size)
+
+
+def value_of(number):
+    return number() if callable(number) else number
+
+
+def place():
+    outer = lax.axis_index("dp")
+    inner = lax.axis_index("fsdp")
+    return lax.rem(outer, 2), lax.div(outer, 2), lax.div(inner, 2), lax.rem(inner, 2)
+
+
+def device(x, y, z, c):
+    return (y * 2 + x, z * 2 + c)
+
+
+class Links:
+    def __init__(self):
+        x, y, z, c = place()
+        self.c = c
+        self.z = z
+        self.chip_own = (y * 2 + x) * 4
+        self.chip_x = (y * 2 + 1 - x) * 4
+        self.chip_y = ((1 - y) * 2 + x) * 4
+        self.chip_d = ((1 - y) * 2 + 1 - x) * 4
+        self.to_core = device(x, y, z, 1 - c)
+        self.to_x = device(1 - x, y, z, c)
+        self.to_y = device(x, 1 - y, z, c)
+        self.to_z = [None] + [device(x, y, lax.rem(z + k, 4), c) for k in (1, 2, 3)]
+        self.started = []
+
+    def greet(self):
+        barrier = pltpu.get_barrier_semaphore()
+        partners = [self.to_core, self.to_x, self.to_y] + self.to_z[1:]
+        for partner in partners:
+            pl.semaphore_signal(barrier, inc=1, device_id=partner, device_id_type=MESH)
+        pl.semaphore_wait(barrier, len(partners))
+
+    def level(self, k):
+        return lax.rem(self.z + k, 4)
+
+    def send(self, ends, sems, target):
+        def copy():
+            src, dst = ends()
+            send_sem, recv_sem = sems()
+            return pltpu.make_async_remote_copy(
+                src_ref=src,
+                dst_ref=dst,
+                send_sem=send_sem,
+                recv_sem=recv_sem,
+                device_id=target,
+                device_id_type=MESH,
+            )
+
+        copy().start()
+        self.started.append(copy)
+
+    def arrived(self, ref, sems, source):
+        pltpu.make_async_remote_copy(
+            src_ref=ref,
+            dst_ref=ref,
+            send_sem=sems[0],
+            recv_sem=sems[1],
+            device_id=source,
+            device_id_type=MESH,
+        ).wait_recv()
+
+    def finish(self, first=0):
+        for copy in self.started[first:]:
+            copy().wait_send()
+        self.started = self.started[:first]
+
+
+def rows_block(ref, rows, columns, base=0):
+    def block(core, chip, count):
+        return ref.at[
+            pl.ds(pl.multiple_of(chip * rows, rows), count * rows),
+            pl.ds(pl.multiple_of(base + core * columns, 128), columns),
+        ]
+
+    return block
+
+
+def lead_block(ref):
+    def block(core, chip, count):
+        return ref.at[core, pl.ds(chip, count)]
+
+    return block
+
+
+class Gather:
+    Z, X, Y, FX, FY, C = 0, 3, 7, 11, 13, 15
+    SEMS = 19
+
+    def __init__(self, links, block, sends, recvs, group):
+        self.links = links
+        self.block = block
+        self.sends = sends
+        self.recvs = recvs
+        self.group = group
+
+    def sems(self, index, there=None):
+        there = index if there is None else there
+        return self.sends.at[self.group, index], self.recvs.at[self.group, there]
+
+    def ship(self, chip, count, index, target, there=None):
+        def ends():
+            ref = self.block(self.links.c, value_of(chip), count)
+            return ref, ref
+
+        self.links.send(ends, lambda: self.sems(index, there), target)
+
+    def step_of(self, column, k):
+        return lambda: column + self.links.level(k)
+
+    def take(self, chip, count, index, source, core=None):
+        core = self.links.c if core is None else core
+        self.links.arrived(self.block(core, value_of(chip), count), self.sems(index), source)
+
+    def first(self):
+        n = self.links
+        own = self.step_of(n.chip_own, 0)
+        for j in (1, 2, 3):
+            self.ship(own, 1, self.Z + j - 1, n.to_z[j], self.Z + 3 - j)
+        self.ship(own, 1, self.X, n.to_x)
+        self.ship(own, 1, self.Y, n.to_y)
+
+    def second(self):
+        n = self.links
+        for k in (1, 2, 3):
+            chip = self.step_of(n.chip_own, k)
+            self.take(chip, 1, self.Z + k - 1, n.to_z[k])
+            self.ship(chip, 1, self.X + k, n.to_x)
+            self.ship(chip, 1, self.Y + k, n.to_y)
+        self.ship(n.chip_own, 4, self.C, n.to_core)
+
+    def third(self):
+        n = self.links
+        for k in (0, 1):
+            chip = self.step_of(n.chip_x, k)
+            self.take(chip, 1, self.X + k, n.to_x)
+            self.ship(chip, 1, self.FY + k, n.to_y)
+        for k in (2, 3):
+            chip = self.step_of(n.chip_y, k)
+            self.take(chip, 1, self.Y + k, n.to_y)
+            self.ship(chip, 1, self.FX + k - 2, n.to_x)
+        for k in (2, 3):
+            self.take(self.step_of(n.chip_x, k), 1, self.X + k, n.to_x)
+        self.ship(n.chip_x, 4, self.C + 1, n.to_core)
+        for k in (0, 1):
+            self.take(self.step_of(n.chip_y, k), 1, self.Y + k, n.to_y)
+        self.ship(n.chip_y, 4, self.C + 2, n.to_core)
+
+    def fourth(self):
+        n = self.links
+        for k in (0, 1):
+            self.take(self.step_of(n.chip_d, k), 1, self.FY + k, n.to_y)
+        for k in (2, 3):
+            self.take(self.step_of(n.chip_d, k), 1, self.FX + k - 2, n.to_x)
+        self.ship(n.chip_d, 4, self.C + 3, n.to_core)
+
+    def last(self):
+        n = self.links
+        for index, chip in enumerate((n.chip_own, n.chip_x, n.chip_y, n.chip_d)):
+            self.take(chip, 4, self.C + index, n.to_core, 1 - n.c)
+
+
+class Scatter:
+    C, DY, DX, OX, OY, Z, F = 0, 4, 5, 6, 8, 10, 13
+    SEMS = 14
+
+    def __init__(self, links, block, mine, rows, held, sends, recvs, group):
+        self.links = links
+        self.block = block
+        self.mine = mine
+        self.rows = rows
+        self.part, self.d_y, self.d_x, self.o_x, self.o_y, self.z_in = held
+        self.sends = sends
+        self.recvs = recvs
+        self.group = group
+        n = links
+        self.columns = (n.chip_d, n.chip_x, n.chip_y, n.chip_own)
+
+    def at(self, ref, start, count):
+        if isinstance(start, int):
+            return ref.at[pl.ds(start * self.rows, count * self.rows)]
+        return ref.at[pl.ds(pl.multiple_of(start * self.rows, self.rows), count * self.rows)]
+
+    def sems(self, index, there=None):
+        there = index if there is None else there
+        return self.sends.at[self.group, index], self.recvs.at[self.group, there]
+
+    def ship(self, ends, index, target, there=None):
+        self.links.send(ends, lambda: self.sems(index, there), target)
+
+    def ship_part(self, start, count, ref, there, index, target):
+        self.ship(
+            lambda: (self.at(self.part, value_of(start), count), self.at(ref, there, count)),
+            index,
+            target,
+        )
+
+    def take(self, ref, start, count, index, source):
+        self.links.arrived(self.at(ref, start, count), self.sems(index), source)
+
+    def add(self, count, start, *others):
+        def step(i, carry):
+            here = self.at(self.part, start + i, 1)
+            total = here[...].astype(jnp.float32)
+            for other in others:
+                total = total + other(i)[...].astype(jnp.float32)
+            here[...] = total.astype(self.part.dtype)
+            return carry
+
+        lax.fori_loop(0, count, step, 0)
+
+    def first(self):
+        n = self.links
+        for index, chip in enumerate(self.columns):
+
+            def ends(chip=chip):
+                return self.block(1 - n.c, chip, 4), self.at(self.part, chip, 4)
+
+            self.ship(ends, self.C + index, n.to_core)
+
+    def second(self):
+        n = self.links
+        for index, chip in enumerate(self.columns):
+            self.take(self.part, chip, 4, self.C + index, n.to_core)
+            self.add(4, chip, lambda i, chip=chip: self.mine(chip + i))
+            if index == 0:
+                self.ship_part(chip, 2, self.d_y, 0, self.DY, n.to_y)
+                self.ship_part(lambda chip=chip: chip + 2, 2, self.d_x, 0, self.DX, n.to_x)
+            elif index == 1:
+                self.ship_part(lambda chip=chip: chip + 2, 2, self.o_x, 2, self.OX + 1, n.to_x)
+            elif index == 2:
+                self.ship_part(chip, 2, self.o_y, 0, self.OY, n.to_y)
+
+    def third(self):
+        n = self.links
+        self.take(self.d_y, 0, 2, self.DY, n.to_y)
+        self.add(2, n.chip_x, lambda i: self.at(self.d_y, i, 1))
+        self.ship_part(n.chip_x, 2, self.o_x, 0, self.OX, n.to_x)
+        self.take(self.d_x, 0, 2, self.DX, n.to_x)
+        self.add(2, n.chip_y + 2, lambda i: self.at(self.d_x, i, 1))
+        self.ship_part(lambda: n.chip_y + 2, 2, self.o_y, 2, self.OY + 1, n.to_y)
+
+    def fourth(self):
+        n = self.links
+        self.take(self.o_x, 2, 2, self.OX + 1, n.to_x)
+        self.take(self.o_y, 0, 2, self.OY, n.to_y)
+        self.take(self.o_x, 0, 2, self.OX, n.to_x)
+        self.take(self.o_y, 2, 2, self.OY + 1, n.to_y)
+        self.add(
+            4,
+            n.chip_own,
+            lambda i: self.at(self.o_x, i, 1),
+            lambda i: self.at(self.o_y, i, 1),
+        )
+        for j in (1, 2, 3):
+
+            def ends(j=j):
+                return (
+                    self.at(self.part, n.chip_own + n.level(j), 1),
+                    self.at(self.z_in, 3 - j, 1),
+                )
+
+            self.ship(ends, self.Z + j - 1, n.to_z[j], self.Z + 3 - j)
+
+    def fifth(self):
+        n = self.links
+        total = self.at(self.part, n.chip_own + n.z, 1)[...].astype(jnp.float32)
+        for k in (1, 2, 3):
+            self.take(self.z_in, k - 1, 1, self.Z + k - 1, n.to_z[k])
+            total = total + self.at(self.z_in, k - 1, 1)[...].astype(jnp.float32)
+        return total
+
+    def trade(self, fin, fin_in):
+        n = self.links
+        rows = self.rows // 2
+        fin[...] = self.fifth()
+        self.ship(lambda: (fin.at[part_of(1 - n.c, rows)], fin_in), self.F, n.to_core)
+
+    def whole(self, fin, fin_in):
+        n = self.links
+        rows = self.rows // 2
+        n.arrived(fin_in, self.sems(self.F), n.to_core)
+        mine = fin[part_of(n.c, rows), :]
+        theirs = fin_in[...]
+        return jnp.where(n.c == 0, mine, theirs), jnp.where(n.c == 0, theirs, mine)
+
+
+def spread_lanes(parts, step):
+    lane = lax.broadcasted_iota(jnp.int32, (8, 128), 1)
+    tiles = [None] * (len(parts) * step // 128)
+
+    def add(index, value):
+        tiles[index] = value if tiles[index] is None else tiles[index] + value
+
+    for i, part in enumerate(parts):
+        part = jnp.where(lane < step, part, 0.0)
+        index, shift = i * step // 128, i * step % 128
+        rolled = pltpu.roll(part, shift, 1) if shift else part
+        if shift + step <= 128:
+            add(index, rolled)
+        else:
+            add(index, jnp.where(lane >= shift, rolled, 0.0))
+            add(index + 1, jnp.where(lane < shift, rolled, 0.0))
+    return tiles
+
+
+def pick_lanes(tiles, step, count):
+    parts = []
+    lane = lax.broadcasted_iota(jnp.int32, (8, 128), 1)
+    for i in range(count):
+        index, shift = i * step // 128, i * step % 128
+        part = pltpu.roll(tiles[index], 128 - shift, 1) if shift else tiles[index]
+        if shift + step > 128:
+            after = pltpu.roll(tiles[index + 1], 128 - shift, 1)
+            part = jnp.where(lane < 128 - shift, part, after)
+        parts.append(jnp.where(lane < step, part, 0.0))
+    return parts
+
+
+def rounded(value):
+    return value.astype(jnp.bfloat16).astype(jnp.float32)
+
+
+def segment_forms(segment_ids, row_lengths, r):
+    segment = segment_ids[r : r + 1, :].astype(jnp.float32)
+    position = lax.broadcasted_iota(jnp.int32, (1, SEQ), 1)
+    return segment, jnp.where(position < row_lengths[r], segment, -1.0)
+
+
+def upright(row):
+    return jnp.broadcast_to(row, (128, SEQ)).T[:, 0:1]
+
+
+def mask_of(rows_form, columns_form):
+    return jnp.where(upright(rows_form) == columns_form, 0.0, MASK_FILL)
+
+
+def staged(n, steps):
+    for index, step in steps.items():
+        pl.when(n == index)(step)
+
+
+def attend_pair(r, p, qkv, context, logsums, bias):
+    rows = part_of(r, SEQ)
+    columns = pl.multiple_of(p * 128, 128)
+    query = qkv[rows, pl.ds(columns, 128)]
+    key = qkv[rows, pl.ds(columns + WIDTH, 128)]
+    value = qkv[rows, pl.ds(columns + 2 * WIDTH, 128)]
+    low = lax.broadcasted_iota(jnp.int32, (SEQ, 128), 1) < HEAD
+    zero = jnp.zeros_like(key)
+    outs, sums = [], []
+    for j in range(2):
+        key_j = jnp.where(low, key, zero) if j == 0 else jnp.where(low, zero, key)
+        scores = dotted(query, key_j, 1, 1) * EXP2_SCALE + bias[rows, 0:SEQ]
+        peak = jnp.max(scores, -1, keepdims=True)
+        shifted = jnp.exp2(scores - peak)
+        total = jnp.sum(shifted, -1, keepdims=True)
+        out = dotted(shifted.astype(jnp.bfloat16), value, 1, 0)
+        outs.append(out * (1.0 / total))
+        sums.append(peak + jnp.log2(total))
+    context[rows, pl.ds(columns, 128)] = jnp.where(low, outs[0], outs[1]).astype(jnp.bfloat16)
+    turned = jnp.where(low, sums[0], sums[1]).T
+    logsums[r, p, 0:1] = turned[0:1]
+    logsums[r, p, 1:2] = turned[HEAD : HEAD + 1]
+
+
+def attend_back_pair(r, p, qkv, d_context, logsums, rowdots, bias):
+    rows = part_of(r, SEQ)
+    columns = pl.multiple_of(p * 128, 128)
+    query = qkv[rows, pl.ds(columns, 128)]
+    key = qkv[rows, pl.ds(columns + WIDTH, 128)]
+    value = qkv[rows, pl.ds(columns + 2 * WIDTH, 128)]
+    grad = d_context[rows, pl.ds(columns, 128)]
+    low = lax.broadcasted_iota(jnp.int32, (SEQ, 128), 1) < HEAD
+    zero = jnp.zeros_like(key)
+    d_query, d_key, d_value = None, [], []
+    for j in range(2):
+        pick = (lambda a: jnp.where(low, a, zero)) if j == 0 else (lambda a: jnp.where(low, zero, a))
+        key_j = pick(key)
+        scores = dotted(key_j, query, 1, 1) * EXP2_SCALE + bias[r]
+        chances = jnp.exp2(scores - logsums[r, p, j : j + 1, :])
+        d_chances = dotted(pick(value), grad, 1, 1)
+        d_scores = (chances * (d_chances - rowdots[r, p, j : j + 1, :])).astype(jnp.bfloat16)
+        d_value.append(dotted(chances.astype(jnp.bfloat16), grad, 1, 0))
+        d_key.append(dotted(d_scores, query, 1, 0))
+        term = dotted(d_scores, key_j, 0, 0)
+        d_query = term if d_query is None else d_query + term
+    scale = 1.0 / math.sqrt(HEAD)
+    low_type = jnp.bfloat16
+    qkv[rows, pl.ds(columns, 128)] = (d_query * scale).astype(low_type)
+    qkv[rows, pl.ds(columns + WIDTH, 128)] = (
+        jnp.where(low, d_key[0], d_key[1]) * scale
+    ).astype(low_type)
+    qkv[rows, pl.ds(columns + 2 * WIDTH, 128)] = jnp.where(low, d_value[0], d_value[1]).astype(
+        low_type
+    )
+
+
+def row_dots(context, d_context, rowdots):
+    shape = (8, 128)
+    head = lax.broadcasted_iota(jnp.int32, shape, 1) // HEAD
+    pick = (head == lax.broadcasted_iota(jnp.int32, shape, 0)).astype(jnp.float32)
+    for r in range(rowdots.shape[0]):
+        for p in range(PAIRS):
+            part = (slice(r * SEQ, (r + 1) * SEQ), slice(p * 128, (p + 1) * 128))
+            both = context[part].astype(jnp.float32) * d_context[part].astype(jnp.float32)
+            rowdots[r, p] = lax.dot_general(
+                pick,
+                both,
+                (((1,), (1,)), ((), ())),
+                precision=lax.Precision.HIGHEST,
+                preferred_element_type=jnp.float32,
+            )
+
+
+def norm_parts(mixed):
+    centred = mixed - jnp.mean(mixed, -1, keepdims=True)
+    scaled = lax.rsqrt(jnp.mean(centred * centred, -1, keepdims=True) + NORM_EPS)
+    return centred * scaled, scaled
+
+
+def norm_back(grad_out, normed, scaled, gain):
+    inner = grad_out * gain
+    return scaled * (
+        inner
+        - jnp.mean(inner, -1, keepdims=True)
+        - normed * jnp.mean(inner * normed, -1, keepdims=True)
+    )
+
+
+def halves(links, src, stage, sends, recvs, index):
+    rows, width = src.shape
+    columns = width // 2
+
+    def ends():
+        return src.at[:, part_of(1 - links.c, columns)], stage.at[part_of(links.c, rows), :]
+
+    links.send(ends, lambda: (sends.at[index], recvs.at[index]), links.to_core)
+    stage[part_of(links.c, rows), :] = src[:, part_of(links.c, columns)]
+
+
+def joined(links, stage, sends, recvs, index, block):
+    rows = stage.shape[0] // 2
+    here = stage.at[part_of(1 - links.c, rows), :]
+    links.arrived(here, (sends.at[index], recvs.at[index]), links.to_core)
+    block(links.c, links.chip_own + links.z, 1)[...] = stage[...].astype(jnp.bfloat16)
+
+
+def passage_loss(r, similar, live_row, teacher_index, teacher_table):
+    scores = similar * (1.0 / SOFTNESS)
+    inside, shares, student, teacher = [], [], [], []
+    for p in range(NPASS):
+        member = live_row == float(p + 1)
+        masked = jnp.where(member, scores, MASK_FILL)
+        peak = jnp.max(masked, -1, keepdims=True)
+        shifted = jnp.exp(masked - peak)
+        total = jnp.sum(shifted, -1, keepdims=True)
+        inside.append(jnp.where(member, shifted, 0.0))
+        shares.append(1.0 / total)
+        student.append(SOFTNESS * jnp.sum(peak + jnp.log(total), axis=0, keepdims=True))
+        teacher.append(jnp.full((1, 1), teacher_table[teacher_index[r, p]], jnp.float32))
+
+    def log_softmax(values):
+        peak = functools.reduce(jnp.maximum, values)
+        total = sum(jnp.exp(value - peak) for value in values)
+        return [value - peak - jnp.log(total) for value in values]
+
+    student = log_softmax(student)
+    teacher = log_softmax(teacher)
+    loss = sum(jnp.exp(t) * (t - s) for t, s in zip(teacher, student))
+    d_similar = sum(
+        part * (share * (jnp.exp(s) - jnp.exp(t)))
+        for part, share, s, t in zip(inside, shares, student, teacher)
+    )
+    return loss, d_similar
+
+
+def first_kernel(*refs):
+    (
+        tokens,
+        w_query,
+        w_key,
+        w_value,
+        w_out,
+        w_up,
+        w_down,
+        w_proj,
+        *vector_refs,
+        b_up,
+        segment_ids,
+        row_lengths,
+        teacher_index,
+        teacher_table,
+    ) = refs[:21]
+    (
+        losses,
+        embeddings,
+        attn_hbm,
+        up_hbm,
+        down_hbm,
+        turned_hbm,
+        qkv_hbm,
+        context_hbm,
+        low_one_hbm,
+        normed_one_hbm,
+        slope_hbm,
+        d_mid_hbm,
+        d_branch_hbm,
+        grad_down_hbm,
+        scaled_one,
+        vectors,
+        grad_vectors,
+        grad_proj,
+        logsums,
+    ) = refs[21:40]
+    (
+        attn_mat,
+        up_mat,
+        down_mat,
+        turned,
+        qkv,
+        context,
+        low_one,
+        normed_one,
+        slope,
+        activated,
+        d_mid,
+        d_branch,
+        grad_down,
+        small_all,
+        cat_attn,
+        stage_attn,
+        stage_out,
+        stage_up,
+        stage_down,
+        proj,
+        up_bias,
+        normed_two,
+        scaled_two,
+        low_two,
+        sends,
+        recvs,
+        half_sends,
+        half_recvs,
+        local_sems,
+        grad_sems,
+    ) = refs[40:]
+    count = tokens.shape[0]
+    rows_dev = count // SEQ
+    links = Links()
+    attn_block = rows_block(attn_mat, 48, 1152)
+    out_block = rows_block(attn_mat, 48, 384, 3 * WIDTH)
+    up_block = rows_block(up_mat, 48, 1536)
+    down_block = rows_block(down_mat, 192, 384)
+    attn = Gather(links, attn_block, sends, recvs, 0)
+    out = Gather(links, out_block, sends, recvs, 1)
+    up = Gather(links, up_block, sends, recvs, 2)
+    down = Gather(links, down_block, sends, recvs, 3)
+    tiny = Gather(links, lead_block(small_all), sends, recvs, 4)
+    own_chip = links.chip_own + links.z
+    kept = []
+
+    def keep(src, dst):
+        copy = pltpu.make_async_copy(src, dst, local_sems.at[len(kept)])
+        copy.start()
+        kept.append(copy)
+
+    for index, ref in enumerate((w_query, w_key, w_value)):
+        cat_attn[:, index * WIDTH : (index + 1) * WIDTH] = ref[...]
+    own_small = small_all.at[links.c, own_chip]
+    own_small[0:24, :] = w_proj[...]
+    own_small[24:40, :] = jnp.zeros((16, 128), jnp.float32)
+    for index, ref in enumerate(vector_refs):
+        own_small[24 + index : 25 + index, 0:24] = ref[...].reshape(1, 24)
+    own_small[32:33, 0:96] = b_up[...].reshape(1, 96)
+
+    links.greet()
+    halves(links, cat_attn, stage_attn, half_sends, half_recvs, 0)
+    tiny.first()
+    halves(links, w_out, stage_out, half_sends, half_recvs, 1)
+    halves(links, w_up, stage_up, half_sends, half_recvs, 2)
+    halves(links, w_down, stage_down, half_sends, half_recvs, 3)
+    joined(links, stage_attn, half_sends, half_recvs, 0, attn_block)
+    attn.first()
+    joined(links, stage_out, half_sends, half_recvs, 1, out_block)
+    joined(links, stage_up, half_sends, half_recvs, 2, up_block)
+    joined(links, stage_down, half_sends, half_recvs, 3, down_block)
+    tiny.second()
+    attn.second()
+    out.first()
+    live_rows = []
+    for r in range(rows_dev):
+        segment, live = segment_forms(segment_ids, row_lengths, r)
+        live_rows.append(live)
+        d_mid[r * SEQ : (r + 1) * SEQ, 0:SEQ] = mask_of(segment, live)
+    tiny.third()
+    attn.third()
+    out.second()
+    up.first()
+    turned[...] = tokens[...].T
+    keep(turned, turned_hbm)
+    tiny.fourth()
+    tiny.last()
+
+    cores = [(i % 2, i // 2) for i in range(SHARDS)]
+    for index, tile in enumerate(spread_lanes([small_all[c, n, 24:32, :] for c, n in cores], 24)):
+        vectors[:, index * 128 : (index + 1) * 128] = rounded(tile)
+    for index, tile in enumerate(spread_lanes([small_all[c, n, 32:40, :] for c, n in cores], 96)):
+        up_bias[:, index * 128 : (index + 1) * 128] = rounded(tile)
+    for r in range(CHIPS):
+        both = jnp.concatenate([small_all[0, r, 0:24, :], small_all[1, r, 0:24, :]], axis=0)
+        proj[r * 48 : (r + 1) * 48, :] = both.astype(jnp.bfloat16)
+    attn.fourth()
+    attn.last()
+
+    def project(step, carry):
+        rows = part_of(step, CHUNK)
+        part = tokens[rows, :]
+        for index in range(3):
+            columns = slice(index * WIDTH, (index + 1) * WIDTH)
+            value = dotted(part, attn_mat[:, columns], 1, 0)
+            if index != 1:
+                value = value + vectors[index // 2 : index // 2 + 1, :]
+            qkv[rows, columns] = value.astype(jnp.bfloat16)
+        staged(step, {1: out.third, 2: up.second, 3: down.first})
+        return carry
+
+    lax.fori_loop(0, count // CHUNK, project, 0)
+    keep(qkv, qkv_hbm)
+
+    def attend(item, carry):
+        attend_pair(lax.div(item, PAIRS), lax.rem(item, PAIRS), qkv, context, logsums, d_mid)
+        staged(
+            item,
+            {
+                0: out.fourth,
+                2: up.third,
+                4: out.last,
+                5: down.second,
+                6: up.fourth,
+                8: up.last,
+                9: down.third,
+            },
+        )
+        return carry
+
+    lax.fori_loop(0, rows_dev * PAIRS, attend, 0)
+    keep(context, context_hbm)
+    keep(attn_mat, attn_hbm)
+
+    def mix(step, carry):
+        rows = part_of(step, CHUNK)
+        mixed = dotted(context[rows, :], attn_mat[:, 3 * WIDTH :], 1, 0) + vectors[2:3, :]
+        normed, scaled = norm_parts(tokens[rows, :].astype(jnp.float32) + mixed)
+        normed_one[rows, :] = normed
+        scaled_one[rows, :] = jnp.broadcast_to(scaled, (CHUNK, 128))
+        low_one[rows, :] = (normed * vectors[3:4, :] + vectors[4:5, :]).astype(jnp.bfloat16)
+        return carry
+
+    lax.fori_loop(0, count // CHUNK, mix, 0)
+    keep(normed_one, normed_one_hbm)
+    keep(low_one, low_one_hbm)
+    keep(up_mat, up_hbm)
+
+    def widen(step, carry):
+        rows = part_of(step, CHUNK)
+        part = low_one[rows, :]
+        for index in range(4):
+            columns = slice(index * WIDTH, (index + 1) * WIDTH)
+            upward = dotted(part, up_mat[:, columns], 1, 0) + up_bias[0:1, columns]
+            chance = 0.5 * (1.0 + lax.erf(upward * ROOT_HALF))
+            activated[rows, columns] = (upward * chance).astype(jnp.bfloat16)
+            density = jnp.exp(-0.5 * upward * upward) * DENSITY_SCALE
+            slope[rows, columns] = (chance + upward * density).astype(jnp.bfloat16)
+        staged(step, {1: down.fourth})
+        return carry
+
+    lax.fori_loop(0, count // CHUNK, widen, 0)
+    keep(slope, slope_hbm)
+    down.last()
+    keep(down_mat, down_hbm)
+
+    grad_vectors[...] = jnp.zeros_like(grad_vectors)
+    grad_proj[...] = jnp.zeros_like(grad_proj)
+    for r in range(rows_dev):
+
+        def narrow(step, carry):
+            here = part_of(step, CHUNK)
+            rows = pl.ds(pl.multiple_of(r * SEQ + step * CHUNK, CHUNK), CHUNK)
+            mixed = dotted(activated[rows, :], down_mat[...], 1, 0) + vectors[5:6, :]
+            mixed = mixed + (normed_one[rows, :] * vectors[3:4, :] + vectors[4:5, :])
+            normed, scaled = norm_parts(mixed)
+            normed_two[here, :] = normed
+            scaled_two[here, :] = jnp.broadcast_to(scaled, (CHUNK, 128))
+            low_two[here, :] = (normed * vectors[6:7, :] + vectors[7:8, :]).astype(jnp.bfloat16)
+            return carry
+
+        lax.fori_loop(0, SEQ // CHUNK, narrow, 0)
+        raw = dotted(low_two[...], proj[...], 1, 0)
+        inverse = lax.rsqrt(jnp.sum(raw * raw, -1, keepdims=True) + UNIT_EPS)
+        embedded = raw * inverse
+        embeddings[r] = embedded
+        low_embed = embedded.astype(jnp.bfloat16)
+        similar = dotted(low_embed[0:QLEN], low_embed, 1, 1)
+        loss, d_similar = passage_loss(r, similar, live_rows[r], teacher_index, teacher_table)
+        losses[r] = loss[0, 0]
+        d_similar = d_similar.astype(jnp.bfloat16)
+        d_embed = dotted(d_similar, low_embed[0:QLEN], 0, 0)
+        d_query = dotted(d_similar, low_embed, 1, 0)
+        d_embed = jnp.concatenate([d_embed[0:QLEN] + d_query, d_embed[QLEN:]], axis=0)
+        along = jnp.sum(d_embed * embedded, -1, keepdims=True)
+        d_raw = (inverse * (d_embed - embedded * along)).astype(jnp.bfloat16)
+        grad_proj[...] += dotted(low_two[...], d_raw, 0, 0)
+        d_hidden = dotted(d_raw, proj[...], 1, 1)
+        normed = normed_two[...]
+        d_mixed = norm_back(d_hidden, normed, scaled_two[:, 0:1], vectors[6:7, :])
+        low_mixed = d_mixed.astype(jnp.bfloat16)
+        rows = slice(r * SEQ, (r + 1) * SEQ)
+        d_mid[rows, :] = d_mixed
+        d_branch[rows, :] = low_mixed
+        grad_vectors[5:6, :] += jnp.sum(low_mixed.astype(jnp.float32), 0, keepdims=True)
+        grad_vectors[6:7, :] += jnp.sum(d_hidden * normed, 0, keepdims=True)
+        grad_vectors[7:8, :] += jnp.sum(d_hidden, 0, keepdims=True)
+    keep(d_mid, d_mid_hbm)
+    keep(d_branch, d_branch_hbm)
+
+    def grad_copy(step, slot):
+        return pltpu.make_async_copy(
+            grad_down.at[slot], grad_down_hbm.at[part_of(step, CHUNK), :], grad_sems.at[slot]
+        )
+
+    def weigh(step, carry):
+        slot = lax.rem(step, 2)
+
+        @pl.when(step >= 2)
+        def _():
+            grad_copy(step - 2, slot).wait()
+
+        part = activated[:, part_of(step, CHUNK)]
+        grad_down[slot] = dotted(part, d_branch[...], 0, 0).astype(jnp.bfloat16)
+        grad_copy(step, slot).start()
+        return carry
+
+    steps = HIDDEN // CHUNK
+    lax.fori_loop(0, steps, weigh, 0)
+    for step in (steps - 2, steps - 1):
+        grad_copy(step, step % 2).wait()
+    links.finish()
+    for copy in kept:
+        copy.wait()
+
+
+def run_first(tokens, weights, vectors, segment_ids, row_lengths, teacher_index, teacher_table):
+    count = tokens.shape[0]
+    rows_dev = count // SEQ
+    vmem = pl.BlockSpec(memory_space=pltpu.VMEM)
+    smem = pl.BlockSpec(memory_space=pltpu.SMEM)
+    anywhere = pl.BlockSpec(memory_space=pl.ANY)
+    low = jnp.bfloat16
+    wide = jnp.float32
+
+    def array(kind, *shape):
+        return jax.ShapeDtypeStruct(shape, kind)
+
+    return pl.pallas_call(
+        first_kernel,
+        out_shape=[
+            array(wide, rows_dev),
+            array(wide, rows_dev, SEQ, EMBED),
+            array(low, WIDTH, HIDDEN),
+            array(low, WIDTH, HIDDEN),
+            array(low, HIDDEN, WIDTH),
+            array(low, WIDTH, count),
+            array(low, count, 3 * WIDTH),
+            array(low, count, WIDTH),
+            array(low, count, WIDTH),
+            array(wide, count, WIDTH),
+            array(low, count, HIDDEN),
+            array(wide, count, WIDTH),
+            array(low, count, WIDTH),
+            array(low, HIDDEN, WIDTH),
+            array(wide, count, 128),
+            array(wide, 8, WIDTH),
+            array(wide, 8, WIDTH),
+            array(wide, WIDTH, EMBED),
+            array(wide, rows_dev, PAIRS, 8, SEQ),
+        ],
+        in_specs=[vmem] * 18 + [smem] * 3,
+        out_specs=[smem, vmem] + [anywhere] * 12 + [vmem] * 5,
+        scratch_shapes=[
+            pltpu.VMEM((WIDTH, HIDDEN), low),
+            pltpu.VMEM((WIDTH, HIDDEN), low),
+            pltpu.VMEM((HIDDEN, WIDTH), low),
+            pltpu.VMEM((WIDTH, count), low),
+            pltpu.VMEM((count, 3 * WIDTH), low),
+            pltpu.VMEM((count, WIDTH), low),
+            pltpu.VMEM((count, WIDTH), low),
+            pltpu.VMEM((count, WIDTH), wide),
+            pltpu.VMEM((count, HIDDEN), low),
+            pltpu.VMEM((count, HIDDEN), low),
+            pltpu.VMEM((count, WIDTH), wide),
+            pltpu.VMEM((count, WIDTH), low),
+            pltpu.VMEM((2, CHUNK, WIDTH), low),
+            pltpu.VMEM((2, CHIPS, SMALL, 128), wide),
+            pltpu.VMEM((24, 3 * WIDTH), wide),
+            pltpu.VMEM((48, 3 * WIDTH // 2), wide),
+            pltpu.VMEM((48, WIDTH // 2), wide),
+            pltpu.VMEM((48, HIDDEN // 2), wide),
+            pltpu.VMEM((192, WIDTH // 2), wide),
+            pltpu.VMEM((WIDTH, EMBED), low),
+            pltpu.VMEM((8, HIDDEN), wide),
+            pltpu.VMEM((SEQ, WIDTH), wide),
+            pltpu.VMEM((SEQ, 128), wide),
+            pltpu.VMEM((SEQ, WIDTH), low),
+            pltpu.SemaphoreType.DMA((5, Gather.SEMS)),
+            pltpu.SemaphoreType.DMA((5, Gather.SEMS)),
+            pltpu.SemaphoreType.DMA((4,)),
+            pltpu.SemaphoreType.DMA((4,)),
+            pltpu.SemaphoreType.DMA((12,)),
+            pltpu.SemaphoreType.DMA((2,)),
+        ],
+        compiler_params=pltpu.CompilerParams(
+            collective_id=0, has_side_effects=True, vmem_limit_bytes=62 * 2**20
+        ),
+        name="forward_gather",
+    )(tokens, *weights, *vectors, segment_ids, row_lengths, teacher_index, teacher_table)
+
+
+def last_kernel(*refs):
+    (
+        attn_hbm,
+        up_hbm,
+        down_hbm,
+        turned_hbm,
+        qkv_hbm,
+        context_hbm,
+        low_one_hbm,
+        normed_one_hbm,
+        slope_hbm,
+        d_mid_hbm,
+        d_branch_hbm,
+        grad_down_hbm,
+        scaled_one,
+        vectors,
+        part_vectors,
+        grad_proj,
+        logsums,
+        segment_ids,
+        row_lengths,
+    ) = refs[:19]
+    (
+        grad_tokens,
+        own_query,
+        own_key,
+        own_value,
+        own_out,
+        own_up,
+        own_down,
+        own_proj,
+        *own_vectors,
+        own_up_bias,
+    ) = refs[19:36]
+    (
+        attn_mat,
+        grads,
+        wide,
+        low_one,
+        turned,
+        d_branch,
+        d_mid,
+        part_down,
+        small_all,
+        rowdots,
+        grad_vectors,
+        grad_up_bias,
+        sends,
+        recvs,
+        local_sems,
+        *rest,
+    ) = refs[36:]
+    held = [rest[6 * i : 6 * i + 6] for i in range(6)]
+    fins = [rest[36 + 2 * i : 38 + 2 * i] for i in range(5)]
+    count = d_mid.shape[0]
+    rows_dev = count // SEQ
+    links = Links()
+    c = links.c
+
+    def scatter(block, rows, group, mine=None):
+        def own(chip):
+            return block(c, chip, 1)
+
+        return Scatter(
+            links, block, own if mine is None else mine, rows, held[group], sends, recvs, group
+        )
+
+    down = scatter(
+        rows_block(grad_down_hbm, 192, 384), 192, 0, lambda chip: part_down.at[part_of(chip, 192), :]
+    )
+    up = scatter(rows_block(grads, 48, 1536), 48, 1)
+    out = scatter(rows_block(grads, 48, 384), 48, 2)
+    most = scatter(rows_block(grads, 48, 768, WIDTH), 48, 3)
+    rest_of = scatter(rows_block(grads, 48, 384, 3 * WIDTH), 48, 4)
+    tiny = scatter(lead_block(small_all), 1, 5)
+
+    def load(src, dst, index):
+        copy = pltpu.make_async_copy(src, dst, local_sems.at[index])
+        copy.start()
+        return copy
+
+    first_loads = [
+        load(d_branch_hbm, d_branch, 0),
+    ]
+    links.greet()
+    down.first()
+    grad_vectors[...] = part_vectors[...]
+
+    def feed_forward(up_mat, down_mat, normed_one):
+        first = first_loads + [load(down_hbm, down_mat, 1), load(slope_hbm, wide, 2)]
+        later = [
+            load(low_one_hbm, low_one, 3),
+            load(grad_down_hbm.at[:, part_of(c, WIDTH // 2)], part_down, 4),
+            load(up_hbm, up_mat, 5),
+            load(d_mid_hbm, d_mid, 6),
+            load(normed_one_hbm, normed_one, 7),
+        ]
+        for copy in first:
+            copy.wait()
+
+        def widen(step, carry):
+            rows = part_of(step, CHUNK)
+            part = d_branch[rows, :]
+            for index in range(4):
+                columns = slice(index * WIDTH, (index + 1) * WIDTH)
+                grad = dotted(part, down_mat[columns, :], 1, 1)
+                wide[rows, columns] = (grad * wide[rows, columns].astype(jnp.float32)).astype(
+                    jnp.bfloat16
+                )
+            return carry
+
+        lax.fori_loop(0, count // CHUNK, widen, 0)
+        for copy in later:
+            copy.wait()
+        down.second()
+
+        def weigh(step, carry):
+            rows = part_of(step, CHUNK)
+            part = low_one[:, rows].T
+            for index in range(4):
+                columns = slice(index * WIDTH, (index + 1) * WIDTH)
+                grads[rows, columns] = dotted(part, wide[:, columns], 1, 0).astype(jnp.bfloat16)
+            return carry
+
+        lax.fori_loop(0, WIDTH // CHUNK, weigh, 0)
+        up.first()
+        ones = jnp.ones((8, count), jnp.bfloat16)
+        for index in range(4):
+            columns = slice(index * WIDTH, (index + 1) * WIDTH)
+            grad_up_bias[:, columns] = dotted(ones, wide[:, columns], 1, 0)
+        down.third()
+
+        def narrow(step, carry):
+            rows = part_of(step, CHUNK)
+            d_hidden = d_mid[rows, :] + dotted(wide[rows, :], up_mat[...], 1, 1)
+            normed = normed_one[rows, :]
+            d_mixed = norm_back(d_hidden, normed, scaled_one[rows, 0:1], vectors[3:4, :])
+            d_mid[rows, :] = d_mixed
+            d_branch[rows, :] = d_mixed.astype(jnp.bfloat16)
+            grad_vectors[3:4, :] += jnp.sum(d_hidden * normed, 0, keepdims=True)
+            grad_vectors[4:5, :] += jnp.sum(d_hidden, 0, keepdims=True)
+            return carry
+
+        lax.fori_loop(0, count // CHUNK, narrow, 0)
+
+    pl.run_scoped(
+        feed_forward,
+        pltpu.VMEM((WIDTH, HIDDEN), jnp.bfloat16),
+        pltpu.VMEM((HIDDEN, WIDTH), jnp.bfloat16),
+        pltpu.VMEM((count, WIDTH), jnp.float32),
+    )
+
+    def attention(context, d_context, bias):
+        loads = [
+            load(context_hbm, context, 8),
+            load(attn_hbm, attn_mat, 9),
+            load(qkv_hbm, wide.at[:, 0 : 3 * WIDTH], 10),
+            load(turned_hbm, turned, 11),
+        ]
+        up.second()
+        links_first = len(links.started)
+        down.fourth()
+        ones = jnp.ones((8, count), jnp.bfloat16)
+        grad_vectors[2:3, :] = dotted(ones, d_branch[...], 1, 0)[0:1]
+        for r in range(rows_dev):
+            segment, live = segment_forms(segment_ids, row_lengths, r)
+            bias[r] = mask_of(live, segment)
+        for copy in loads:
+            copy.wait()
+
+        def give(step, carry):
+            rows = part_of(step, CHUNK)
+            d_context[rows, :] = dotted(d_branch[rows, :], attn_mat[:, 3 * WIDTH :], 1, 1).astype(
+                jnp.bfloat16
+            )
+            return carry
+
+        lax.fori_loop(0, count // CHUNK, give, 0)
+        row_dots(context, d_context, rowdots)
+        links.finish()
+
+        def weigh_out(step, carry):
+            rows = part_of(step, CHUNK)
+            part = context[:, rows].T
+            grads[rows, 0:WIDTH] = dotted(part, d_branch[...], 1, 0).astype(jnp.bfloat16)
+            return carry
+
+        lax.fori_loop(0, WIDTH // CHUNK, weigh_out, 0)
+        out.first()
+
+        def down_trade():
+            down.trade(*fins[0])
+
+        def down_whole():
+            low, high = down.whole(*fins[0])
+            own_down[:, : WIDTH // 2] = low
+            own_down[:, WIDTH // 2 :] = high
+
+        def up_trade():
+            up.trade(*fins[1])
+
+        def up_whole():
+            low, high = up.whole(*fins[1])
+            own_up[:, : HIDDEN // 2] = low
+            own_up[:, HIDDEN // 2 :] = high
+
+        def out_trade():
+            out.trade(*fins[2])
+
+        def out_whole():
+            low, high = out.whole(*fins[2])
+            own_out[:, : WIDTH // 2] = low
+            own_out[:, WIDTH // 2 :] = high
+
+        def attend(first, steps):
+            def step(item, carry):
+                r = lax.rem(item, rows_dev)
+                p = lax.div(item, rows_dev)
+                attend_back_pair(r, p, wide, d_context, logsums, rowdots, bias)
+                staged(item, steps)
+                return carry
+
+            return step
+
+        lax.fori_loop(
+            0,
+            4 * rows_dev,
+            attend(
+                0,
+                {0: up.third, 1: out.second, 2: down_trade, 3: up.fourth, 4: out.third, 5: down_whole, 6: out.fourth, 7: up_trade},
+            ),
+            0,
+        )
+
+        def weigh(first, pairs, base):
+            def step(step, carry):
+                rows = part_of(step, CHUNK)
+                part = turned[rows, :]
+                for index in range(3):
+                    start = index * WIDTH + first * 128
+                    there = base + index * pairs * 128
+                    grads[rows, there : there + pairs * 128] = dotted(
+                        part, wide[:, start : start + pairs * 128], 1, 0
+                    ).astype(jnp.bfloat16)
+                return carry
+
+            lax.fori_loop(0, WIDTH // CHUNK, step, 0)
+
+        weigh(0, 4, WIDTH)
+        most.first()
+        lax.fori_loop(
+            4 * rows_dev,
+            6 * rows_dev,
+            attend(4 * rows_dev, {8: up_whole, 9: most.second, 10: out_trade, 11: most.third}),
+            0,
+        )
+        weigh(4, 2, 3 * WIDTH)
+        rest_of.first()
+        out_whole()
+        for index in (0, 2):
+            total = dotted(ones, wide[:, index * WIDTH : (index + 1) * WIDTH], 1, 0)
+            grad_vectors[index // 2 : index // 2 + 1, :] = total[0:1]
+
+    pl.run_scoped(
+        attention,
+        pltpu.VMEM((count, WIDTH), jnp.bfloat16),
+        pltpu.VMEM((count, WIDTH), jnp.bfloat16),
+        pltpu.VMEM((rows_dev, SEQ, SEQ), jnp.float32),
+    )
+
+    tiles = [grad_vectors[:, i * 128 : (i + 1) * 128] for i in range(WIDTH // 128)]
+    for i, part in enumerate(pick_lanes(tiles, 24, SHARDS)):
+        small_all[i % 2, i // 2, 24:32, :] = part
+    tiles = [grad_up_bias[:, i * 128 : (i + 1) * 128] for i in range(HIDDEN // 128)]
+    for i, part in enumerate(pick_lanes(tiles, 96, SHARDS)):
+        small_all[i % 2, i // 2, 32:40, :] = part
+        small_all[i % 2, i // 2, 0:24, :] = grad_proj[i * 24 : (i + 1) * 24, :]
+    tiny.first()
+
+    def back(step, carry):
+        rows = part_of(step, CHUNK)
+        value = dotted(wide[rows, 0 : 3 * WIDTH], attn_mat[:, 0 : 3 * WIDTH], 1, 1)
+        grad_tokens[rows, :] = value + d_mid[rows, :]
+        return carry
+
+    most.fourth()
+    rest_of.second()
+    tiny.second()
+    lax.fori_loop(0, 2, back, 0)
+    rest_of.third()
+    tiny.third()
+    lax.fori_loop(2, 4, back, 0)
+    rest_of.fourth()
+    tiny.fourth()
+    most.trade(*fins[3])
+    rest_of.trade(*fins[4])
+    total = tiny.fifth()[0]
+    own_proj[...] = total[0:24, :]
+    for index, ref in enumerate(own_vectors):
+        ref[...] = total[24 + index : 25 + index, 0:24].reshape(24)
+    own_up_bias[...] = total[32:33, 0:96].reshape(96)
+    low, high = most.whole(*fins[3])
+    own_query[:, 0:512] = low[:, 0:512]
+    own_key[:, 0:256] = low[:, 512:768]
+    own_key[:, 256:512] = high[:, 0:256]
+    own_value[:, 0:512] = high[:, 256:768]
+    low, high = rest_of.whole(*fins[4])
+    own_query[:, 512:768] = low[:, 0:256]
+    own_key[:, 512:640] = low[:, 256:384]
+    own_key[:, 640:768] = high[:, 0:128]
+    own_value[:, 512:768] = high[:, 128:384]
+    links.finish()
+
+
+def run_last(kept, segment_ids, row_lengths):
+    count = kept[9].shape[0]
+    rows_dev = count // SEQ
+    vmem = pl.BlockSpec(memory_space=pltpu.VMEM)
+    smem = pl.BlockSpec(memory_space=pltpu.SMEM)
+    anywhere = pl.BlockSpec(memory_space=pl.ANY)
+    low = jnp.bfloat16
+    wide = jnp.float32
+
+    def array(*shape):
+        return jax.ShapeDtypeStruct(shape, wide)
+
+    def held(unit, kind):
+        return [pltpu.VMEM((n * unit[0],) + unit[1:], kind) for n in (16, 2, 2, 4, 4, 3)]
+
+    blocks = ((192, 384), (48, 1536), (48, 384), (48, 768), (48, 384))
+    buffers = []
+    for block in blocks:
+        buffers += held(block, low)
+    buffers += held((1, SMALL, 128), wide)
+    for rows, columns in blocks:
+        buffers += [pltpu.VMEM((rows, columns), wide), pltpu.VMEM((rows // 2, columns), wide)]
+    return pl.pallas_call(
+        last_kernel,
+        out_shape=[
+            array(count, WIDTH),
+            array(24, WIDTH),
+            array(24, WIDTH),
+            array(24, WIDTH),
+            array(24, WIDTH),
+            array(24, HIDDEN),
+            array(96, WIDTH),
+            array(24, EMBED),
+        ]
+        + [array(24)] * 8
+        + [array(96)],
+        in_specs=[anywhere] * 12 + [vmem] * 6 + [smem],
+        out_specs=[vmem] * 17,
+        scratch_shapes=[
+            pltpu.VMEM((WIDTH, HIDDEN), low),
+            pltpu.VMEM((WIDTH, HIDDEN), low),
+            pltpu.VMEM((count, HIDDEN), low),
+            pltpu.VMEM((count, WIDTH), low),
+            pltpu.VMEM((WIDTH, count), low),
+            pltpu.VMEM((count, WIDTH), low),
+            pltpu.VMEM((count, WIDTH), wide),
+            pltpu.VMEM((HIDDEN, WIDTH // 2), low),
+            pltpu.VMEM((2, CHIPS, SMALL, 128), wide),
+            pltpu.VMEM((rows_dev, PAIRS, 8, SEQ), wide),
+            pltpu.VMEM((8, WIDTH), wide),
+            pltpu.VMEM((8, HIDDEN), wide),
+            pltpu.SemaphoreType.DMA((6, Scatter.SEMS)),
+            pltpu.SemaphoreType.DMA((6, Scatter.SEMS)),
+            pltpu.SemaphoreType.DMA((12,)),
+        ]
+        + buffers,
+        compiler_params=pltpu.CompilerParams(
+            collective_id=1, has_side_effects=True, vmem_limit_bytes=63 * 2**20
+        ),
+        name="backward_scatter",
+    )(*kept, segment_ids, row_lengths)
+
+
+def body_tiles(
+    tokens,
+    w_query,
+    b_query,
+    w_key,
+    w_value,
+    b_value,
+    w_out,
+    b_out,
+    gain_one,
+    shift_one,
+    w_up,
+    b_up,
+    w_down,
+    b_down,
+    gain_two,
+    shift_two,
+    w_proj,
+    segment_ids,
+    row_lengths,
+    teacher_index,
+    teacher_table,
+):
+    rows_dev, _, width = tokens.shape
+    losses, embeddings, *kept = run_first(
+        tokens.reshape(rows_dev * SEQ, width),
+        (w_query, w_key, w_value, w_out, w_up, w_down, w_proj),
+        (b_query, b_value, b_out, gain_one, shift_one, b_down, gain_two, shift_two, b_up),
+        segment_ids,
+        row_lengths,
+        teacher_index,
+        teacher_table,
+    )
+    (
+        grad_tokens,
+        grad_query,
+        grad_key,
+        grad_value,
+        grad_out,
+        grad_up,
+        grad_down,
+        grad_proj,
+        grad_query_bias,
+        grad_value_bias,
+        grad_out_bias,
+        grad_gain_first,
+        grad_shift_first,
+        grad_down_bias,
+        grad_gain_second,
+        grad_shift_second,
+        grad_up_bias,
+    ) = run_last(kept, segment_ids, row_lengths)
+    return (
+        losses,
+        embeddings,
+        grad_tokens.reshape(rows_dev, SEQ, width),
+        grad_query,
+        grad_query_bias,
+        grad_key,
+        grad_value,
+        grad_value_bias,
+        grad_out,
+        grad_out_bias,
+        grad_gain_first,
+        grad_shift_first,
+        grad_up,
+        grad_up_bias,
+        grad_down,
+        grad_down_bias,
+        grad_gain_second,
+        grad_shift_second,
+        grad_proj,
+    )
+
+
 def solution(mesh):
     in_specs = (
         P(("dp", "fsdp"), None, None),
@@ -417,4 +1732,5 @@
         P(("dp", "fsdp")),
         P(("dp", "fsdp"), None),
     )
+    body = body_tiles if fits(mesh) else body_whole
     return jax.shard_map(body, mesh=mesh, in_specs=in_specs, out_specs=out_specs, check_vma=False)

time: 1410 us -> 238 us (0.17)
  waiting for transfers between devices: 535 us -> 0 us
  matrix products: 363 us -> 0 us
  Pallas kernels: 0 us -> 222 us
  local copies, waits for them, and re-layouts: 184 us -> 14.4 us
  blocking collectives: 124 us -> 0 us
  loops' own time: 96 us -> 0 us
  other arithmetic: 79.8 us -> 0 us
  between operations: 15 us -> 0.82 us
    dot_general x193 -> x0, matrix products: 363 us -> none  [the longest x79 132 us: against(): lax.dot_general(left, right, (((1,), (1,)), ((), ())), preferred_element_...]
    reduce_scatter x3 -> x0, waiting for transfers between devices: 283 us -> none  [the longest x1 142 us: spread_grads(): lax.psum_scatter(terms[9], ('dp', 'fsdp'), scatter_dimension=0, tiled=True)]
    pallas_call x0 -> x2, Pallas kernels: none -> 222 us  [the longest x1 114 us: run_last(): pl.pallas_call(last_kernel, out_shape=[array(count, WIDTH), array(24, WID...]
    unnamed x17 -> x0, waiting for transfers between devices: 200 us -> none
    another operation x2 -> x0, loops' own time: 96 us -> none  [the longest x1 48 us: body(): lax.map(attend_back, (query_heads, key_heads, value_heads, d_context_head...]
    unnamed x2 -> x0, blocking collectives: 82.9 us -> none
    dynamic_slice x168 -> x0, local copies, waits for them, and re-layouts: 74.1 us -> none  [the longest x48 28.3 us: visibility(): lax.dynamic_index_in_dim(row_lengths, row_index, 0, keepdims=False)]
    all_gather x6 -> x0, waiting for transfers between devices: 52.6 us -> none  [the longest x1 48.7 us: collect(): lax.all_gather(sent[2], ('dp', 'fsdp'), axis=0, tiled=True)]
  transfers between devices with their start and end apart: 13 -> 0, of which waited for: 6 -> 0; matrix products, arithmetic and copies ran while one was open for 42% -> 0% of each run, Pallas kernels for 0% -> 0%
where the time goes in v1:
time: 238 us; the launch traced here: 237 us
  Pallas kernels  222 us (93%)
  local copies, waits for them, and re-layouts  14.4 us (6%)
    pallas_call x1, Pallas kernels, run_last(): pl.pallas_call(last_kernel, out_shape=[array(count, WIDTH), array(24, WID...  114 us
    pallas_call x1, Pallas kernels, run_first(): pl.pallas_call(first_kernel, out_shape=[array(wide, rows_dev), array(wide...  108 us
    unnamed x55, local copies, waits for them, and re-layouts  14.4 us

profile of v1, /device:TPU:0, one launch (start us, length us, event | category | flops | bytes accessed | tf_op | source)
XLA Modules:
  0.0 237.5 jit_solution(12905699970700731865)
XLA Ops:
  0.7 108.5 %forward_gather.1 = (f32[2]{0:T(128)}, f32[2,512,128]{2,1,0:T(8,128)}, bf16[768,3072]{1,0:T(8,128)(2,1)}, bf16[768,3072]{1,0:T(8,128)(2,1)}, bf16[3072,768]{1,0:...) custom-call(bf16[1024,768]{1,0:T(8,128)(2,1)} %bitcast.3, ...), custom_call_target="tpu_custom_call" | custom-call | tf_op jit(solution)/shard_map/forward_gather/pallas_call | solution.py:1174
  109.2 113.7 %backward_scatter.1 = (f32[1024,768]{1,0:T(8,128)}, f32[24,768]{1,0:T(8,128)}, f32[24,768]{1,0:T(8,128)}, f32[24,768]{1,0:T(8,128)}, f32[24,768]{1,0:T(8,128)}, ...) custom-call(bf16[768,3072]{1,0:T(8,128)(2,1)} %get-tuple-element.57., ...), custom_call_target="tpu_custom_call" | custom-call | tf_op jit(solution)/shard_map/backward_scatter/pallas_call | solution.py:1574
  222.9 0.0 copy-done.17
  222.9 0.5 copy.59
  223.4 0.8 copy.60
  224.4 3.9 %copy.61 = f32[2,512,768]{2,1,0:T(8,128)} copy(f32[2,512,768]{2,1,0:T(8,128)} %bitcast.2) | data formatting | bytes 6291456
  228.3 0.6 copy.62
  228.9 0.5 copy.63
  229.4 0.6 copy.64
  230.0 0.0 copy-done.4
  230.1 0.6 copy.65
  230.7 0.5 copy.66
  231.2 0.6 copy.67
  231.8 0.5 copy.68
  232.4 0.5 copy.69
  232.9 0.5 copy.70
  233.4 0.7 copy.71
  234.1 0.5 copy.72
  234.6 0.7 copy.73
  235.3 0.5 copy.74
  235.8 0.5 copy.75
  236.4 0.0 copy-done.8
  236.4 0.5 copy.76
  236.9 0.6 copy.77
  (33 shorter events, 0.1 us)
Async XLA Ops:
  109.2 113.8 %copy-start.17 = (f32[2]{0:T(128)S(1)}, f32[2]{0:T(128)}, u32[]{:S(2)}) copy-start(f32[2]{0:T(128)} %get-tuple-element.110) | copy-start | bytes 28
  109.2 114.3 %copy-start = (f32[2,512,128]{2,1,0:T(8,128)S(1)}, f32[2,512,128]{2,1,0:T(8,128)}, u32[]{:S(2)}) copy-start(f32[2,512,128]{2,1,0:T(8,128)} %get-tuple-element.111) | copy-start | bytes 1572868
  224.2 4.0 %copy-start.6 = (f32[24,768]{1,0:T(8,128)S(1)}, f32[24,768]{1,0:T(8,128)}, u32[]{:S(2)}) copy-start(f32[24,768]{1,0:T(8,128)} %get-tuple-element.113) | copy-start | bytes 221188
  224.2 4.7 %copy-start.16 = (f32[24]{0:T(128)S(1)}, f32[24]{0:T(128)}, u32[]{:S(2)}) copy-start(f32[24]{0:T(128)} %get-tuple-element.114) | copy-start | bytes 292
  224.2 5.2 %copy-start.5 = (f32[24,768]{1,0:T(8,128)S(1)}, f32[24,768]{1,0:T(8,128)}, u32[]{:S(2)}) copy-start(f32[24,768]{1,0:T(8,128)} %get-tuple-element.115) | copy-start | bytes 221188
  224.2 5.8 %copy-start.4 = (f32[24,768]{1,0:T(8,128)S(1)}, f32[24,768]{1,0:T(8,128)}, u32[]{:S(2)}) copy-start(f32[24,768]{1,0:T(8,128)} %get-tuple-element.116) | copy-start | bytes 221188
  224.2 6.4 %copy-start.15 = (f32[24]{0:T(128)S(1)}, f32[24]{0:T(128)}, u32[]{:S(2)}) copy-start(f32[24]{0:T(128)} %get-tuple-element.117) | copy-start | bytes 292
  224.3 6.9 %copy-start.3 = (f32[24,768]{1,0:T(8,128)S(1)}, f32[24,768]{1,0:T(8,128)}, u32[]{:S(2)}) copy-start(f32[24,768]{1,0:T(8,128)} %get-tuple-element.118) | copy-start | bytes 221188
  224.3 7.6 %copy-start.14 = (f32[24]{0:T(128)S(1)}, f32[24]{0:T(128)}, u32[]{:S(2)}) copy-start(f32[24]{0:T(128)} %get-tuple-element.119) | copy-start | bytes 292
  224.3 8.1 %copy-start.13 = (f32[24]{0:T(128)S(1)}, f32[24]{0:T(128)}, u32[]{:S(2)}) copy-start(f32[24]{0:T(128)} %get-tuple-element.120) | copy-start | bytes 292
  224.3 8.6 %copy-start.12 = (f32[24]{0:T(128)S(1)}, f32[24]{0:T(128)}, u32[]{:S(2)}) copy-start(f32[24]{0:T(128)} %get-tuple-element.121) | copy-start | bytes 292
  224.3 9.1 %copy-start.2 = (f32[24,3072]{1,0:T(8,128)S(1)}, f32[24,3072]{1,0:T(8,128)}, u32[]{:S(2)}) copy-start(f32[24,3072]{1,0:T(8,128)} %get-tuple-element.122) | copy-start | bytes 884740
  224.3 9.8 %copy-start.11 = (f32[96]{0:T(128)S(1)}, f32[96]{0:T(128)}, u32[]{:S(2)}) copy-start(f32[96]{0:T(128)} %get-tuple-element.123) | copy-start | bytes 1156
  224.3 10.3 %copy-start.1 = (f32[96,768]{1,0:T(8,128)S(1)}, f32[96,768]{1,0:T(8,128)}, u32[]{:S(2)}) copy-start(f32[96,768]{1,0:T(8,128)} %get-tuple-element.124) | copy-start | bytes 884740
  224.3 11.0 %copy-start.10 = (f32[24]{0:T(128)S(1)}, f32[24]{0:T(128)}, u32[]{:S(2)}) copy-start(f32[24]{0:T(128)} %get-tuple-element.125) | copy-start | bytes 292
  224.3 11.5 %copy-start.9 = (f32[24]{0:T(128)S(1)}, f32[24]{0:T(128)}, u32[]{:S(2)}) copy-start(f32[24]{0:T(128)} %get-tuple-element.126) | copy-start | bytes 292
  224.3 12.0 %copy-start.8 = (f32[24]{0:T(128)S(1)}, f32[24]{0:T(128)}, u32[]{:S(2)}) copy-start(f32[24]{0:T(128)} %get-tuple-element.127) | copy-start | bytes 292
  224.4 12.5 %copy-start.7 = (f32[24,128]{1,0:T(8,128)S(1)}, f32[24,128]{1,0:T(8,128)}, u32[]{:S(2)}) copy-start(f32[24,128]{1,0:T(8,128)} %get-tuple-element.128) | copy-start | bytes 36868

commit v2 on v1

--- a/solution.py
+++ b/solution.py
@@ -431,6 +431,14 @@
         self.to_x = device(1 - x, y, z, c)
         self.to_y = device(x, 1 - y, z, c)
         self.to_z = [None] + [device(x, y, lax.rem(z + k, 4), c) for k in (1, 2, 3)]
+        self.inner = (z == 1) | (z == 2)
+        paired = z + 1 - 2 * lax.rem(z, 2)
+        self.to_pair = device(x, y, paired, c)
+        self.to_middle = device(x, y, jnp.where(self.inner, 3 - z, paired), c)
+        far = jnp.where(z < 2, 1, -1)
+        near = jnp.where(self.inner, 3 - z, z + 2 * far)
+        last = jnp.where(self.inner, 3 - z + far, z + 3 * far)
+        self.levels = [z, paired, near, last]
         self.started = []
 
     def greet(self):
@@ -443,7 +451,7 @@
     def level(self, k):
         return lax.rem(self.z + k, 4)
 
-    def send(self, ends, sems, target):
+    def send(self, ends, sems, target, inner=False):
         def copy():
             src, dst = ends()
             send_sem, recv_sem = sems()
@@ -456,8 +464,18 @@
                 device_id_type=MESH,
             )
 
-        copy().start()
-        self.started.append(copy)
+        def start():
+            copy().start()
+
+        def wait():
+            copy().wait_send()
+
+        if inner:
+            pl.when(self.inner)(start)
+            self.started.append(lambda: pl.when(self.inner)(wait))
+        else:
+            start()
+            self.started.append(wait)
 
     def arrived(self, ref, sems, source):
         pltpu.make_async_remote_copy(
@@ -470,8 +488,8 @@
         ).wait_recv()
 
     def finish(self, first=0):
-        for copy in self.started[first:]:
-            copy().wait_send()
+        for wait in self.started[first:]:
+            wait()
         self.started = self.started[:first]
 
 
@@ -493,8 +511,8 @@
 
 
 class Gather:
-    Z, X, Y, FX, FY, C = 0, 3, 7, 11, 13, 15
-    SEMS = 19
+    Z, X, Y, FX, FY, C, ZF = 0, 3, 7, 11, 13, 15, 19
+    SEMS = 21
 
     def __init__(self, links, block, sends, recvs, group):
         self.links = links
@@ -507,47 +525,53 @@
         there = index if there is None else there
         return self.sends.at[self.group, index], self.recvs.at[self.group, there]
 
-    def ship(self, chip, count, index, target, there=None):
+    def ship(self, chip, count, index, target, there=None, inner=False):
         def ends():
             ref = self.block(self.links.c, value_of(chip), count)
             return ref, ref
 
-        self.links.send(ends, lambda: self.sems(index, there), target)
+        self.links.send(ends, lambda: self.sems(index, there), target, inner)
 
     def step_of(self, column, k):
-        return lambda: column + self.links.level(k)
+        return lambda: column + self.links.levels[k]
 
     def take(self, chip, count, index, source, core=None):
         core = self.links.c if core is None else core
         self.links.arrived(self.block(core, value_of(chip), count), self.sems(index), source)
 
-    def first(self):
+    def along(self):
         n = self.links
         own = self.step_of(n.chip_own, 0)
-        for j in (1, 2, 3):
-            self.ship(own, 1, self.Z + j - 1, n.to_z[j], self.Z + 3 - j)
-        self.ship(own, 1, self.X, n.to_x)
-        self.ship(own, 1, self.Y, n.to_y)
-
-    def second(self):
+        self.ship(own, 1, self.Z, n.to_pair)
+        self.ship(own, 1, self.Z + 1, n.to_middle, inner=True)
+
+    def across(self, k):
         n = self.links
-        for k in (1, 2, 3):
-            chip = self.step_of(n.chip_own, k)
-            self.take(chip, 1, self.Z + k - 1, n.to_z[k])
-            self.ship(chip, 1, self.X + k, n.to_x)
-            self.ship(chip, 1, self.Y + k, n.to_y)
-        self.ship(n.chip_own, 4, self.C, n.to_core)
-
-    def third(self):
+        chip = self.step_of(n.chip_own, k)
+        if k:
+            self.take(chip, 1, self.Z + k - 1, n.to_pair if k == 1 else n.to_middle)
+            if k == 1:
+                self.ship(chip, 1, self.Z + 2, n.to_middle, inner=True)
+            else:
+                self.ship(chip, 1, self.ZF + k - 2, n.to_pair, self.Z + k - 1, inner=True)
+        self.ship(chip, 1, self.X + k, n.to_x)
+        self.ship(chip, 1, self.Y + k, n.to_y)
+        if k == 3:
+            self.ship(n.chip_own, 4, self.C, n.to_core)
+
+    def onward(self, k):
         n = self.links
-        for k in (0, 1):
+        if k < 2:
             chip = self.step_of(n.chip_x, k)
             self.take(chip, 1, self.X + k, n.to_x)
             self.ship(chip, 1, self.FY + k, n.to_y)
-        for k in (2, 3):
+        else:
             chip = self.step_of(n.chip_y, k)
             self.take(chip, 1, self.Y + k, n.to_y)
             self.ship(chip, 1, self.FX + k - 2, n.to_x)
+
+    def beside(self):
+        n = self.links
         for k in (2, 3):
             self.take(self.step_of(n.chip_x, k), 1, self.X + k, n.to_x)
         self.ship(n.chip_x, 4, self.C + 1, n.to_core)
@@ -555,7 +579,7 @@
             self.take(self.step_of(n.chip_y, k), 1, self.Y + k, n.to_y)
         self.ship(n.chip_y, 4, self.C + 2, n.to_core)
 
-    def fourth(self):
+    def opposite(self):
         n = self.links
         for k in (0, 1):
             self.take(self.step_of(n.chip_d, k), 1, self.FY + k, n.to_y)
@@ -573,16 +597,19 @@
     C, DY, DX, OX, OY, Z, F = 0, 4, 5, 6, 8, 10, 13
     SEMS = 14
 
-    def __init__(self, links, block, mine, rows, held, sends, recvs, group):
+    def __init__(self, links, block, mine, rows, held, fin, deliver, sends, recvs, group):
         self.links = links
         self.block = block
         self.mine = mine
         self.rows = rows
         self.part, self.d_y, self.d_x, self.o_x, self.o_y, self.z_in = held
+        self.fin = fin
+        self.deliver = deliver
         self.sends = sends
         self.recvs = recvs
         self.group = group
         n = links
+        self.sent = []
         self.columns = (n.chip_d, n.chip_x, n.chip_y, n.chip_own)
 
     def at(self, ref, start, count):
@@ -626,25 +653,28 @@
                 return self.block(1 - n.c, chip, 4), self.at(self.part, chip, 4)
 
             self.ship(ends, self.C + index, n.to_core)
-
-    def second(self):
+            self.sent.append(n.started[-1])
+
+    def second(self, index):
         n = self.links
-        for index, chip in enumerate(self.columns):
-            self.take(self.part, chip, 4, self.C + index, n.to_core)
-            self.add(4, chip, lambda i, chip=chip: self.mine(chip + i))
-            if index == 0:
-                self.ship_part(chip, 2, self.d_y, 0, self.DY, n.to_y)
-                self.ship_part(lambda chip=chip: chip + 2, 2, self.d_x, 0, self.DX, n.to_x)
-            elif index == 1:
-                self.ship_part(lambda chip=chip: chip + 2, 2, self.o_x, 2, self.OX + 1, n.to_x)
-            elif index == 2:
-                self.ship_part(chip, 2, self.o_y, 0, self.OY, n.to_y)
-
-    def third(self):
+        chip = self.columns[index]
+        self.take(self.part, chip, 4, self.C + index, n.to_core)
+        self.add(4, chip, lambda i: self.mine(chip + i))
+        if index == 0:
+            self.ship_part(chip, 2, self.d_y, 0, self.DY, n.to_y)
+            self.ship_part(lambda: chip + 2, 2, self.d_x, 0, self.DX, n.to_x)
+        elif index == 1:
+            self.ship_part(lambda: chip + 2, 2, self.o_x, 2, self.OX + 1, n.to_x)
+        elif index == 2:
+            self.ship_part(chip, 2, self.o_y, 0, self.OY, n.to_y)
+
+    def third(self, index):
         n = self.links
-        self.take(self.d_y, 0, 2, self.DY, n.to_y)
-        self.add(2, n.chip_x, lambda i: self.at(self.d_y, i, 1))
-        self.ship_part(n.chip_x, 2, self.o_x, 0, self.OX, n.to_x)
+        if index == 0:
+            self.take(self.d_y, 0, 2, self.DY, n.to_y)
+            self.add(2, n.chip_x, lambda i: self.at(self.d_y, i, 1))
+            self.ship_part(n.chip_x, 2, self.o_x, 0, self.OX, n.to_x)
+            return
         self.take(self.d_x, 0, 2, self.DX, n.to_x)
         self.add(2, n.chip_y + 2, lambda i: self.at(self.d_x, i, 1))
         self.ship_part(lambda: n.chip_y + 2, 2, self.o_y, 2, self.OY + 1, n.to_y)
@@ -679,19 +709,32 @@
             total = total + self.at(self.z_in, k - 1, 1)[...].astype(jnp.float32)
         return total
 
-    def trade(self, fin, fin_in):
+    def trade(self):
+        if self.fin is None:
+            self.deliver(self.fifth())
+            return
+        fin, fin_in = self.fin
         n = self.links
         rows = self.rows // 2
         fin[...] = self.fifth()
         self.ship(lambda: (fin.at[part_of(1 - n.c, rows)], fin_in), self.F, n.to_core)
 
-    def whole(self, fin, fin_in):
+    def whole(self):
+        if self.fin is None:
+            return
+        fin, fin_in = self.fin
         n = self.links
         rows = self.rows // 2
         n.arrived(fin_in, self.sems(self.F), n.to_core)
         mine = fin[part_of(n.c, rows), :]
         theirs = fin_in[...]
-        return jnp.where(n.c == 0, mine, theirs), jnp.where(n.c == 0, theirs, mine)
+        self.deliver(jnp.where(n.c == 0, mine, theirs), jnp.where(n.c == 0, theirs, mine))
+
+    def settle(self):
+        for wait in self.sent:
+            wait()
+            self.links.started.remove(wait)
+        self.sent = []
 
 
 def spread_lanes(parts, step):
@@ -744,9 +787,256 @@
     return jnp.where(upright(rows_form) == columns_form, 0.0, MASK_FILL)
 
 
-def staged(n, steps):
-    for index, step in steps.items():
-        pl.when(n == index)(step)
+FIRST_PLAN = (
+    "t.across0",
+    "u.across0",
+    "a.along",
+    "o.across0",
+    "a.across1",
+    "a.across0",
+    "t.along",
+    "a.across2",
+    "o.along",
+    "a.across3",
+    "t.across1",
+    "o.across1",
+    "o.across2",
+    "t.across2",
+    "d.along",
+    "bias",
+    "t.across3",
+    "a.onward0",
+    "a.onward1",
+    "a.onward2",
+    "t.onward0",
+    "a.onward3",
+    "u.along",
+    "t.onward2",
+    "t.onward1",
+    "t.onward3",
+    "a.beside",
+    "u.across1",
+    "o.across3",
+    "u.across2",
+    "turn",
+    "t.opposite",
+    "a.opposite",
+    "t.beside",
+    "u.across3",
+    "a.last",
+    "o.onward2",
+    "d.across1",
+    "t.last",
+    "vec",
+    "project",
+    "p0",
+    "p1",
+    "d.across2",
+    "p2",
+    "p3",
+    "o.onward0",
+    "o.onward1",
+    "o.onward3",
+    "attend",
+    "u.onward2",
+    "a0",
+    "o.beside",
+    "u.onward0",
+    "u.onward3",
+    "a1",
+    "u.onward1",
+    "a2",
+    "a3",
+    "d.across0",
+    "u.beside",
+    "a4",
+    "d.across3",
+    "a5",
+    "o.opposite",
+    "a6",
+    "a7",
+    "o.last",
+    "d.onward2",
+    "a8",
+    "a9",
+    "a10",
+    "u.opposite",
+    "a11",
+    "mix",
+    "m0",
+    "m1",
+    "d.onward0",
+    "d.onward1",
+    "m2",
+    "m3",
+    "u.last",
+    "widen",
+    "w0",
+    "d.onward3",
+    "d.beside",
+    "w1",
+    "w2",
+    "d.opposite",
+    "w3",
+    "d.last",
+    "narrow",
+)
+
+LAST_PLAN = (
+    "pre",
+    "ld",
+    "d.first",
+    "w0",
+    "w1",
+    "d.second0",
+    "w2",
+    "w3",
+    "wu0",
+    "d.second1",
+    "d.second2",
+    "wu1",
+    "wu2",
+    "d.third0",
+    "bc",
+    "u.first",
+    "n0",
+    "d.third1",
+    "n1",
+    "n2",
+    "n3",
+    "u.second0",
+    "u.second1",
+    "misc",
+    "g0",
+    "u.second2",
+    "u.second3",
+    "d.second3",
+    "g1",
+    "g2",
+    "g3",
+    "d.fourth",
+    "rd",
+    "wo0",
+    "wo1",
+    "wo2",
+    "a0",
+    "o.first",
+    "a1",
+    "o.second0",
+    "a2",
+    "u.third0",
+    "u.third1",
+    "o.second1",
+    "a3",
+    "a4",
+    "a5",
+    "a6",
+    "a7",
+    "u.fourth",
+    "o.third0",
+    "wm0",
+    "o.second2",
+    "o.third1",
+    "wm1",
+    "wm2",
+    "m.first",
+    "a8",
+    "m.second0",
+    "a9",
+    "m.second1",
+    "m.second2",
+    "a10",
+    "o.second3",
+    "m.third1",
+    "m.third0",
+    "a11",
+    "wr0",
+    "o.fourth",
+    "wr1",
+    "wr2",
+    "r.first",
+    "vec",
+    "r.second0",
+    "m.second3",
+    "r.second1",
+    "r.second2",
+    "m.fourth",
+    "t.first",
+    "u.trade",
+    "d.trade",
+    "b0",
+    "t.second0",
+    "b1",
+    "r.third1",
+    "r.third0",
+    "d.whole",
+    "r.second3",
+    "t.second1",
+    "t.second2",
+    "t.third1",
+    "u.whole",
+    "t.third0",
+    "t.second3",
+    "r.fourth",
+    "m.trade",
+    "t.fourth",
+    "o.trade",
+    "b2",
+    "b3",
+    "o.whole",
+    "r.trade",
+    "m.whole",
+    "t.trade",
+    "r.whole",
+    "t.whole",
+    "end",
+)
+
+
+class Plan:
+    def __init__(self, names, groups):
+        self.groups = groups
+        self.inside = {}
+        self.queue = list(names)
+
+    def call(self, name):
+        group, method = name.split(".")
+        if method[-1].isdigit():
+            getattr(self.groups[group], method[:-1])(int(method[-1]))
+        else:
+            getattr(self.groups[group], method)()
+
+    def until(self, name):
+        while True:
+            step = self.queue.pop(0)
+            if step == name:
+                return
+            self.call(step)
+
+    def loop(self, letter, first, count, body):
+        steps = {}
+        self.until(f"{letter}{first}")
+        for index in range(first, first + count):
+            steps[index] = []
+            ahead = f"{letter}{index + 1}"
+            while self.queue[0] != ahead and "." in self.queue[0]:
+                steps[index].append(self.queue.pop(0))
+            if index + 1 < first + count:
+                self.queue.pop(0)
+
+        def run(step, carry):
+            body(step)
+            for index, names in steps.items():
+                if names:
+
+                    @pl.when(step == index)
+                    def _(names=names):
+                        for name in names:
+                            self.call(name)
+
+            return carry
+
+        lax.fori_loop(first, first + count, run, 0)
 
 
 def attend_pair(r, p, qkv, context, logsums, bias):
@@ -848,11 +1138,29 @@
     stage[part_of(links.c, rows), :] = src[:, part_of(links.c, columns)]
 
 
-def joined(links, stage, sends, recvs, index, block):
-    rows = stage.shape[0] // 2
-    here = stage.at[part_of(1 - links.c, rows), :]
-    links.arrived(here, (sends.at[index], recvs.at[index]), links.to_core)
-    block(links.c, links.chip_own + links.z, 1)[...] = stage[...].astype(jnp.bfloat16)
+class Joined(Gather):
+    def join_from(self, stage, sends, recvs, index):
+        self.parts = (stage, sends, recvs, index)
+        return self
+
+    def join(self):
+        if self.parts is None:
+            return
+        n = self.links
+        stage, sends, recvs, index = self.parts
+        self.parts = None
+        rows = stage.shape[0] // 2
+        here = stage.at[part_of(1 - n.c, rows), :]
+        n.arrived(here, (sends.at[index], recvs.at[index]), n.to_core)
+        self.block(n.c, n.chip_own + n.z, 1)[...] = stage[...].astype(jnp.bfloat16)
+
+    def along(self):
+        self.join()
+        super().along()
+
+    def across(self, k):
+        self.join()
+        super().across(k)
 
 
 def passage_loss(r, similar, live_row, teacher_index, teacher_table):
@@ -957,14 +1265,16 @@
     count = tokens.shape[0]
     rows_dev = count // SEQ
     links = Links()
-    attn_block = rows_block(attn_mat, 48, 1152)
-    out_block = rows_block(attn_mat, 48, 384, 3 * WIDTH)
-    up_block = rows_block(up_mat, 48, 1536)
-    down_block = rows_block(down_mat, 192, 384)
-    attn = Gather(links, attn_block, sends, recvs, 0)
-    out = Gather(links, out_block, sends, recvs, 1)
-    up = Gather(links, up_block, sends, recvs, 2)
-    down = Gather(links, down_block, sends, recvs, 3)
+
+    def gather(block, group, stage):
+        return Joined(links, block, sends, recvs, group).join_from(
+            stage, half_sends, half_recvs, group
+        )
+
+    attn = gather(rows_block(attn_mat, 48, 1152), 0, stage_attn)
+    out = gather(rows_block(attn_mat, 48, 384, 3 * WIDTH), 1, stage_out)
+    up = gather(rows_block(up_mat, 48, 1536), 2, stage_up)
+    down = gather(rows_block(down_mat, 192, 384), 3, stage_down)
     tiny = Gather(links, lead_block(small_all), sends, recvs, 4)
     own_chip = links.chip_own + links.z
     kept = []
@@ -985,32 +1295,20 @@
 
     links.greet()
     halves(links, cat_attn, stage_attn, half_sends, half_recvs, 0)
-    tiny.first()
     halves(links, w_out, stage_out, half_sends, half_recvs, 1)
     halves(links, w_up, stage_up, half_sends, half_recvs, 2)
     halves(links, w_down, stage_down, half_sends, half_recvs, 3)
-    joined(links, stage_attn, half_sends, half_recvs, 0, attn_block)
-    attn.first()
-    joined(links, stage_out, half_sends, half_recvs, 1, out_block)
-    joined(links, stage_up, half_sends, half_recvs, 2, up_block)
-    joined(links, stage_down, half_sends, half_recvs, 3, down_block)
-    tiny.second()
-    attn.second()
-    out.first()
+    plan = Plan(FIRST_PLAN, {"a": attn, "o": out, "u": up, "d": down, "t": tiny})
+    plan.until("bias")
     live_rows = []
     for r in range(rows_dev):
         segment, live = segment_forms(segment_ids, row_lengths, r)
         live_rows.append(live)
         d_mid[r * SEQ : (r + 1) * SEQ, 0:SEQ] = mask_of(segment, live)
-    tiny.third()
-    attn.third()
-    out.second()
-    up.first()
+    plan.until("turn")
     turned[...] = tokens[...].T
     keep(turned, turned_hbm)
-    tiny.fourth()
-    tiny.last()
-
+    plan.until("vec")
     cores = [(i % 2, i // 2) for i in range(SHARDS)]
     for index, tile in enumerate(spread_lanes([small_all[c, n, 24:32, :] for c, n in cores], 24)):
         vectors[:, index * 128 : (index + 1) * 128] = rounded(tile)
@@ -1019,10 +1317,9 @@
     for r in range(CHIPS):
         both = jnp.concatenate([small_all[0, r, 0:24, :], small_all[1, r, 0:24, :]], axis=0)
         proj[r * 48 : (r + 1) * 48, :] = both.astype(jnp.bfloat16)
-    attn.fourth()
-    attn.last()
-
-    def project(step, carry):
+    plan.until("project")
+
+    def project(step):
         rows = part_of(step, CHUNK)
         part = tokens[rows, :]
         for index in range(3):
@@ -1031,47 +1328,34 @@
             if index != 1:
                 value = value + vectors[index // 2 : index // 2 + 1, :]
             qkv[rows, columns] = value.astype(jnp.bfloat16)
-        staged(step, {1: out.third, 2: up.second, 3: down.first})
-        return carry
-
-    lax.fori_loop(0, count // CHUNK, project, 0)
+
+    plan.loop("p", 0, count // CHUNK, project)
     keep(qkv, qkv_hbm)
-
-    def attend(item, carry):
+    plan.until("attend")
+
+    def attend(item):
         attend_pair(lax.div(item, PAIRS), lax.rem(item, PAIRS), qkv, context, logsums, d_mid)
-        staged(
-            item,
-            {
-                0: out.fourth,
-                2: up.third,
-                4: out.last,
-                5: down.second,
-                6: up.fourth,
-                8: up.last,
-                9: down.third,
-            },
-        )
-        return carry
-
-    lax.fori_loop(0, rows_dev * PAIRS, attend, 0)
+
+    plan.loop("a", 0, rows_dev * PAIRS, attend)
     keep(context, context_hbm)
+    plan.until("mix")
     keep(attn_mat, attn_hbm)
 
-    def mix(step, carry):
+    def mix(step):
         rows = part_of(step, CHUNK)
         mixed = dotted(context[rows, :], attn_mat[:, 3 * WIDTH :], 1, 0) + vectors[2:3, :]
         normed, scaled = norm_parts(tokens[rows, :].astype(jnp.float32) + mixed)
         normed_one[rows, :] = normed
         scaled_one[rows, :] = jnp.broadcast_to(scaled, (CHUNK, 128))
         low_one[rows, :] = (normed * vectors[3:4, :] + vectors[4:5, :]).astype(jnp.bfloat16)
-        return carry
-
-    lax.fori_loop(0, count // CHUNK, mix, 0)
+
+    plan.loop("m", 0, count // CHUNK, mix)
     keep(normed_one, normed_one_hbm)
     keep(low_one, low_one_hbm)
+    plan.until("widen")
     keep(up_mat, up_hbm)
 
-    def widen(step, carry):
+    def widen(step):
         rows = part_of(step, CHUNK)
         part = low_one[rows, :]
         for index in range(4):
@@ -1081,12 +1365,10 @@
             activated[rows, columns] = (upward * chance).astype(jnp.bfloat16)
             density = jnp.exp(-0.5 * upward * upward) * DENSITY_SCALE
             slope[rows, columns] = (chance + upward * density).astype(jnp.bfloat16)
-        staged(step, {1: down.fourth})
-        return carry
-
-    lax.fori_loop(0, count // CHUNK, widen, 0)
+
+    plan.loop("w", 0, count // CHUNK, widen)
     keep(slope, slope_hbm)
-    down.last()
+    plan.until("narrow")
     keep(down_mat, down_hbm)
 
     grad_vectors[...] = jnp.zeros_like(grad_vectors)
@@ -1258,17 +1540,11 @@
         row_lengths,
     ) = refs[:19]
     (
-        grad_tokens,
-        own_query,
-        own_key,
-        own_value,
-        own_out,
-        own_up,
+        grad_tokens_hbm,
+        own_rows,
         own_down,
-        own_proj,
-        *own_vectors,
-        own_up_bias,
-    ) = refs[19:36]
+        own_small,
+    ) = refs[19:23]
     (
         attn_mat,
         grads,
@@ -1285,8 +1561,12 @@
         sends,
         recvs,
         local_sems,
+        slope_sems,
+        qkv_sems,
+        grad_sems,
+        context,
         *rest,
-    ) = refs[36:]
+    ) = refs[23:]
     held = [rest[6 * i : 6 * i + 6] for i in range(6)]
     fins = [rest[36 + 2 * i : 38 + 2 * i] for i in range(5)]
     count = d_mid.shape[0]
@@ -1294,49 +1574,111 @@
     links = Links()
     c = links.c
 
-    def scatter(block, rows, group, mine=None):
+    def scatter(block, rows, group, deliver, mine=None):
         def own(chip):
             return block(c, chip, 1)
 
-        return Scatter(
-            links, block, own if mine is None else mine, rows, held[group], sends, recvs, group
-        )
-
-    down = scatter(
-        rows_block(grad_down_hbm, 192, 384), 192, 0, lambda chip: part_down.at[part_of(chip, 192), :]
-    )
-    up = scatter(rows_block(grads, 48, 1536), 48, 1)
-    out = scatter(rows_block(grads, 48, 384), 48, 2)
-    most = scatter(rows_block(grads, 48, 768, WIDTH), 48, 3)
-    rest_of = scatter(rows_block(grads, 48, 384, 3 * WIDTH), 48, 4)
-    tiny = scatter(lead_block(small_all), 1, 5)
+        own = own if mine is None else mine
+        fin = fins[group] if group < 5 else None
+        return Scatter(links, block, own, rows, held[group], fin, deliver, sends, recvs, group)
+
+    def down_mine(chip):
+        return part_down.at[part_of(chip, 192), :]
+
+    def halves_to(ref, start, columns):
+        def deliver(low, high):
+            ref[:, start : start + columns] = low
+            ref[:, start + columns : start + 2 * columns] = high
+
+        return deliver
+
+    def most_out(low, high):
+        own_rows[:, 0:512] = low[:, 0:512]
+        own_rows[:, 768:1024] = low[:, 512:768]
+        own_rows[:, 1024:1280] = high[:, 0:256]
+        own_rows[:, 1536:2048] = high[:, 256:768]
+
+    def rest_out(low, high):
+        own_rows[:, 512:768] = low[:, 0:256]
+        own_rows[:, 1280:1408] = low[:, 256:384]
+        own_rows[:, 1408:1536] = high[:, 0:128]
+        own_rows[:, 2048:2304] = high[:, 128:384]
+
+    def tiny_out(total):
+        own_small[...] = total[0]
+
+    down = scatter(rows_block(grad_down_hbm, 192, 384), 192, 0, halves_to(own_down, 0, WIDTH // 2), down_mine)
+    up = scatter(rows_block(grads, 48, 1536), 48, 1, halves_to(own_rows, HIDDEN, HIDDEN // 2))
+    out = scatter(rows_block(grads, 48, 384), 48, 2, halves_to(own_rows, 3 * WIDTH, WIDTH // 2))
+    most = scatter(rows_block(grads, 48, 768, WIDTH), 48, 3, most_out)
+    rest_of = scatter(rows_block(grads, 48, 384, 3 * WIDTH), 48, 4, rest_out)
+    tiny = scatter(lead_block(small_all), 1, 5, tiny_out)
 
     def load(src, dst, index):
-        copy = pltpu.make_async_copy(src, dst, local_sems.at[index])
-        copy.start()
-        return copy
-
+        return pltpu.make_async_copy(src, dst, local_sems.at[index])
+
+    def start(copies):
+        for copy in copies:
+            copy.start()
+
+    def wait(copies):
+        for copy in copies:
+            copy.wait()
+
+    plan = Plan(
+        LAST_PLAN, {"d": down, "u": up, "o": out, "m": most, "r": rest_of, "t": tiny}
+    )
+    plan.until("pre")
     first_loads = [
         load(d_branch_hbm, d_branch, 0),
+        load(grad_down_hbm.at[:, part_of(c, WIDTH // 2)], part_down, 1),
     ]
+    late_loads = [
+        load(context_hbm, context, 2),
+        load(attn_hbm, attn_mat, 3),
+        load(turned_hbm, turned, 4),
+    ]
+    start(first_loads[:1])
     links.greet()
-    down.first()
     grad_vectors[...] = part_vectors[...]
+    ones = jnp.ones((8, count), jnp.bfloat16)
+
+    def slope_load(step):
+        rows = part_of(step, CHUNK)
+        return pltpu.make_async_copy(slope_hbm.at[rows, :], wide.at[rows, :], slope_sems.at[step])
+
+    def qkv_load(step):
+        rows = part_of(step, CHUNK)
+        return pltpu.make_async_copy(
+            qkv_hbm.at[rows, :], wide.at[rows, 0 : 3 * WIDTH], qkv_sems.at[step]
+        )
+
+    def grad_store(step):
+        rows = part_of(step, CHUNK)
+        return pltpu.make_async_copy(
+            d_mid.at[rows, :], grad_tokens_hbm.at[rows, :], grad_sems.at[step]
+        )
+
+    steps = count // CHUNK
 
     def feed_forward(up_mat, down_mat, normed_one):
-        first = first_loads + [load(down_hbm, down_mat, 1), load(slope_hbm, wide, 2)]
-        later = [
-            load(low_one_hbm, low_one, 3),
-            load(grad_down_hbm.at[:, part_of(c, WIDTH // 2)], part_down, 4),
-            load(up_hbm, up_mat, 5),
-            load(d_mid_hbm, d_mid, 6),
-            load(normed_one_hbm, normed_one, 7),
+        ahead = [load(down_hbm, down_mat, 5)]
+        start(ahead)
+        for step in range(steps):
+            slope_load(step).start()
+        start(first_loads[1:])
+        middle = [
+            load(low_one_hbm, low_one, 6),
+            load(up_hbm, up_mat, 7),
+            load(d_mid_hbm, d_mid, 8),
+            load(normed_one_hbm, normed_one, 9),
         ]
-        for copy in first:
-            copy.wait()
-
-        def widen(step, carry):
+        plan.until("ld")
+        wait(first_loads[:1] + ahead)
+
+        def widen(step):
             rows = part_of(step, CHUNK)
+            slope_load(step).wait()
             part = d_branch[rows, :]
             for index in range(4):
                 columns = slice(index * WIDTH, (index + 1) * WIDTH)
@@ -1344,41 +1686,42 @@
                 wide[rows, columns] = (grad * wide[rows, columns].astype(jnp.float32)).astype(
                     jnp.bfloat16
                 )
-            return carry
-
-        lax.fori_loop(0, count // CHUNK, widen, 0)
-        for copy in later:
-            copy.wait()
-        down.second()
-
-        def weigh(step, carry):
+
+            @pl.when(step == 0)
+            def _():
+                wait(first_loads[1:])
+                start(middle)
+
+        plan.loop("w", 0, steps, widen)
+        wait(middle[:1])
+
+        def weigh(step):
             rows = part_of(step, CHUNK)
             part = low_one[:, rows].T
             for index in range(4):
                 columns = slice(index * WIDTH, (index + 1) * WIDTH)
                 grads[rows, columns] = dotted(part, wide[:, columns], 1, 0).astype(jnp.bfloat16)
-            return carry
-
-        lax.fori_loop(0, WIDTH // CHUNK, weigh, 0)
-        up.first()
-        ones = jnp.ones((8, count), jnp.bfloat16)
+
+        plan.loop("wu", 0, WIDTH // CHUNK, weigh)
+        plan.until("bc")
+        start(late_loads)
         for index in range(4):
             columns = slice(index * WIDTH, (index + 1) * WIDTH)
             grad_up_bias[:, columns] = dotted(ones, wide[:, columns], 1, 0)
-        down.third()
-
-        def narrow(step, carry):
+        wait(middle[1:])
+
+        def narrow(step):
             rows = part_of(step, CHUNK)
             d_hidden = d_mid[rows, :] + dotted(wide[rows, :], up_mat[...], 1, 1)
+            qkv_load(step).start()
             normed = normed_one[rows, :]
             d_mixed = norm_back(d_hidden, normed, scaled_one[rows, 0:1], vectors[3:4, :])
             d_mid[rows, :] = d_mixed
             d_branch[rows, :] = d_mixed.astype(jnp.bfloat16)
             grad_vectors[3:4, :] += jnp.sum(d_hidden * normed, 0, keepdims=True)
             grad_vectors[4:5, :] += jnp.sum(d_hidden, 0, keepdims=True)
-            return carry
-
-        lax.fori_loop(0, count // CHUNK, narrow, 0)
+
+        plan.loop("n", 0, steps, narrow)
 
     pl.run_scoped(
         feed_forward,
@@ -1387,90 +1730,41 @@
         pltpu.VMEM((count, WIDTH), jnp.float32),
     )
 
-    def attention(context, d_context, bias):
-        loads = [
-            load(context_hbm, context, 8),
-            load(attn_hbm, attn_mat, 9),
-            load(qkv_hbm, wide.at[:, 0 : 3 * WIDTH], 10),
-            load(turned_hbm, turned, 11),
-        ]
-        up.second()
-        links_first = len(links.started)
-        down.fourth()
-        ones = jnp.ones((8, count), jnp.bfloat16)
+    def attention(d_context, bias):
+        plan.until("misc")
         grad_vectors[2:3, :] = dotted(ones, d_branch[...], 1, 0)[0:1]
         for r in range(rows_dev):
             segment, live = segment_forms(segment_ids, row_lengths, r)
             bias[r] = mask_of(live, segment)
-        for copy in loads:
-            copy.wait()
-
-        def give(step, carry):
+        wait(late_loads)
+
+        def give(step):
             rows = part_of(step, CHUNK)
             d_context[rows, :] = dotted(d_branch[rows, :], attn_mat[:, 3 * WIDTH :], 1, 1).astype(
                 jnp.bfloat16
             )
-            return carry
-
-        lax.fori_loop(0, count // CHUNK, give, 0)
+
+        plan.loop("g", 0, steps, give)
+        plan.until("rd")
         row_dots(context, d_context, rowdots)
-        links.finish()
-
-        def weigh_out(step, carry):
+        up.settle()
+
+        def weigh_out(step):
             rows = part_of(step, CHUNK)
             part = context[:, rows].T
             grads[rows, 0:WIDTH] = dotted(part, d_branch[...], 1, 0).astype(jnp.bfloat16)
-            return carry
-
-        lax.fori_loop(0, WIDTH // CHUNK, weigh_out, 0)
-        out.first()
-
-        def down_trade():
-            down.trade(*fins[0])
-
-        def down_whole():
-            low, high = down.whole(*fins[0])
-            own_down[:, : WIDTH // 2] = low
-            own_down[:, WIDTH // 2 :] = high
-
-        def up_trade():
-            up.trade(*fins[1])
-
-        def up_whole():
-            low, high = up.whole(*fins[1])
-            own_up[:, : HIDDEN // 2] = low
-            own_up[:, HIDDEN // 2 :] = high
-
-        def out_trade():
-            out.trade(*fins[2])
-
-        def out_whole():
-            low, high = out.whole(*fins[2])
-            own_out[:, : WIDTH // 2] = low
-            own_out[:, WIDTH // 2 :] = high
-
-        def attend(first, steps):
-            def step(item, carry):
-                r = lax.rem(item, rows_dev)
-                p = lax.div(item, rows_dev)
-                attend_back_pair(r, p, wide, d_context, logsums, rowdots, bias)
-                staged(item, steps)
-                return carry
-
-            return step
-
-        lax.fori_loop(
-            0,
-            4 * rows_dev,
-            attend(
-                0,
-                {0: up.third, 1: out.second, 2: down_trade, 3: up.fourth, 4: out.third, 5: down_whole, 6: out.fourth, 7: up_trade},
-            ),
-            0,
-        )
+
+        plan.loop("wo", 0, WIDTH // CHUNK, weigh_out)
+        for step in range(steps):
+            qkv_load(step).wait()
+
+        def attend(item):
+            r = lax.rem(item, rows_dev)
+            p = lax.div(item, rows_dev)
+            attend_back_pair(r, p, wide, d_context, logsums, rowdots, bias)
 
         def weigh(first, pairs, base):
-            def step(step, carry):
+            def step(step):
                 rows = part_of(step, CHUNK)
                 part = turned[rows, :]
                 for index in range(3):
@@ -1479,32 +1773,23 @@
                     grads[rows, there : there + pairs * 128] = dotted(
                         part, wide[:, start : start + pairs * 128], 1, 0
                     ).astype(jnp.bfloat16)
-                return carry
-
-            lax.fori_loop(0, WIDTH // CHUNK, step, 0)
-
-        weigh(0, 4, WIDTH)
-        most.first()
-        lax.fori_loop(
-            4 * rows_dev,
-            6 * rows_dev,
-            attend(4 * rows_dev, {8: up_whole, 9: most.second, 10: out_trade, 11: most.third}),
-            0,
-        )
-        weigh(4, 2, 3 * WIDTH)
-        rest_of.first()
-        out_whole()
-        for index in (0, 2):
-            total = dotted(ones, wide[:, index * WIDTH : (index + 1) * WIDTH], 1, 0)
-            grad_vectors[index // 2 : index // 2 + 1, :] = total[0:1]
+
+            return step
+
+        plan.loop("a", 0, 4 * rows_dev, attend)
+        plan.loop("wm", 0, WIDTH // CHUNK, weigh(0, 4, WIDTH))
+        plan.loop("a", 4 * rows_dev, 2 * rows_dev, attend)
+        plan.loop("wr", 0, WIDTH // CHUNK, weigh(4, 2, 3 * WIDTH))
 
     pl.run_scoped(
         attention,
         pltpu.VMEM((count, WIDTH), jnp.bfloat16),
-        pltpu.VMEM((count, WIDTH), jnp.bfloat16),
         pltpu.VMEM((rows_dev, SEQ, SEQ), jnp.float32),
     )
-
+    plan.until("vec")
+    for index in (0, 2):
+        total = dotted(ones, wide[:, index * WIDTH : (index + 1) * WIDTH], 1, 0)
+        grad_vectors[index // 2 : index // 2 + 1, :] = total[0:1]
     tiles = [grad_vectors[:, i * 128 : (i + 1) * 128] for i in range(WIDTH // 128)]
     for i, part in enumerate(pick_lanes(tiles, 24, SHARDS)):
         small_all[i % 2, i // 2, 24:32, :] = part
@@ -1512,40 +1797,17 @@
     for i, part in enumerate(pick_lanes(tiles, 96, SHARDS)):
         small_all[i % 2, i // 2, 32:40, :] = part
         small_all[i % 2, i // 2, 0:24, :] = grad_proj[i * 24 : (i + 1) * 24, :]
-    tiny.first()
-
-    def back(step, carry):
+
+    def back(step):
         rows = part_of(step, CHUNK)
         value = dotted(wide[rows, 0 : 3 * WIDTH], attn_mat[:, 0 : 3 * WIDTH], 1, 1)
-        grad_tokens[rows, :] = value + d_mid[rows, :]
-        return carry
-
-    most.fourth()
-    rest_of.second()
-    tiny.second()
-    lax.fori_loop(0, 2, back, 0)
-    rest_of.third()
-    tiny.third()
-    lax.fori_loop(2, 4, back, 0)
-    rest_of.fourth()
-    tiny.fourth()
-    most.trade(*fins[3])
-    rest_of.trade(*fins[4])
-    total = tiny.fifth()[0]
-    own_proj[...] = total[0:24, :]
-    for index, ref in enumerate(own_vectors):
-        ref[...] = total[24 + index : 25 + index, 0:24].reshape(24)
-    own_up_bias[...] = total[32:33, 0:96].reshape(96)
-    low, high = most.whole(*fins[3])
-    own_query[:, 0:512] = low[:, 0:512]
-    own_key[:, 0:256] = low[:, 512:768]
-    own_key[:, 256:512] = high[:, 0:256]
-    own_value[:, 0:512] = high[:, 256:768]
-    low, high = rest_of.whole(*fins[4])
-    own_query[:, 512:768] = low[:, 0:256]
-    own_key[:, 512:640] = low[:, 256:384]
-    own_key[:, 640:768] = high[:, 0:128]
-    own_value[:, 512:768] = high[:, 128:384]
+        d_mid[rows, :] += value
+        grad_store(step).start()
+
+    plan.loop("b", 0, steps, back)
+    plan.until("end")
+    for step in range(steps):
+        grad_store(step).wait()
     links.finish()
 
 
@@ -1575,18 +1837,12 @@
         last_kernel,
         out_shape=[
             array(count, WIDTH),
-            array(24, WIDTH),
-            array(24, WIDTH),
-            array(24, WIDTH),
-            array(24, WIDTH),
-            array(24, HIDDEN),
+            array(24, 2 * HIDDEN),
             array(96, WIDTH),
-            array(24, EMBED),
-        ]
-        + [array(24)] * 8
-        + [array(96)],
+            array(SMALL, 128),
+        ],
         in_specs=[anywhere] * 12 + [vmem] * 6 + [smem],
-        out_specs=[vmem] * 17,
+        out_specs=[anywhere] + [vmem] * 3,
         scratch_shapes=[
             pltpu.VMEM((WIDTH, HIDDEN), low),
             pltpu.VMEM((WIDTH, HIDDEN), low),
@@ -1602,7 +1858,11 @@
             pltpu.VMEM((8, HIDDEN), wide),
             pltpu.SemaphoreType.DMA((6, Scatter.SEMS)),
             pltpu.SemaphoreType.DMA((6, Scatter.SEMS)),
-            pltpu.SemaphoreType.DMA((12,)),
+            pltpu.SemaphoreType.DMA((10,)),
+            pltpu.SemaphoreType.DMA((count // CHUNK,)),
+            pltpu.SemaphoreType.DMA((count // CHUNK,)),
+            pltpu.SemaphoreType.DMA((count // CHUNK,)),
+            pltpu.VMEM((count, WIDTH), low),
         ]
         + buffers,
         compiler_params=pltpu.CompilerParams(
@@ -1610,6 +1870,77 @@
         ),
         name="backward_scatter",
     )(*kept, segment_ids, row_lengths)
+
+
+def pass_kernel(*refs):
+    sources, losses = refs[:5], refs[5]
+    grad_tokens, embeddings, query, key, value, out, up, down, proj, *vectors = refs[6:23]
+    up_bias, own_losses = refs[23:25]
+    held, (in_sems, out_sems) = refs[25:30], refs[30:]
+    pieces = 4
+    through = []
+    for src, mid, dst in zip(sources[:2], held[:2], (grad_tokens, embeddings)):
+        rows = src.shape[0] // pieces
+        for piece in range(pieces):
+            part = pl.ds(piece * rows, rows)
+            index = len(through)
+            through.append(
+                (
+                    pltpu.make_async_copy(src.at[part], mid.at[part], in_sems.at[index]),
+                    pltpu.make_async_copy(mid.at[part], dst.at[part], out_sems.at[index]),
+                )
+            )
+    small = [
+        pltpu.make_async_copy(src, mid, in_sems.at[2 * pieces + index])
+        for index, (src, mid) in enumerate(zip(sources[2:], held[2:]))
+    ]
+    for copy in small:
+        copy.start()
+    for here, _ in through:
+        here.start()
+    for copy in small:
+        copy.wait()
+    rows, down_in, small_in = held[2:]
+    for index, ref in enumerate((query, key, value, out)):
+        ref[...] = rows[:, index * WIDTH : (index + 1) * WIDTH]
+    up[...] = rows[:, HIDDEN:]
+    down[...] = down_in[...]
+    proj[...] = small_in[0:24, :]
+    for index, ref in enumerate(vectors):
+        ref[...] = small_in[24 + index : 25 + index, 0:24].reshape(24)
+    up_bias[...] = small_in[32:33, 0:96].reshape(96)
+    for index in range(losses.shape[0]):
+        own_losses[index] = losses[index]
+    for here, there in through:
+        here.wait()
+        there.start()
+    for _, there in through:
+        there.wait()
+
+
+def run_pass(*arrays):
+    vmem = pl.BlockSpec(memory_space=pltpu.VMEM)
+    smem = pl.BlockSpec(memory_space=pltpu.SMEM)
+    anywhere = pl.BlockSpec(memory_space=pl.ANY)
+
+    def array(*shape):
+        return jax.ShapeDtypeStruct(shape, jnp.float32)
+
+    whole = [array(*a.shape) for a in arrays]
+    return pl.pallas_call(
+        pass_kernel,
+        out_shape=whole[:2]
+        + [array(24, WIDTH)] * 4
+        + [array(24, HIDDEN), array(96, WIDTH), array(24, EMBED)]
+        + [array(24)] * 8
+        + [array(96), whole[-1]],
+        in_specs=[anywhere] * 5 + [smem],
+        out_specs=[anywhere] * 2 + [vmem] * 16 + [smem],
+        scratch_shapes=[pltpu.VMEM(a.shape, a.dtype) for a in arrays[:5]]
+        + [pltpu.SemaphoreType.DMA((11,)), pltpu.SemaphoreType.DMA((8,))],
+        compiler_params=pltpu.CompilerParams(vmem_limit_bytes=62 * 2**20),
+        name="hand_over",
+    )(*arrays)
 
 
 def body_tiles(
@@ -1645,8 +1976,10 @@
         teacher_index,
         teacher_table,
     )
+    grad_tokens, *small = run_last(kept, segment_ids, row_lengths)
     (
         grad_tokens,
+        embeddings,
         grad_query,
         grad_key,
         grad_value,
@@ -1663,10 +1996,11 @@
         grad_gain_second,
         grad_shift_second,
         grad_up_bias,
-    ) = run_last(kept, segment_ids, row_lengths)
+        losses,
+    ) = run_pass(grad_tokens, embeddings.reshape(rows_dev * SEQ, EMBED), *small, losses)
     return (
         losses,
-        embeddings,
+        embeddings.reshape(rows_dev, SEQ, EMBED),
         grad_tokens.reshape(rows_dev, SEQ, width),
         grad_query,
         grad_query_bias,

time: 238 us -> 193 us (0.81)
  Pallas kernels: 222 us -> 192 us
  local copies, waits for them, and re-layouts: 14.4 us -> 0 us
    pallas_call x1 -> x2, Pallas kernels: 114 us -> 90.9 us  [the longest x1 85.8 us: run_last(): pl.pallas_call(last_kernel, out_shape=[array(count, WIDTH), array(24, 2 *...]
    unnamed x55 -> x0, local copies, waits for them, and re-layouts: 14.4 us -> none
    pallas_call x1, Pallas kernels: 108 us -> 101 us  [run_first(): pl.pallas_call(first_kernel, out_shape=[array(wide, rows_dev), array(wide...]
where the time goes in v2:
time: 193 us
  Pallas kernels  192 us (99%)
    pallas_call x1, Pallas kernels, run_first(): pl.pallas_call(first_kernel, out_shape=[array(wide, rows_dev), array(wide...  101 us
    pallas_call x1, Pallas kernels, run_last(): pl.pallas_call(last_kernel, out_shape=[array(count, WIDTH), array(24, 2 *...  85.8 us
    pallas_call x1, Pallas kernels, run_pass(): pl.pallas_call(pass_kernel, out_shape=whole[:2] + [array(24, WIDTH)] * 4...  5.03 us

profile of v2, /device:TPU:0, one launch (start us, length us, event | category | flops | bytes accessed | tf_op | source)
XLA Modules:
  0.0 193.0 jit_solution(8504738150749984276)
XLA Ops:
  0.7 101.2 %forward_gather.1 = (f32[2]{0:T(128)}, f32[2,512,128]{2,1,0:T(8,128)}, bf16[768,3072]{1,0:T(8,128)(2,1)}, bf16[768,3072]{1,0:T(8,128)(2,1)}, bf16[3072,768]{1,0:...) custom-call(bf16[1024,768]{1,0:T(8,128)(2,1)} %bitcast.4, ...), custom_call_target="tpu_custom_call" | custom-call | tf_op jit(solution)/shard_map/forward_gather/pallas_call | solution.py:1456
  101.9 85.8 %backward_scatter.1 = (f32[1024,768]{1,0:T(8,128)}, f32[24,6144]{1,0:T(8,128)}, f32[96,768]{1,0:T(8,128)}, f32[40,128]{1,0:T(8,128)}) custom-call(bf16[768,3072]{1,0:T(8,128)(2,1)} %get-tuple-element.61.refs_0_, bf16[768,3072]{1,0:T(8,128)(2,1)} %get-tuple-element.62.refs_1_, bf16[3072,768]{1,0:T(8,128)(2,1)} %get-tuple-element.63.refs_2_, ...), custom_call_target="tpu_custom_call" | custom-call | tf_op jit(solution)/shard_map/backward_scatter/pallas_call | solution.py:1836
  187.7 5.0 %hand_over.1 = (f32[1024,768]{1,0:T(8,128)}, f32[1024,128]{1,0:T(8,128)}, f32[24,768]{1,0:T(8,128)}, f32[24,768]{1,0:T(8,128)}, f32[24,768]{1,0:T(8,128)}, /*ind...) custom-call(f32[1024,768]{1,0:T(8,128)} %get-tuple-element.78.refs_0, ...), custom_call_target="tpu_custom_call" | custom-call | tf_op jit(solution)/shard_map/hand_over/pallas_call | solution.py:1930

commit v3 on v2

--- a/solution.py
+++ b/solution.py
@@ -376,7 +376,8 @@
 
 
 MESH = pl.DeviceIdType.MESH
-EXP2_SCALE = 1.4426950408889634 / math.sqrt(HEAD)
+LOG2_E = 1.4426950408889634
+EXP2_SCALE = LOG2_E / math.sqrt(HEAD)
 SHARDS = 32
 CHIPS = 16
 WIDTH = 768
@@ -385,6 +386,7 @@
 SMALL = 40
 PAIRS = HEADS // 2
 CHUNK = 256
+HALF = 512
 
 
 def fits(mesh):
@@ -510,6 +512,35 @@
     return block
 
 
+def column_of(chip):
+    return lax.div(chip, 4)
+
+
+def level_of(chip):
+    return lax.rem(chip, 4)
+
+
+def grid_block(ref, columns, base=0):
+    def block(core, chip, count):
+        lanes = pl.ds(pl.multiple_of(base + core * columns, 128), columns)
+        if count == 4:
+            return ref.at[column_of(chip), :, :, lanes]
+        if count == 0:
+            return ref.at[:, level_of(chip), :, lanes]
+        return ref.at[column_of(chip), level_of(chip), :, lanes]
+
+    return block
+
+
+def lead_grid_block(ref):
+    def block(core, chip, count):
+        if count == 0:
+            return ref.at[core, :, level_of(chip)]
+        return ref.at[core, column_of(chip), level_of(chip)]
+
+    return block
+
+
 class Gather:
     Z, X, Y, FX, FY, C, ZF = 0, 3, 7, 11, 13, 15, 19
     SEMS = 21
@@ -593,11 +624,81 @@
             self.take(chip, 4, self.C + index, n.to_core, 1 - n.c)
 
 
+class LevelGather(Gather):
+    X, Y, F, Z, ZF, C = 0, 1, 2, 3, 6, 8
+
+    def own(self):
+        n = self.links
+        chip = self.step_of(n.chip_own, 0)
+        self.ship(chip, 1, self.X, n.to_x)
+        self.ship(chip, 1, self.Y, n.to_y)
+
+    def diag(self):
+        n = self.links
+        chip = self.step_of(n.chip_x, 0)
+        self.take(chip, 1, self.X, n.to_x)
+        self.ship(chip, 1, self.F, n.to_y)
+
+    def set(self, k):
+        n = self.links
+        level = self.step_of(n.chip_own, k)
+        if k == 0:
+            self.take(self.step_of(n.chip_y, 0), 1, self.Y, n.to_y)
+            self.take(self.step_of(n.chip_d, 0), 1, self.F, n.to_y)
+            self.ship(level, 0, self.Z, n.to_pair)
+            self.ship(level, 0, self.Z + 1, n.to_middle, inner=True)
+        else:
+            self.take(level, 0, self.Z + k - 1, n.to_pair if k == 1 else n.to_middle)
+            if k == 1:
+                self.ship(level, 0, self.Z + 2, n.to_middle, inner=True)
+            else:
+                self.ship(level, 0, self.ZF + k - 2, n.to_pair, self.Z + k - 1, inner=True)
+        self.ship(level, 0, self.C + k, n.to_core)
+
+    def last(self):
+        n = self.links
+        for k in range(4):
+            self.take(self.step_of(n.chip_own, k), 0, self.C + k, n.to_core, 1 - n.c)
+
+
+class Joined:
+    def join_from(self, stage, sends, recvs, index):
+        self.parts = (stage, sends, recvs, index)
+        return self
+
+    def join(self):
+        if self.parts is None:
+            return
+        n = self.links
+        stage, sends, recvs, index = self.parts
+        self.parts = None
+        rows = stage.shape[0] // 2
+        here = stage.at[part_of(1 - n.c, rows), :]
+        n.arrived(here, (sends.at[index], recvs.at[index]), n.to_core)
+        self.block(n.c, n.chip_own + n.z, 1)[...] = stage[...].astype(jnp.bfloat16)
+
+
+class JoinedGather(Joined, Gather):
+    def along(self):
+        self.join()
+        super().along()
+
+    def across(self, k):
+        self.join()
+        super().across(k)
+
+
+class JoinedLevelGather(Joined, LevelGather):
+    def own(self):
+        self.join()
+        super().own()
+
+
 class Scatter:
     C, DY, DX, OX, OY, Z, F = 0, 4, 5, 6, 8, 10, 13
     SEMS = 14
 
-    def __init__(self, links, block, mine, rows, held, fin, deliver, sends, recvs, group):
+    def __init__(self, links, block, mine, rows, held, fin, deliver, sends, recvs, group, whole=False):
         self.links = links
         self.block = block
         self.mine = mine
@@ -610,6 +711,7 @@
         self.group = group
         n = links
         self.sent = []
+        self.once = whole
         self.columns = (n.chip_d, n.chip_x, n.chip_y, n.chip_own)
 
     def at(self, ref, start, count):
@@ -647,6 +749,9 @@
 
     def first(self):
         n = self.links
+        if self.once:
+            self.ship(lambda: (self.block(1 - n.c, 0, 16), self.at(self.part, 0, 16)), self.C, n.to_core)
+            return
         for index, chip in enumerate(self.columns):
 
             def ends(chip=chip):
@@ -657,9 +762,20 @@
 
     def second(self, index):
         n = self.links
+        if self.once:
+            self.take(self.part, 0, 16, self.C, n.to_core)
+            self.add(16, 0, self.mine)
+            for index in range(3):
+                self.pass_on(index)
+            return
         chip = self.columns[index]
         self.take(self.part, chip, 4, self.C + index, n.to_core)
         self.add(4, chip, lambda i: self.mine(chip + i))
+        self.pass_on(index)
+
+    def pass_on(self, index):
+        n = self.links
+        chip = self.columns[index]
         if index == 0:
             self.ship_part(chip, 2, self.d_y, 0, self.DY, n.to_y)
             self.ship_part(lambda: chip + 2, 2, self.d_x, 0, self.DX, n.to_x)
@@ -788,157 +904,146 @@
 
 
 FIRST_PLAN = (
-    "t.across0",
+    "o.own",
+    "t.own",
+    "a.along",
+    "u.along",
+    "a.across0",
+    "t.diag",
     "u.across0",
-    "a.along",
-    "o.across0",
     "a.across1",
-    "a.across0",
-    "t.along",
     "a.across2",
-    "o.along",
+    "t.set0",
     "a.across3",
-    "t.across1",
-    "o.across1",
-    "o.across2",
-    "t.across2",
+    "bias",
     "d.along",
-    "bias",
-    "t.across3",
     "a.onward0",
     "a.onward1",
     "a.onward2",
-    "t.onward0",
+    "t.set1",
+    "o.diag",
     "a.onward3",
-    "u.along",
-    "t.onward2",
-    "t.onward1",
-    "t.onward3",
     "a.beside",
+    "t.set2",
     "u.across1",
-    "o.across3",
     "u.across2",
     "turn",
-    "t.opposite",
+    "t.set3",
     "a.opposite",
-    "t.beside",
-    "u.across3",
-    "a.last",
-    "o.onward2",
-    "d.across1",
     "t.last",
     "vec",
+    "a.last",
     "project",
+    "u.across3",
+    "o.set0",
     "p0",
     "p1",
+    "p2",
+    "d.across1",
+    "p3",
+    "attend",
+    "u.onward0",
+    "a0",
+    "a1",
+    "a2",
+    "u.onward2",
+    "a3",
     "d.across2",
-    "p2",
-    "p3",
-    "o.onward0",
-    "o.onward1",
-    "o.onward3",
-    "attend",
-    "u.onward2",
-    "a0",
-    "o.beside",
-    "u.onward0",
+    "u.onward1",
     "u.onward3",
-    "a1",
-    "u.onward1",
-    "a2",
-    "a3",
-    "d.across0",
-    "u.beside",
     "a4",
-    "d.across3",
+    "o.set1",
     "a5",
-    "o.opposite",
     "a6",
+    "o.set2",
     "a7",
-    "o.last",
-    "d.onward2",
     "a8",
     "a9",
+    "o.set3",
+    "u.beside",
+    "d.across0",
     "a10",
+    "a11",
+    "o.last",
+    "mix",
+    "d.across3",
+    "d.onward2",
+    "m0",
     "u.opposite",
-    "a11",
-    "mix",
-    "m0",
     "m1",
+    "m2",
+    "m3",
     "d.onward0",
     "d.onward1",
-    "m2",
-    "m3",
     "u.last",
     "widen",
     "w0",
-    "d.onward3",
-    "d.beside",
     "w1",
     "w2",
+    "d.onward3",
+    "w3",
+    "w4",
+    "d.beside",
+    "w5",
+    "w6",
+    "w7",
+    "w8",
     "d.opposite",
-    "w3",
+    "w9",
+    "w10",
+    "w11",
     "d.last",
     "narrow",
 )
 
 LAST_PLAN = (
     "pre",
+    "d.first",
+    "d.second0",
     "ld",
-    "d.first",
     "w0",
+    "d.second1",
     "w1",
-    "d.second0",
     "w2",
+    "d.second2",
     "w3",
     "wu0",
-    "d.second1",
-    "d.second2",
     "wu1",
+    "d.third0",
     "wu2",
-    "d.third0",
     "bc",
     "u.first",
+    "d.third1",
     "n0",
-    "d.third1",
     "n1",
-    "n2",
-    "n3",
     "u.second0",
     "u.second1",
     "misc",
+    "d.second3",
     "g0",
+    "d.fourth",
     "u.second2",
+    "rd",
     "u.second3",
-    "d.second3",
-    "g1",
-    "g2",
-    "g3",
-    "d.fourth",
-    "rd",
     "wo0",
-    "wo1",
-    "wo2",
     "a0",
+    "a1",
     "o.first",
-    "a1",
-    "o.second0",
+    "u.third0",
     "a2",
-    "u.third0",
     "u.third1",
-    "o.second1",
     "a3",
     "a4",
     "a5",
     "a6",
+    "o.second0",
     "a7",
     "u.fourth",
-    "o.third0",
     "wm0",
-    "o.second2",
-    "o.third1",
     "wm1",
     "wm2",
+    "o.third0",
+    "o.third1",
     "m.first",
     "a8",
     "m.second0",
@@ -946,48 +1051,39 @@
     "m.second1",
     "m.second2",
     "a10",
-    "o.second3",
+    "a11",
     "m.third1",
     "m.third0",
-    "a11",
+    "m.second3",
     "wr0",
-    "o.fourth",
     "wr1",
     "wr2",
     "r.first",
+    "o.fourth",
     "vec",
     "r.second0",
-    "m.second3",
-    "r.second1",
-    "r.second2",
-    "m.fourth",
     "t.first",
     "u.trade",
-    "d.trade",
+    "m.fourth",
     "b0",
+    "r.third1",
+    "r.third0",
     "t.second0",
     "b1",
-    "r.third1",
-    "r.third0",
+    "r.fourth",
+    "t.third0",
+    "d.trade",
+    "t.third1",
+    "t.fourth",
+    "u.whole",
+    "o.trade",
+    "r.trade",
     "d.whole",
-    "r.second3",
-    "t.second1",
-    "t.second2",
-    "t.third1",
-    "u.whole",
-    "t.third0",
-    "t.second3",
-    "r.fourth",
     "m.trade",
-    "t.fourth",
-    "o.trade",
-    "b2",
-    "b3",
+    "t.trade",
+    "m.whole",
+    "r.whole",
     "o.whole",
-    "r.trade",
-    "m.whole",
-    "t.trade",
-    "r.whole",
     "t.whole",
     "end",
 )
@@ -1039,13 +1135,47 @@
         lax.fori_loop(first, first + count, run, 0)
 
 
-def attend_pair(r, p, qkv, context, logsums, bias):
+def lanes_in_head(shape):
+    return lax.broadcasted_iota(jnp.int32, shape, 1) & (HEAD - 1)
+
+
+def low_head(shape):
+    return lax.broadcasted_iota(jnp.int32, shape, 1) < HEAD
+
+
+def two_parts(value):
+    first = rounded(value)
+    return first, value - first
+
+
+def three_parts(value):
+    first, rest = two_parts(value)
+    second, third = two_parts(rest)
+    return first, second, third
+
+
+PARTS = 16
+
+
+def query_codes(segment):
+    lane = lanes_in_head((SEQ, 128)).astype(jnp.float32)
+    return jnp.where(lane == upright(segment), 1.0, 0.0).astype(jnp.bfloat16)
+
+
+def key_codes(live):
+    lane = lanes_in_head((SEQ, 128))
+    hidden = jnp.where(lane.astype(jnp.float32) == upright(live), 0.0, MASK_FILL)
+    parts = jnp.where((lane >= PARTS) & (lane < PARTS + 3), 1.0, 0.0)
+    return jnp.where(lane <= NPASS, hidden, parts).astype(jnp.bfloat16)
+
+
+def attend_pair(r, p, qkv, context, codes, bias, segments):
     rows = part_of(r, SEQ)
     columns = pl.multiple_of(p * 128, 128)
     query = qkv[rows, pl.ds(columns, 128)]
     key = qkv[rows, pl.ds(columns + WIDTH, 128)]
     value = qkv[rows, pl.ds(columns + 2 * WIDTH, 128)]
-    low = lax.broadcasted_iota(jnp.int32, (SEQ, 128), 1) < HEAD
+    low = low_head((SEQ, 128))
     zero = jnp.zeros_like(key)
     outs, sums = [], []
     for j in range(2):
@@ -1058,58 +1188,69 @@
         outs.append(out * (1.0 / total))
         sums.append(peak + jnp.log2(total))
     context[rows, pl.ds(columns, 128)] = jnp.where(low, outs[0], outs[1]).astype(jnp.bfloat16)
-    turned = jnp.where(low, sums[0], sums[1]).T
-    logsums[r, p, 0:1] = turned[0:1]
-    logsums[r, p, 1:2] = turned[HEAD : HEAD + 1]
-
-
-def attend_back_pair(r, p, qkv, d_context, logsums, rowdots, bias):
+    first, second, third = three_parts(jnp.where(low, sums[1], sums[0]) * (-1.0 / EXP2_SCALE))
+    lane = lanes_in_head((SEQ, 128))
+    code = jnp.where(lane == PARTS + 2, third, segments[rows, :].astype(jnp.float32))
+    code = jnp.where(lane == PARTS + 1, second, code)
+    code = jnp.where(lane == PARTS, first, code)
+    codes[rows, pl.ds(columns, 128)] = code.astype(jnp.bfloat16)
+
+
+def dot_codes(r, p, context, d_context, codes):
+    rows = part_of(r, SEQ)
+    columns = part_of(p, 128)
+    both = context[rows, columns].astype(jnp.float32) * d_context[rows, columns].astype(jnp.float32)
+    first, second = two_parts(both)
+    shape = (128, 128)
+    other = low_head(shape) != (lax.broadcasted_iota(jnp.int32, shape, 0) < HEAD)
+    other = jnp.where(other, -1.0, 0.0).astype(jnp.bfloat16)
+    total = dotted(first.astype(jnp.bfloat16), other, 1, 0)
+    total = total + dotted(second.astype(jnp.bfloat16), other, 1, 0)
+    first, second = two_parts(total)
+    lane = lanes_in_head((SEQ, 128))
+    code = jnp.where(lane == PARTS, first, jnp.where(lane == PARTS + 1, second, 0.0))
+    codes[rows, columns] = code.astype(jnp.bfloat16)
+
+
+def pick_head(masks, j, value, code):
+    return value * masks[j] + code * masks[1 - j]
+
+
+def attend_back_pair(r, p, qkv, d_context, query_code, grad_code, key_code, value_code, lows):
     rows = part_of(r, SEQ)
     columns = pl.multiple_of(p * 128, 128)
     query = qkv[rows, pl.ds(columns, 128)]
     key = qkv[rows, pl.ds(columns + WIDTH, 128)]
     value = qkv[rows, pl.ds(columns + 2 * WIDTH, 128)]
     grad = d_context[rows, pl.ds(columns, 128)]
-    low = lax.broadcasted_iota(jnp.int32, (SEQ, 128), 1) < HEAD
-    zero = jnp.zeros_like(key)
-    d_query, d_key, d_value = None, [], []
+    query_c = query_code[rows, pl.ds(columns, 128)]
+    grad_c = grad_code[rows, pl.ds(columns, 128)]
+    key_c = key_code[rows, :]
+    value_c = value_code[...]
+    masks = (lows[0], lows[1])
+    d_query, d_key, d_value = [], [], []
     for j in range(2):
-        pick = (lambda a: jnp.where(low, a, zero)) if j == 0 else (lambda a: jnp.where(low, zero, a))
-        key_j = pick(key)
-        scores = dotted(key_j, query, 1, 1) * EXP2_SCALE + bias[r]
-        chances = jnp.exp2(scores - logsums[r, p, j : j + 1, :])
-        d_chances = dotted(pick(value), grad, 1, 1)
-        d_scores = (chances * (d_chances - rowdots[r, p, j : j + 1, :])).astype(jnp.bfloat16)
+        scores = dotted(pick_head(masks, j, key, key_c), pick_head(masks, j, query, query_c), 1, 1)
+        chances = jnp.exp2(scores * EXP2_SCALE)
+        d_chances = dotted(
+            pick_head(masks, j, value, value_c), pick_head(masks, j, grad, grad_c), 1, 1
+        )
+        d_scores = (chances * d_chances).astype(jnp.bfloat16)
         d_value.append(dotted(chances.astype(jnp.bfloat16), grad, 1, 0))
         d_key.append(dotted(d_scores, query, 1, 0))
-        term = dotted(d_scores, key_j, 0, 0)
-        d_query = term if d_query is None else d_query + term
+        d_query.append(dotted(d_scores, key, 0, 0))
+    low = low_head((SEQ, 128))
     scale = 1.0 / math.sqrt(HEAD)
     low_type = jnp.bfloat16
-    qkv[rows, pl.ds(columns, 128)] = (d_query * scale).astype(low_type)
+    qkv[rows, pl.ds(columns, 128)] = (jnp.where(low, d_query[0], d_query[1]) * scale).astype(
+        low_type
+    )
     qkv[rows, pl.ds(columns + WIDTH, 128)] = (
         jnp.where(low, d_key[0], d_key[1]) * scale
     ).astype(low_type)
     qkv[rows, pl.ds(columns + 2 * WIDTH, 128)] = jnp.where(low, d_value[0], d_value[1]).astype(
         low_type
     )
-
-
-def row_dots(context, d_context, rowdots):
-    shape = (8, 128)
-    head = lax.broadcasted_iota(jnp.int32, shape, 1) // HEAD
-    pick = (head == lax.broadcasted_iota(jnp.int32, shape, 0)).astype(jnp.float32)
-    for r in range(rowdots.shape[0]):
-        for p in range(PAIRS):
-            part = (slice(r * SEQ, (r + 1) * SEQ), slice(p * 128, (p + 1) * 128))
-            both = context[part].astype(jnp.float32) * d_context[part].astype(jnp.float32)
-            rowdots[r, p] = lax.dot_general(
-                pick,
-                both,
-                (((1,), (1,)), ((), ())),
-                precision=lax.Precision.HIGHEST,
-                preferred_element_type=jnp.float32,
-            )
 
 
 def norm_parts(mixed):
@@ -1136,31 +1277,6 @@
 
     links.send(ends, lambda: (sends.at[index], recvs.at[index]), links.to_core)
     stage[part_of(links.c, rows), :] = src[:, part_of(links.c, columns)]
-
-
-class Joined(Gather):
-    def join_from(self, stage, sends, recvs, index):
-        self.parts = (stage, sends, recvs, index)
-        return self
-
-    def join(self):
-        if self.parts is None:
-            return
-        n = self.links
-        stage, sends, recvs, index = self.parts
-        self.parts = None
-        rows = stage.shape[0] // 2
-        here = stage.at[part_of(1 - n.c, rows), :]
-        n.arrived(here, (sends.at[index], recvs.at[index]), n.to_core)
-        self.block(n.c, n.chip_own + n.z, 1)[...] = stage[...].astype(jnp.bfloat16)
-
-    def along(self):
-        self.join()
-        super().along()
-
-    def across(self, k):
-        self.join()
-        super().across(k)
 
 
 def passage_loss(r, similar, live_row, teacher_index, teacher_table):
@@ -1224,11 +1340,11 @@
         d_mid_hbm,
         d_branch_hbm,
         grad_down_hbm,
+        codes_hbm,
         scaled_one,
         vectors,
         grad_vectors,
         grad_proj,
-        logsums,
     ) = refs[21:40]
     (
         attn_mat,
@@ -1255,6 +1371,8 @@
         normed_two,
         scaled_two,
         low_two,
+        codes,
+        segments,
         sends,
         recvs,
         half_sends,
@@ -1266,16 +1384,16 @@
     rows_dev = count // SEQ
     links = Links()
 
-    def gather(block, group, stage):
-        return Joined(links, block, sends, recvs, group).join_from(
+    def gather(kind, block, group, stage):
+        return kind(links, block, sends, recvs, group).join_from(
             stage, half_sends, half_recvs, group
         )
 
-    attn = gather(rows_block(attn_mat, 48, 1152), 0, stage_attn)
-    out = gather(rows_block(attn_mat, 48, 384, 3 * WIDTH), 1, stage_out)
-    up = gather(rows_block(up_mat, 48, 1536), 2, stage_up)
-    down = gather(rows_block(down_mat, 192, 384), 3, stage_down)
-    tiny = Gather(links, lead_block(small_all), sends, recvs, 4)
+    attn = gather(JoinedGather, grid_block(attn_mat, 1152), 0, stage_attn)
+    out = gather(JoinedLevelGather, grid_block(attn_mat, 384, 3 * WIDTH), 1, stage_out)
+    up = gather(JoinedGather, rows_block(up_mat, 48, 1536), 2, stage_up)
+    down = gather(JoinedGather, rows_block(down_mat, 192, 384), 3, stage_down)
+    tiny = LevelGather(links, lead_grid_block(small_all), sends, recvs, 4)
     own_chip = links.chip_own + links.z
     kept = []
 
@@ -1286,7 +1404,7 @@
 
     for index, ref in enumerate((w_query, w_key, w_value)):
         cat_attn[:, index * WIDTH : (index + 1) * WIDTH] = ref[...]
-    own_small = small_all.at[links.c, own_chip]
+    own_small = tiny.block(links.c, own_chip, 1)
     own_small[0:24, :] = w_proj[...]
     own_small[24:40, :] = jnp.zeros((16, 128), jnp.float32)
     for index, ref in enumerate(vector_refs):
@@ -1305,45 +1423,48 @@
         segment, live = segment_forms(segment_ids, row_lengths, r)
         live_rows.append(live)
         d_mid[r * SEQ : (r + 1) * SEQ, 0:SEQ] = mask_of(segment, live)
+        segments[r * SEQ : (r + 1) * SEQ, :] = query_codes(segment)
     plan.until("turn")
     turned[...] = tokens[...].T
     keep(turned, turned_hbm)
     plan.until("vec")
-    cores = [(i % 2, i // 2) for i in range(SHARDS)]
-    for index, tile in enumerate(spread_lanes([small_all[c, n, 24:32, :] for c, n in cores], 24)):
+    cores = [(i % 2, i // 8, i // 2 % 4) for i in range(SHARDS)]
+    for index, tile in enumerate(spread_lanes([small_all[c, n, m, 24:32, :] for c, n, m in cores], 24)):
         vectors[:, index * 128 : (index + 1) * 128] = rounded(tile)
-    for index, tile in enumerate(spread_lanes([small_all[c, n, 32:40, :] for c, n in cores], 96)):
+    for index, tile in enumerate(spread_lanes([small_all[c, n, m, 32:40, :] for c, n, m in cores], 96)):
         up_bias[:, index * 128 : (index + 1) * 128] = rounded(tile)
     for r in range(CHIPS):
-        both = jnp.concatenate([small_all[0, r, 0:24, :], small_all[1, r, 0:24, :]], axis=0)
+        both = [small_all[c, r // 4, r % 4, 0:24, :] for c in range(2)]
+        both = jnp.concatenate(both, axis=0)
         proj[r * 48 : (r + 1) * 48, :] = both.astype(jnp.bfloat16)
     plan.until("project")
 
     def project(step):
         rows = part_of(step, CHUNK)
-        part = tokens[rows, :]
-        for index in range(3):
-            columns = slice(index * WIDTH, (index + 1) * WIDTH)
-            value = dotted(part, attn_mat[:, columns], 1, 0)
-            if index != 1:
-                value = value + vectors[index // 2 : index // 2 + 1, :]
-            qkv[rows, columns] = value.astype(jnp.bfloat16)
+        weights = attn_mat[:, :, :, 0 : 3 * WIDTH].reshape(WIDTH, 3 * WIDTH)
+        value = dotted(tokens[rows, :], weights, 1, 0)
+        qkv[rows, 0:WIDTH] = (value[:, 0:WIDTH] + vectors[0:1, :]).astype(jnp.bfloat16)
+        qkv[rows, WIDTH : 2 * WIDTH] = value[:, WIDTH : 2 * WIDTH].astype(jnp.bfloat16)
+        qkv[rows, 2 * WIDTH :] = (value[:, 2 * WIDTH :] + vectors[1:2, :]).astype(jnp.bfloat16)
 
     plan.loop("p", 0, count // CHUNK, project)
     keep(qkv, qkv_hbm)
     plan.until("attend")
 
     def attend(item):
-        attend_pair(lax.div(item, PAIRS), lax.rem(item, PAIRS), qkv, context, logsums, d_mid)
+        r, p = lax.div(item, PAIRS), lax.rem(item, PAIRS)
+        attend_pair(r, p, qkv, context, codes, d_mid, segments)
 
     plan.loop("a", 0, rows_dev * PAIRS, attend)
     keep(context, context_hbm)
+    keep(codes, codes_hbm)
     plan.until("mix")
     keep(attn_mat, attn_hbm)
 
     def mix(step):
         rows = part_of(step, CHUNK)
-        mixed = dotted(context[rows, :], attn_mat[:, 3 * WIDTH :], 1, 0) + vectors[2:3, :]
+        weights = attn_mat[:, :, :, 3 * WIDTH :].reshape(WIDTH, WIDTH)
+        mixed = dotted(context[rows, :], weights, 1, 0) + vectors[2:3, :]
         normed, scaled = norm_parts(tokens[rows, :].astype(jnp.float32) + mixed)
         normed_one[rows, :] = normed
         scaled_one[rows, :] = jnp.broadcast_to(scaled, (CHUNK, 128))
@@ -1356,17 +1477,14 @@
     keep(up_mat, up_hbm)
 
     def widen(step):
-        rows = part_of(step, CHUNK)
-        part = low_one[rows, :]
-        for index in range(4):
-            columns = slice(index * WIDTH, (index + 1) * WIDTH)
-            upward = dotted(part, up_mat[:, columns], 1, 0) + up_bias[0:1, columns]
-            chance = 0.5 * (1.0 + lax.erf(upward * ROOT_HALF))
-            activated[rows, columns] = (upward * chance).astype(jnp.bfloat16)
-            density = jnp.exp(-0.5 * upward * upward) * DENSITY_SCALE
-            slope[rows, columns] = (chance + upward * density).astype(jnp.bfloat16)
-
-    plan.loop("w", 0, count // CHUNK, widen)
+        columns = part_of(step, CHUNK)
+        upward = dotted(low_one[...], up_mat[:, columns], 1, 0) + up_bias[0:1, columns]
+        chance = 0.5 * (1.0 + lax.erf(upward * ROOT_HALF))
+        density = jnp.exp2(upward * upward * (-0.5 * LOG2_E)) * DENSITY_SCALE
+        activated[:, columns] = (upward * chance).astype(jnp.bfloat16)
+        slope[:, columns] = (chance + upward * density).astype(jnp.bfloat16)
+
+    plan.loop("w", 0, HIDDEN // CHUNK, widen)
     keep(slope, slope_hbm)
     plan.until("narrow")
     keep(down_mat, down_hbm)
@@ -1375,18 +1493,13 @@
     grad_proj[...] = jnp.zeros_like(grad_proj)
     for r in range(rows_dev):
 
-        def narrow(step, carry):
-            here = part_of(step, CHUNK)
-            rows = pl.ds(pl.multiple_of(r * SEQ + step * CHUNK, CHUNK), CHUNK)
-            mixed = dotted(activated[rows, :], down_mat[...], 1, 0) + vectors[5:6, :]
-            mixed = mixed + (normed_one[rows, :] * vectors[3:4, :] + vectors[4:5, :])
-            normed, scaled = norm_parts(mixed)
-            normed_two[here, :] = normed
-            scaled_two[here, :] = jnp.broadcast_to(scaled, (CHUNK, 128))
-            low_two[here, :] = (normed * vectors[6:7, :] + vectors[7:8, :]).astype(jnp.bfloat16)
-            return carry
-
-        lax.fori_loop(0, SEQ // CHUNK, narrow, 0)
+        rows = slice(r * SEQ, (r + 1) * SEQ)
+        mixed = dotted(activated[rows, :], down_mat[...], 1, 0) + vectors[5:6, :]
+        mixed = mixed + (normed_one[rows, :] * vectors[3:4, :] + vectors[4:5, :])
+        normed, scaled = norm_parts(mixed)
+        normed_two[...] = normed
+        scaled_two[...] = jnp.broadcast_to(scaled, (SEQ, 128))
+        low_two[...] = (normed * vectors[6:7, :] + vectors[7:8, :]).astype(jnp.bfloat16)
         raw = dotted(low_two[...], proj[...], 1, 0)
         inverse = lax.rsqrt(jnp.sum(raw * raw, -1, keepdims=True) + UNIT_EPS)
         embedded = raw * inverse
@@ -1417,7 +1530,7 @@
 
     def grad_copy(step, slot):
         return pltpu.make_async_copy(
-            grad_down.at[slot], grad_down_hbm.at[part_of(step, CHUNK), :], grad_sems.at[slot]
+            grad_down.at[slot], grad_down_hbm.at[part_of(step, WIDTH), :], grad_sems.at[slot]
         )
 
     def weigh(step, carry):
@@ -1427,12 +1540,12 @@
         def _():
             grad_copy(step - 2, slot).wait()
 
-        part = activated[:, part_of(step, CHUNK)]
+        part = activated[:, part_of(step, WIDTH)]
         grad_down[slot] = dotted(part, d_branch[...], 0, 0).astype(jnp.bfloat16)
         grad_copy(step, slot).start()
         return carry
 
-    steps = HIDDEN // CHUNK
+    steps = HIDDEN // WIDTH
     lax.fori_loop(0, steps, weigh, 0)
     for step in (steps - 2, steps - 1):
         grad_copy(step, step % 2).wait()
@@ -1458,7 +1571,7 @@
         out_shape=[
             array(wide, rows_dev),
             array(wide, rows_dev, SEQ, EMBED),
-            array(low, WIDTH, HIDDEN),
+            array(low, 4, 4, 48, HIDDEN),
             array(low, WIDTH, HIDDEN),
             array(low, HIDDEN, WIDTH),
             array(low, WIDTH, count),
@@ -1470,16 +1583,16 @@
             array(wide, count, WIDTH),
             array(low, count, WIDTH),
             array(low, HIDDEN, WIDTH),
+            array(low, count, WIDTH),
             array(wide, count, 128),
             array(wide, 8, WIDTH),
             array(wide, 8, WIDTH),
             array(wide, WIDTH, EMBED),
-            array(wide, rows_dev, PAIRS, 8, SEQ),
         ],
         in_specs=[vmem] * 18 + [smem] * 3,
-        out_specs=[smem, vmem] + [anywhere] * 12 + [vmem] * 5,
+        out_specs=[smem, vmem] + [anywhere] * 13 + [vmem] * 4,
         scratch_shapes=[
-            pltpu.VMEM((WIDTH, HIDDEN), low),
+            pltpu.VMEM((4, 4, 48, HIDDEN), low),
             pltpu.VMEM((WIDTH, HIDDEN), low),
             pltpu.VMEM((HIDDEN, WIDTH), low),
             pltpu.VMEM((WIDTH, count), low),
@@ -1491,8 +1604,8 @@
             pltpu.VMEM((count, HIDDEN), low),
             pltpu.VMEM((count, WIDTH), wide),
             pltpu.VMEM((count, WIDTH), low),
-            pltpu.VMEM((2, CHUNK, WIDTH), low),
-            pltpu.VMEM((2, CHIPS, SMALL, 128), wide),
+            pltpu.VMEM((2, WIDTH, WIDTH), low),
+            pltpu.VMEM((2, 4, 4, SMALL, 128), wide),
             pltpu.VMEM((24, 3 * WIDTH), wide),
             pltpu.VMEM((48, 3 * WIDTH // 2), wide),
             pltpu.VMEM((48, WIDTH // 2), wide),
@@ -1503,11 +1616,13 @@
             pltpu.VMEM((SEQ, WIDTH), wide),
             pltpu.VMEM((SEQ, 128), wide),
             pltpu.VMEM((SEQ, WIDTH), low),
+            pltpu.VMEM((count, WIDTH), low),
+            pltpu.VMEM((count, 128), low),
             pltpu.SemaphoreType.DMA((5, Gather.SEMS)),
             pltpu.SemaphoreType.DMA((5, Gather.SEMS)),
             pltpu.SemaphoreType.DMA((4,)),
             pltpu.SemaphoreType.DMA((4,)),
-            pltpu.SemaphoreType.DMA((12,)),
+            pltpu.SemaphoreType.DMA((13,)),
             pltpu.SemaphoreType.DMA((2,)),
         ],
         compiler_params=pltpu.CompilerParams(
@@ -1531,11 +1646,11 @@
         d_mid_hbm,
         d_branch_hbm,
         grad_down_hbm,
+        codes_hbm,
         scaled_one,
         vectors,
         part_vectors,
         grad_proj,
-        logsums,
         segment_ids,
         row_lengths,
     ) = refs[:19]
@@ -1550,12 +1665,10 @@
         grads,
         wide,
         low_one,
-        turned,
         d_branch,
         d_mid,
         part_down,
         small_all,
-        rowdots,
         grad_vectors,
         grad_up_bias,
         sends,
@@ -1564,7 +1677,9 @@
         slope_sems,
         qkv_sems,
         grad_sems,
-        context,
+        key_code,
+        value_code,
+        lows,
         *rest,
     ) = refs[23:]
     held = [rest[6 * i : 6 * i + 6] for i in range(6)]
@@ -1580,7 +1695,9 @@
 
         own = own if mine is None else mine
         fin = fins[group] if group < 5 else None
-        return Scatter(links, block, own, rows, held[group], fin, deliver, sends, recvs, group)
+        return Scatter(
+            links, block, own, rows, held[group], fin, deliver, sends, recvs, group, group in (2, 4, 5)
+        )
 
     def down_mine(chip):
         return part_down.at[part_of(chip, 192), :]
@@ -1633,40 +1750,42 @@
         load(d_branch_hbm, d_branch, 0),
         load(grad_down_hbm.at[:, part_of(c, WIDTH // 2)], part_down, 1),
     ]
-    late_loads = [
-        load(context_hbm, context, 2),
-        load(attn_hbm, attn_mat, 3),
-        load(turned_hbm, turned, 4),
-    ]
-    start(first_loads[:1])
+    attn_load = load(attn_hbm, attn_mat, 3)
+    start(first_loads)
     links.greet()
+    wait(first_loads[1:])
     grad_vectors[...] = part_vectors[...]
     ones = jnp.ones((8, count), jnp.bfloat16)
 
     def slope_load(step):
-        rows = part_of(step, CHUNK)
-        return pltpu.make_async_copy(slope_hbm.at[rows, :], wide.at[rows, :], slope_sems.at[step])
+        columns = part_of(step, WIDTH)
+        return pltpu.make_async_copy(
+            slope_hbm.at[:, columns], wide.at[:, columns], slope_sems.at[step]
+        )
 
     def qkv_load(step):
-        rows = part_of(step, CHUNK)
+        rows = part_of(step, HALF)
         return pltpu.make_async_copy(
             qkv_hbm.at[rows, :], wide.at[rows, 0 : 3 * WIDTH], qkv_sems.at[step]
         )
 
     def grad_store(step):
-        rows = part_of(step, CHUNK)
+        rows = part_of(step, HALF)
         return pltpu.make_async_copy(
             d_mid.at[rows, :], grad_tokens_hbm.at[rows, :], grad_sems.at[step]
         )
 
-    steps = count // CHUNK
+    steps = count // HALF
+    quarters = HIDDEN // WIDTH
+
+    def weights(start, columns):
+        return attn_mat[:, :, :, start : start + columns].reshape(WIDTH, columns)
 
     def feed_forward(up_mat, down_mat, normed_one):
         ahead = [load(down_hbm, down_mat, 5)]
         start(ahead)
-        for step in range(steps):
+        for step in range(quarters):
             slope_load(step).start()
-        start(first_loads[1:])
         middle = [
             load(low_one_hbm, low_one, 6),
             load(up_hbm, up_mat, 7),
@@ -1677,41 +1796,32 @@
         wait(first_loads[:1] + ahead)
 
         def widen(step):
-            rows = part_of(step, CHUNK)
+            columns = part_of(step, WIDTH)
             slope_load(step).wait()
-            part = d_branch[rows, :]
-            for index in range(4):
-                columns = slice(index * WIDTH, (index + 1) * WIDTH)
-                grad = dotted(part, down_mat[columns, :], 1, 1)
-                wide[rows, columns] = (grad * wide[rows, columns].astype(jnp.float32)).astype(
-                    jnp.bfloat16
-                )
+            grad = dotted(d_branch[...], down_mat[columns, :], 1, 1)
+            wide[:, columns] = (grad * wide[:, columns].astype(jnp.float32)).astype(jnp.bfloat16)
 
             @pl.when(step == 0)
             def _():
-                wait(first_loads[1:])
                 start(middle)
 
-        plan.loop("w", 0, steps, widen)
+        plan.loop("w", 0, quarters, widen)
         wait(middle[:1])
 
         def weigh(step):
             rows = part_of(step, CHUNK)
-            part = low_one[:, rows].T
-            for index in range(4):
-                columns = slice(index * WIDTH, (index + 1) * WIDTH)
-                grads[rows, columns] = dotted(part, wide[:, columns], 1, 0).astype(jnp.bfloat16)
+            grads[rows, :] = dotted(low_one[:, rows], wide[...], 0, 0).astype(jnp.bfloat16)
 
         plan.loop("wu", 0, WIDTH // CHUNK, weigh)
         plan.until("bc")
-        start(late_loads)
+        attn_load.start()
         for index in range(4):
             columns = slice(index * WIDTH, (index + 1) * WIDTH)
             grad_up_bias[:, columns] = dotted(ones, wide[:, columns], 1, 0)
         wait(middle[1:])
 
         def narrow(step):
-            rows = part_of(step, CHUNK)
+            rows = part_of(step, HALF)
             d_hidden = d_mid[rows, :] + dotted(wide[rows, :], up_mat[...], 1, 1)
             qkv_load(step).start()
             normed = normed_one[rows, :]
@@ -1730,61 +1840,73 @@
         pltpu.VMEM((count, WIDTH), jnp.float32),
     )
 
-    def attention(d_context, bias):
+    def attention(d_context, context, codes, turned):
+        loads = [
+            load(context_hbm, context, 2),
+            load(codes_hbm, codes, 4),
+            load(turned_hbm, turned, 10),
+        ]
+        start(loads)
         plan.until("misc")
         grad_vectors[2:3, :] = dotted(ones, d_branch[...], 1, 0)[0:1]
         for r in range(rows_dev):
-            segment, live = segment_forms(segment_ids, row_lengths, r)
-            bias[r] = mask_of(live, segment)
-        wait(late_loads)
-
-        def give(step):
-            rows = part_of(step, CHUNK)
-            d_context[rows, :] = dotted(d_branch[rows, :], attn_mat[:, 3 * WIDTH :], 1, 1).astype(
-                jnp.bfloat16
-            )
-
-        plan.loop("g", 0, steps, give)
+            _, live = segment_forms(segment_ids, row_lengths, r)
+            key_code[r * SEQ : (r + 1) * SEQ, :] = key_codes(live)
+        low = low_head((SEQ, 128))
+        lows[0] = jnp.where(low, 1.0, 0.0).astype(jnp.bfloat16)
+        lows[1] = jnp.where(low, 0.0, 1.0).astype(jnp.bfloat16)
+        lane = lanes_in_head((SEQ, 128))
+        parts = (lane == PARTS) | (lane == PARTS + 1)
+        value_code[...] = jnp.where(parts, 1.0, 0.0).astype(jnp.bfloat16)
+        attn_load.wait()
+
+        plan.until("g0")
+        d_context[...] = dotted(d_branch[...], weights(3 * WIDTH, WIDTH), 1, 1).astype(jnp.bfloat16)
         plan.until("rd")
-        row_dots(context, d_context, rowdots)
+
+        wait(loads[:1])
+
+        def gather_dots(item, carry):
+            dot_codes(lax.rem(item, rows_dev), lax.div(item, rows_dev), context, d_context, low_one)
+            return carry
+
+        lax.fori_loop(0, rows_dev * PAIRS, gather_dots, 0)
         up.settle()
 
-        def weigh_out(step):
-            rows = part_of(step, CHUNK)
-            part = context[:, rows].T
-            grads[rows, 0:WIDTH] = dotted(part, d_branch[...], 1, 0).astype(jnp.bfloat16)
-
-        plan.loop("wo", 0, WIDTH // CHUNK, weigh_out)
+        plan.until("wo0")
+        grads[:, 0:WIDTH] = dotted(context[...], d_branch[...], 0, 0).astype(jnp.bfloat16)
         for step in range(steps):
             qkv_load(step).wait()
+
+        wait(loads[1:])
 
         def attend(item):
             r = lax.rem(item, rows_dev)
             p = lax.div(item, rows_dev)
-            attend_back_pair(r, p, wide, d_context, logsums, rowdots, bias)
+            attend_back_pair(
+                r, p, wide, d_context, codes, low_one, key_code, value_code, lows
+            )
 
         def weigh(first, pairs, base):
-            def step(step):
-                rows = part_of(step, CHUNK)
-                part = turned[rows, :]
-                for index in range(3):
-                    start = index * WIDTH + first * 128
-                    there = base + index * pairs * 128
-                    grads[rows, there : there + pairs * 128] = dotted(
-                        part, wide[:, start : start + pairs * 128], 1, 0
-                    ).astype(jnp.bfloat16)
+            def step(index):
+                size = pairs * 128
+                here = pl.ds(pl.multiple_of(index * WIDTH + first * 128, 128), size)
+                there = pl.ds(pl.multiple_of(base + index * size, 128), size)
+                grads[:, there] = dotted(turned[...], wide[:, here], 1, 0).astype(jnp.bfloat16)
 
             return step
 
         plan.loop("a", 0, 4 * rows_dev, attend)
-        plan.loop("wm", 0, WIDTH // CHUNK, weigh(0, 4, WIDTH))
+        plan.loop("wm", 0, 3, weigh(0, 4, WIDTH))
         plan.loop("a", 4 * rows_dev, 2 * rows_dev, attend)
-        plan.loop("wr", 0, WIDTH // CHUNK, weigh(4, 2, 3 * WIDTH))
+        plan.loop("wr", 0, 3, weigh(4, 2, 3 * WIDTH))
 
     pl.run_scoped(
         attention,
         pltpu.VMEM((count, WIDTH), jnp.bfloat16),
-        pltpu.VMEM((rows_dev, SEQ, SEQ), jnp.float32),
+        pltpu.VMEM((count, WIDTH), jnp.bfloat16),
+        pltpu.VMEM((count, WIDTH), jnp.bfloat16),
+        pltpu.VMEM((WIDTH, count), jnp.bfloat16),
     )
     plan.until("vec")
     for index in (0, 2):
@@ -1799,8 +1921,8 @@
         small_all[i % 2, i // 2, 0:24, :] = grad_proj[i * 24 : (i + 1) * 24, :]
 
     def back(step):
-        rows = part_of(step, CHUNK)
-        value = dotted(wide[rows, 0 : 3 * WIDTH], attn_mat[:, 0 : 3 * WIDTH], 1, 1)
+        rows = part_of(step, HALF)
+        value = dotted(wide[rows, 0 : 3 * WIDTH], weights(0, 3 * WIDTH), 1, 1)
         d_mid[rows, :] += value
         grad_store(step).start()
 
@@ -1841,28 +1963,28 @@
             array(96, WIDTH),
             array(SMALL, 128),
         ],
-        in_specs=[anywhere] * 12 + [vmem] * 6 + [smem],
+        in_specs=[anywhere] * 13 + [vmem] * 5 + [smem],
         out_specs=[anywhere] + [vmem] * 3,
         scratch_shapes=[
-            pltpu.VMEM((WIDTH, HIDDEN), low),
+            pltpu.VMEM((4, 4, 48, HIDDEN), low),
             pltpu.VMEM((WIDTH, HIDDEN), low),
             pltpu.VMEM((count, HIDDEN), low),
             pltpu.VMEM((count, WIDTH), low),
-            pltpu.VMEM((WIDTH, count), low),
             pltpu.VMEM((count, WIDTH), low),
             pltpu.VMEM((count, WIDTH), wide),
             pltpu.VMEM((HIDDEN, WIDTH // 2), low),
             pltpu.VMEM((2, CHIPS, SMALL, 128), wide),
-            pltpu.VMEM((rows_dev, PAIRS, 8, SEQ), wide),
             pltpu.VMEM((8, WIDTH), wide),
             pltpu.VMEM((8, HIDDEN), wide),
             pltpu.SemaphoreType.DMA((6, Scatter.SEMS)),
             pltpu.SemaphoreType.DMA((6, Scatter.SEMS)),
-            pltpu.SemaphoreType.DMA((10,)),
-            pltpu.SemaphoreType.DMA((count // CHUNK,)),
-            pltpu.SemaphoreType.DMA((count // CHUNK,)),
-            pltpu.SemaphoreType.DMA((count // CHUNK,)),
-            pltpu.VMEM((count, WIDTH), low),
+            pltpu.SemaphoreType.DMA((11,)),
+            pltpu.SemaphoreType.DMA((HIDDEN // WIDTH,)),
+            pltpu.SemaphoreType.DMA((count // HALF,)),
+            pltpu.SemaphoreType.DMA((count // HALF,)),
+            pltpu.VMEM((count, 128), low),
+            pltpu.VMEM((SEQ, 128), low),
+            pltpu.VMEM((2, SEQ, 128), low),
         ]
         + buffers,
         compiler_params=pltpu.CompilerParams(

time: 193 us -> 179 us (0.927)
  Pallas kernels: 192 us -> 178 us
    pallas_call x1, Pallas kernels: 101 us -> 93.9 us  [run_first(): pl.pallas_call(first_kernel, out_shape=[array(wide, rows_dev), array(wide...]
    pallas_call x1, Pallas kernels: 85.8 us -> 79.2 us  [run_last(): pl.pallas_call(last_kernel, out_shape=[array(count, WIDTH), array(24, 2 *...]
where the time goes in v3:
time: 179 us
  Pallas kernels  178 us (99%)
    pallas_call x1, Pallas kernels, run_first(): pl.pallas_call(first_kernel, out_shape=[array(wide, rows_dev), array(wide...  93.9 us
    pallas_call x1, Pallas kernels, run_last(): pl.pallas_call(last_kernel, out_shape=[array(count, WIDTH), array(24, 2 *...  79.2 us
    pallas_call x1, Pallas kernels, run_pass(): pl.pallas_call(pass_kernel, out_shape=whole[:2] + [array(24, WIDTH)] * 4...  5.03 us

profile of v3, /device:TPU:0, one launch (start us, length us, event | category | flops | bytes accessed | tf_op | source)
XLA Modules:
  0.0 179.1 jit_solution(16243023912138346542)
XLA Ops:
  0.7 93.9 %forward_gather.1 = (f32[2]{0:T(128)}, f32[2,512,128]{2,1,0:T(8,128)}, bf16[4,4,48,3072]{3,2,1,0:T(8,128)(2,1)}, bf16[768,3072]{1,0:T(8,128)(2,1)}, bf16[3072,76...) custom-call(bf16[1024,768]{1,0:T(8,128)(2,1)} %bitcast.4, ...), custom_call_target="tpu_custom_call" | custom-call | tf_op jit(solution)/shard_map/forward_gather/pallas_call | solution.py:1569
  94.6 79.2 %backward_scatter.1 = (f32[1024,768]{1,0:T(8,128)}, f32[24,6144]{1,0:T(8,128)}, f32[96,768]{1,0:T(8,128)}, f32[40,128]{1,0:T(8,128)}) custom-call(bf16[4,4,48,3072]{3,2,1,0:T(8,128)(2,1)} %get-tuple-element.61.refs_0_, bf16[768,3072]{1,0:T(8,128)(2,1)} %get-tuple-element.62.refs_1_, bf16[3072,768]{1,0:T(8,128)(2,1)} %get-tuple-element.63.refs_2_, ...), custom_call_target="tpu_custom_call" | custom-call | tf_op jit(solution)/shard_map/backward_scatter/pallas_call | solution.py:1958
  173.9 5.0 %hand_over.1 = (f32[1024,768]{1,0:T(8,128)}, f32[1024,128]{1,0:T(8,128)}, f32[24,768]{1,0:T(8,128)}, f32[24,768]{1,0:T(8,128)}, f32[24,768]{1,0:T(8,128)}, /*ind...) custom-call(f32[1024,768]{1,0:T(8,128)} %get-tuple-element.78.refs_0, ...), custom_call_target="tpu_custom_call" | custom-call | tf_op jit(solution)/shard_map/hand_over/pallas_call | solution.py:2052

commit v4 on v3

--- a/solution.py
+++ b/solution.py
@@ -443,12 +443,14 @@
         self.levels = [z, paired, near, last]
         self.started = []
 
+    def hail(self):
+        barrier = pltpu.get_barrier_semaphore()
+        self.partners = [self.to_core, self.to_x, self.to_y] + self.to_z[1:]
+        for partner in self.partners:
+            pl.semaphore_signal(barrier, inc=1, device_id=partner, device_id_type=MESH)
+
     def greet(self):
-        barrier = pltpu.get_barrier_semaphore()
-        partners = [self.to_core, self.to_x, self.to_y] + self.to_z[1:]
-        for partner in partners:
-            pl.semaphore_signal(barrier, inc=1, device_id=partner, device_id_type=MESH)
-        pl.semaphore_wait(barrier, len(partners))
+        pl.semaphore_wait(pltpu.get_barrier_semaphore(), len(self.partners))
 
     def level(self, k):
         return lax.rem(self.z + k, 4)
@@ -712,6 +714,7 @@
         n = links
         self.sent = []
         self.once = whole
+        self.span = 4 if whole else 2
         self.columns = (n.chip_d, n.chip_x, n.chip_y, n.chip_own)
 
     def at(self, ref, start, count):
@@ -737,15 +740,17 @@
         self.links.arrived(self.at(ref, start, count), self.sems(index), source)
 
     def add(self, count, start, *others):
+        size = min(count, self.span)
+
         def step(i, carry):
-            here = self.at(self.part, start + i, 1)
-            total = here[...].astype(jnp.float32)
+            here = self.at(self.part, start + i * size, size)
+            total = here[...]
             for other in others:
-                total = total + other(i)[...].astype(jnp.float32)
-            here[...] = total.astype(self.part.dtype)
+                total = total + other(i * size, size)[...]
+            here[...] = total
             return carry
 
-        lax.fori_loop(0, count, step, 0)
+        lax.fori_loop(0, count // size, step, 0)
 
     def first(self):
         n = self.links
@@ -770,7 +775,7 @@
             return
         chip = self.columns[index]
         self.take(self.part, chip, 4, self.C + index, n.to_core)
-        self.add(4, chip, lambda i: self.mine(chip + i))
+        self.add(4, chip, lambda i, size: self.mine(chip + i, size))
         self.pass_on(index)
 
     def pass_on(self, index):
@@ -788,11 +793,11 @@
         n = self.links
         if index == 0:
             self.take(self.d_y, 0, 2, self.DY, n.to_y)
-            self.add(2, n.chip_x, lambda i: self.at(self.d_y, i, 1))
+            self.add(2, n.chip_x, lambda i, size: self.at(self.d_y, i, size))
             self.ship_part(n.chip_x, 2, self.o_x, 0, self.OX, n.to_x)
             return
         self.take(self.d_x, 0, 2, self.DX, n.to_x)
-        self.add(2, n.chip_y + 2, lambda i: self.at(self.d_x, i, 1))
+        self.add(2, n.chip_y + 2, lambda i, size: self.at(self.d_x, i, size))
         self.ship_part(lambda: n.chip_y + 2, 2, self.o_y, 2, self.OY + 1, n.to_y)
 
     def fourth(self):
@@ -804,8 +809,8 @@
         self.add(
             4,
             n.chip_own,
-            lambda i: self.at(self.o_x, i, 1),
-            lambda i: self.at(self.o_y, i, 1),
+            lambda i, size: self.at(self.o_x, i, size),
+            lambda i, size: self.at(self.o_y, i, size),
         )
         for j in (1, 2, 3):
 
@@ -848,8 +853,9 @@
 
     def settle(self):
         for wait in self.sent:
-            wait()
-            self.links.started.remove(wait)
+            if wait in self.links.started:
+                wait()
+                self.links.started.remove(wait)
         self.sent = []
 
 
@@ -904,86 +910,86 @@
 
 
 FIRST_PLAN = (
-    "o.own",
+    "a.along",
     "t.own",
-    "a.along",
-    "u.along",
     "a.across0",
     "t.diag",
+    "u.along",
+    "o.own",
     "u.across0",
     "a.across1",
+    "t.set0",
     "a.across2",
-    "t.set0",
+    "bias",
+    "t.set1",
     "a.across3",
-    "bias",
-    "d.along",
     "a.onward0",
     "a.onward1",
+    "d.along",
+    "turn",
     "a.onward2",
-    "t.set1",
+    "t.set2",
+    "a.onward3",
+    "t.set3",
     "o.diag",
-    "a.onward3",
     "a.beside",
-    "t.set2",
     "u.across1",
     "u.across2",
-    "turn",
-    "t.set3",
     "a.opposite",
+    "u.across3",
     "t.last",
+    "u.onward0",
+    "o.set0",
     "vec",
+    "u.onward1",
     "a.last",
     "project",
-    "u.across3",
-    "o.set0",
+    "d.across1",
     "p0",
     "p1",
     "p2",
-    "d.across1",
     "p3",
+    "u.onward2",
     "attend",
-    "u.onward0",
+    "d.across2",
+    "d.across0",
     "a0",
     "a1",
     "a2",
-    "u.onward2",
+    "u.onward3",
     "a3",
-    "d.across2",
-    "u.onward1",
-    "u.onward3",
+    "o.set1",
+    "o.set2",
     "a4",
-    "o.set1",
     "a5",
     "a6",
-    "o.set2",
     "a7",
+    "o.set3",
     "a8",
+    "u.beside",
     "a9",
-    "o.set3",
-    "u.beside",
-    "d.across0",
     "a10",
+    "d.across3",
+    "d.onward0",
+    "o.last",
     "a11",
-    "o.last",
     "mix",
-    "d.across3",
     "d.onward2",
+    "u.opposite",
     "m0",
-    "u.opposite",
+    "d.onward1",
     "m1",
     "m2",
     "m3",
-    "d.onward0",
-    "d.onward1",
     "u.last",
     "widen",
     "w0",
     "w1",
+    "d.onward3",
     "w2",
-    "d.onward3",
     "w3",
+    "d.beside",
     "w4",
-    "d.beside",
     "w5",
     "w6",
     "w7",
@@ -1002,87 +1008,87 @@
     "d.second0",
     "ld",
     "w0",
+    "w1",
     "d.second1",
-    "w1",
     "w2",
-    "d.second2",
     "w3",
     "wu0",
+    "d.second2",
     "wu1",
+    "wu2",
     "d.third0",
-    "wu2",
+    "u.first",
     "bc",
-    "u.first",
     "d.third1",
     "n0",
     "n1",
+    "misc",
+    "g0",
     "u.second0",
     "u.second1",
-    "misc",
-    "d.second3",
-    "g0",
-    "d.fourth",
+    "rd",
     "u.second2",
-    "rd",
     "u.second3",
     "wo0",
+    "d.second3",
+    "o.first",
     "a0",
+    "d.fourth",
     "a1",
-    "o.first",
+    "a2",
+    "a3",
+    "u.third1",
     "u.third0",
-    "a2",
-    "u.third1",
-    "a3",
     "a4",
+    "o.second0",
     "a5",
     "a6",
-    "o.second0",
     "a7",
-    "u.fourth",
     "wm0",
     "wm1",
+    "u.fourth",
     "wm2",
+    "m.first",
+    "o.third1",
     "o.third0",
-    "o.third1",
-    "m.first",
     "a8",
     "m.second0",
     "a9",
+    "a10",
     "m.second1",
     "m.second2",
-    "a10",
     "a11",
+    "wr0",
+    "o.fourth",
     "m.third1",
+    "m.second3",
     "m.third0",
-    "m.second3",
-    "wr0",
     "wr1",
     "wr2",
     "r.first",
-    "o.fourth",
     "vec",
+    "d.trade",
     "r.second0",
-    "t.first",
-    "u.trade",
     "m.fourth",
     "b0",
+    "t.first",
+    "r.third0",
     "r.third1",
-    "r.third0",
     "t.second0",
+    "u.trade",
+    "r.fourth",
+    "d.whole",
+    "t.third1",
+    "o.trade",
+    "t.third0",
+    "u.whole",
     "b1",
-    "r.fourth",
-    "t.third0",
-    "d.trade",
-    "t.third1",
+    "m.trade",
     "t.fourth",
-    "u.whole",
-    "o.trade",
     "r.trade",
-    "d.whole",
-    "m.trade",
     "t.trade",
+    "r.whole",
     "m.whole",
-    "r.whole",
     "o.whole",
     "t.whole",
     "end",
@@ -1196,10 +1202,9 @@
     codes[rows, pl.ds(columns, 128)] = code.astype(jnp.bfloat16)
 
 
-def dot_codes(r, p, context, d_context, codes):
-    rows = part_of(r, SEQ)
+def dot_codes(p, context, d_context, codes):
     columns = part_of(p, 128)
-    both = context[rows, columns].astype(jnp.float32) * d_context[rows, columns].astype(jnp.float32)
+    both = context[:, columns].astype(jnp.float32) * d_context[:, columns].astype(jnp.float32)
     first, second = two_parts(both)
     shape = (128, 128)
     other = low_head(shape) != (lax.broadcasted_iota(jnp.int32, shape, 0) < HEAD)
@@ -1207,9 +1212,9 @@
     total = dotted(first.astype(jnp.bfloat16), other, 1, 0)
     total = total + dotted(second.astype(jnp.bfloat16), other, 1, 0)
     first, second = two_parts(total)
-    lane = lanes_in_head((SEQ, 128))
+    lane = lanes_in_head(total.shape)
     code = jnp.where(lane == PARTS, first, jnp.where(lane == PARTS + 1, second, 0.0))
-    codes[rows, columns] = code.astype(jnp.bfloat16)
+    codes[:, columns] = code.astype(jnp.bfloat16)
 
 
 def pick_head(masks, j, value, code):
@@ -1279,55 +1284,56 @@
     stage[part_of(links.c, rows), :] = src[:, part_of(links.c, columns)]
 
 
-def passage_loss(r, similar, live_row, teacher_index, teacher_table):
+def passage_loss(similar, live, teacher_index, teacher_table):
+    rows_dev = similar.shape[0] // QLEN
     scores = similar * (1.0 / SOFTNESS)
     inside, shares, student, teacher = [], [], [], []
     for p in range(NPASS):
-        member = live_row == float(p + 1)
+        member = live == float(p + 1)
         masked = jnp.where(member, scores, MASK_FILL)
         peak = jnp.max(masked, -1, keepdims=True)
         shifted = jnp.exp(masked - peak)
         total = jnp.sum(shifted, -1, keepdims=True)
         inside.append(jnp.where(member, shifted, 0.0))
         shares.append(1.0 / total)
-        student.append(SOFTNESS * jnp.sum(peak + jnp.log(total), axis=0, keepdims=True))
-        teacher.append(jnp.full((1, 1), teacher_table[teacher_index[r, p]], jnp.float32))
+        sums = peak + jnp.log(total)
+        student.append(
+            [
+                SOFTNESS * jnp.sum(sums[r * QLEN : (r + 1) * QLEN], axis=0, keepdims=True)
+                for r in range(rows_dev)
+            ]
+        )
+        teacher.append(
+            [
+                jnp.full((1, 1), teacher_table[teacher_index[r, p]], jnp.float32)
+                for r in range(rows_dev)
+            ]
+        )
 
     def log_softmax(values):
         peak = functools.reduce(jnp.maximum, values)
         total = sum(jnp.exp(value - peak) for value in values)
         return [value - peak - jnp.log(total) for value in values]
 
-    student = log_softmax(student)
-    teacher = log_softmax(teacher)
-    loss = sum(jnp.exp(t) * (t - s) for t, s in zip(teacher, student))
+    losses, slopes = [], []
+    for r in range(rows_dev):
+        ours = log_softmax([row[r] for row in student])
+        theirs = log_softmax([row[r] for row in teacher])
+        losses.append(sum(jnp.exp(t) * (t - s) for t, s in zip(theirs, ours)))
+        slopes.append([jnp.broadcast_to(jnp.exp(s) - jnp.exp(t), (QLEN, 1)) for t, s in zip(theirs, ours)])
     d_similar = sum(
-        part * (share * (jnp.exp(s) - jnp.exp(t)))
-        for part, share, s, t in zip(inside, shares, student, teacher)
-    )
-    return loss, d_similar
+        part * (share * jnp.concatenate([row[p] for row in slopes], axis=0))
+        for p, (part, share) in enumerate(zip(inside, shares))
+    )
+    return losses, d_similar
 
 
 def first_kernel(*refs):
-    (
-        tokens,
-        w_query,
-        w_key,
-        w_value,
-        w_out,
-        w_up,
-        w_down,
-        w_proj,
-        *vector_refs,
-        b_up,
-        segment_ids,
-        row_lengths,
-        teacher_index,
-        teacher_table,
-    ) = refs[:21]
+    given = refs[:18]
+    row_lengths, teacher_index, teacher_table = refs[18:21]
     (
         losses,
-        embeddings,
+        embeddings_hbm,
         attn_hbm,
         up_hbm,
         down_hbm,
@@ -1341,10 +1347,10 @@
         d_branch_hbm,
         grad_down_hbm,
         codes_hbm,
-        scaled_one,
-        vectors,
-        grad_vectors,
-        grad_proj,
+        scaled_one_hbm,
+        vectors_hbm,
+        grad_vectors_hbm,
+        grad_proj_hbm,
     ) = refs[21:40]
     (
         attn_mat,
@@ -1368,9 +1374,8 @@
         stage_down,
         proj,
         up_bias,
-        normed_two,
         scaled_two,
-        low_two,
+        d_raw,
         codes,
         segments,
         sends,
@@ -1379,10 +1384,41 @@
         half_recvs,
         local_sems,
         grad_sems,
+        embeddings,
+        scaled_one,
+        vectors,
+        grad_vectors,
+        grad_proj,
+        given_sems,
+        *taken,
     ) = refs[40:]
+    (
+        tokens,
+        w_query,
+        w_key,
+        w_value,
+        w_out,
+        w_up,
+        w_down,
+        w_proj,
+        *vector_refs,
+        b_up,
+        segment_ids,
+    ) = taken
     count = tokens.shape[0]
     rows_dev = count // SEQ
     links = Links()
+    links.hail()
+    loads = [
+        pltpu.make_async_copy(src, dst, given_sems.at[index])
+        for index, (src, dst) in enumerate(zip(given, taken))
+    ]
+    later = (0, len(loads) - 1)
+    for index, load in enumerate(loads):
+        if index not in later:
+            load.start()
+    for index in later:
+        loads[index].start()
 
     def gather(kind, block, group, stage):
         return kind(links, block, sends, recvs, group).join_from(
@@ -1402,6 +1438,9 @@
         copy.start()
         kept.append(copy)
 
+    for index, load in enumerate(loads):
+        if index not in later:
+            load.wait()
     for index, ref in enumerate((w_query, w_key, w_value)):
         cat_attn[:, index * WIDTH : (index + 1) * WIDTH] = ref[...]
     own_small = tiny.block(links.c, own_chip, 1)
@@ -1416,8 +1455,10 @@
     halves(links, w_out, stage_out, half_sends, half_recvs, 1)
     halves(links, w_up, stage_up, half_sends, half_recvs, 2)
     halves(links, w_down, stage_down, half_sends, half_recvs, 3)
-    plan = Plan(FIRST_PLAN, {"a": attn, "o": out, "u": up, "d": down, "t": tiny})
+    plan = Plan(FIRST_PLAN, {"a": attn, "o": out, "u": up, "d": down, "t": tiny, "l": links})
     plan.until("bias")
+    for index in later:
+        loads[index].wait()
     live_rows = []
     for r in range(rows_dev):
         segment, live = segment_forms(segment_ids, row_lengths, r)
@@ -1437,6 +1478,7 @@
         both = [small_all[c, r // 4, r % 4, 0:24, :] for c in range(2)]
         both = jnp.concatenate(both, axis=0)
         proj[r * 48 : (r + 1) * 48, :] = both.astype(jnp.bfloat16)
+    keep(vectors, vectors_hbm)
     plan.until("project")
 
     def project(step):
@@ -1472,6 +1514,7 @@
 
     plan.loop("m", 0, count // CHUNK, mix)
     keep(normed_one, normed_one_hbm)
+    keep(scaled_one, scaled_one_hbm)
     keep(low_one, low_one_hbm)
     plan.until("widen")
     keep(up_mat, up_hbm)
@@ -1490,41 +1533,55 @@
     keep(down_mat, down_hbm)
 
     grad_vectors[...] = jnp.zeros_like(grad_vectors)
-    grad_proj[...] = jnp.zeros_like(grad_proj)
     for r in range(rows_dev):
-
         rows = slice(r * SEQ, (r + 1) * SEQ)
         mixed = dotted(activated[rows, :], down_mat[...], 1, 0) + vectors[5:6, :]
         mixed = mixed + (normed_one[rows, :] * vectors[3:4, :] + vectors[4:5, :])
         normed, scaled = norm_parts(mixed)
-        normed_two[...] = normed
-        scaled_two[...] = jnp.broadcast_to(scaled, (SEQ, 128))
-        low_two[...] = (normed * vectors[6:7, :] + vectors[7:8, :]).astype(jnp.bfloat16)
-        raw = dotted(low_two[...], proj[...], 1, 0)
-        inverse = lax.rsqrt(jnp.sum(raw * raw, -1, keepdims=True) + UNIT_EPS)
-        embedded = raw * inverse
-        embeddings[r] = embedded
-        low_embed = embedded.astype(jnp.bfloat16)
-        similar = dotted(low_embed[0:QLEN], low_embed, 1, 1)
-        loss, d_similar = passage_loss(r, similar, live_rows[r], teacher_index, teacher_table)
-        losses[r] = loss[0, 0]
-        d_similar = d_similar.astype(jnp.bfloat16)
-        d_embed = dotted(d_similar, low_embed[0:QLEN], 0, 0)
-        d_query = dotted(d_similar, low_embed, 1, 0)
-        d_embed = jnp.concatenate([d_embed[0:QLEN] + d_query, d_embed[QLEN:]], axis=0)
-        along = jnp.sum(d_embed * embedded, -1, keepdims=True)
-        d_raw = (inverse * (d_embed - embedded * along)).astype(jnp.bfloat16)
-        grad_proj[...] += dotted(low_two[...], d_raw, 0, 0)
-        d_hidden = dotted(d_raw, proj[...], 1, 1)
-        normed = normed_two[...]
-        d_mixed = norm_back(d_hidden, normed, scaled_two[:, 0:1], vectors[6:7, :])
+        d_mid[rows, :] = normed
+        scaled_two[rows, :] = jnp.broadcast_to(scaled, (SEQ, 128))
+        d_branch[rows, :] = (normed * vectors[6:7, :] + vectors[7:8, :]).astype(jnp.bfloat16)
+    raw = dotted(d_branch[...], proj[...], 1, 0)
+    inverse = lax.rsqrt(jnp.sum(raw * raw, -1, keepdims=True) + UNIT_EPS)
+    embedded = raw * inverse
+    embeddings[...] = embedded.reshape(rows_dev, SEQ, EMBED)
+    keep(embeddings, embeddings_hbm)
+    low_embed = embedded.astype(jnp.bfloat16)
+    starts = [r * SEQ for r in range(rows_dev)]
+    heads = [low_embed[start : start + QLEN] for start in starts]
+    wholes = [low_embed[start : start + SEQ] for start in starts]
+    similar = jnp.concatenate([dotted(h, w, 1, 1) for h, w in zip(heads, wholes)], axis=0)
+    live = jnp.concatenate([jnp.broadcast_to(row, (QLEN, SEQ)) for row in live_rows], axis=0)
+    row_losses, d_similar = passage_loss(similar, live, teacher_index, teacher_table)
+    for r in range(rows_dev):
+        losses[r] = row_losses[r][0, 0]
+    d_similar = d_similar.astype(jnp.bfloat16)
+    d_parts = []
+    for r in range(rows_dev):
+        d_row = d_similar[r * QLEN : (r + 1) * QLEN]
+        d_whole = dotted(d_row, heads[r], 0, 0)
+        d_parts += [d_whole[0:QLEN] + dotted(d_row, wholes[r], 1, 0), d_whole[QLEN:]]
+    d_embed = jnp.concatenate(d_parts, axis=0)
+    along = jnp.sum(d_embed * embedded, -1, keepdims=True)
+    d_raw[...] = (inverse * (d_embed - embedded * along)).astype(jnp.bfloat16)
+    grad_proj[...] = dotted(d_branch[...], d_raw[...], 0, 0)
+    keep(grad_proj, grad_proj_hbm)
+
+    def unmix(step, carry):
+        rows = part_of(step, CHUNK)
+        d_hidden = dotted(d_raw[rows, :], proj[...], 1, 1)
+        normed = d_mid[rows, :]
+        d_mixed = norm_back(d_hidden, normed, scaled_two[rows, 0:1], vectors[6:7, :])
         low_mixed = d_mixed.astype(jnp.bfloat16)
-        rows = slice(r * SEQ, (r + 1) * SEQ)
         d_mid[rows, :] = d_mixed
         d_branch[rows, :] = low_mixed
         grad_vectors[5:6, :] += jnp.sum(low_mixed.astype(jnp.float32), 0, keepdims=True)
         grad_vectors[6:7, :] += jnp.sum(d_hidden * normed, 0, keepdims=True)
         grad_vectors[7:8, :] += jnp.sum(d_hidden, 0, keepdims=True)
+        return carry
+
+    lax.fori_loop(0, count // CHUNK, unmix, 0)
+    keep(grad_vectors, grad_vectors_hbm)
     keep(d_mid, d_mid_hbm)
     keep(d_branch, d_branch_hbm)
 
@@ -1557,7 +1614,6 @@
 def run_first(tokens, weights, vectors, segment_ids, row_lengths, teacher_index, teacher_table):
     count = tokens.shape[0]
     rows_dev = count // SEQ
-    vmem = pl.BlockSpec(memory_space=pltpu.VMEM)
     smem = pl.BlockSpec(memory_space=pltpu.SMEM)
     anywhere = pl.BlockSpec(memory_space=pl.ANY)
     low = jnp.bfloat16
@@ -1589,8 +1645,8 @@
             array(wide, 8, WIDTH),
             array(wide, WIDTH, EMBED),
         ],
-        in_specs=[vmem] * 18 + [smem] * 3,
-        out_specs=[smem, vmem] + [anywhere] * 13 + [vmem] * 4,
+        in_specs=[anywhere] * 18 + [smem] * 3,
+        out_specs=[smem] + [anywhere] * 18,
         scratch_shapes=[
             pltpu.VMEM((4, 4, 48, HIDDEN), low),
             pltpu.VMEM((WIDTH, HIDDEN), low),
@@ -1613,18 +1669,24 @@
             pltpu.VMEM((192, WIDTH // 2), wide),
             pltpu.VMEM((WIDTH, EMBED), low),
             pltpu.VMEM((8, HIDDEN), wide),
-            pltpu.VMEM((SEQ, WIDTH), wide),
-            pltpu.VMEM((SEQ, 128), wide),
-            pltpu.VMEM((SEQ, WIDTH), low),
+            pltpu.VMEM((count, 128), wide),
+            pltpu.VMEM((count, EMBED), low),
             pltpu.VMEM((count, WIDTH), low),
             pltpu.VMEM((count, 128), low),
             pltpu.SemaphoreType.DMA((5, Gather.SEMS)),
             pltpu.SemaphoreType.DMA((5, Gather.SEMS)),
             pltpu.SemaphoreType.DMA((4,)),
             pltpu.SemaphoreType.DMA((4,)),
-            pltpu.SemaphoreType.DMA((13,)),
+            pltpu.SemaphoreType.DMA((18,)),
             pltpu.SemaphoreType.DMA((2,)),
-        ],
+            pltpu.VMEM((rows_dev, SEQ, EMBED), wide),
+            pltpu.VMEM((count, 128), wide),
+            pltpu.VMEM((8, WIDTH), wide),
+            pltpu.VMEM((8, WIDTH), wide),
+            pltpu.VMEM((WIDTH, EMBED), wide),
+            pltpu.SemaphoreType.DMA((18,)),
+        ]
+        + [pltpu.VMEM(a.shape, a.dtype) for a in (tokens, *weights, *vectors, segment_ids)],
         compiler_params=pltpu.CompilerParams(
             collective_id=0, has_side_effects=True, vmem_limit_bytes=62 * 2**20
         ),
@@ -1647,11 +1709,11 @@
         d_branch_hbm,
         grad_down_hbm,
         codes_hbm,
-        scaled_one,
-        vectors,
-        part_vectors,
-        grad_proj,
-        segment_ids,
+        scaled_one_hbm,
+        vectors_hbm,
+        part_vectors_hbm,
+        grad_proj_hbm,
+        segment_ids_hbm,
         row_lengths,
     ) = refs[:19]
     (
@@ -1675,11 +1737,16 @@
         recvs,
         local_sems,
         slope_sems,
+        down_sems,
         qkv_sems,
         grad_sems,
         key_code,
         value_code,
         lows,
+        scaled_one,
+        vectors,
+        grad_proj,
+        segment_ids,
         *rest,
     ) = refs[23:]
     held = [rest[6 * i : 6 * i + 6] for i in range(6)]
@@ -1690,8 +1757,8 @@
     c = links.c
 
     def scatter(block, rows, group, deliver, mine=None):
-        def own(chip):
-            return block(c, chip, 1)
+        def own(chip, units):
+            return block(c, chip, units)
 
         own = own if mine is None else mine
         fin = fins[group] if group < 5 else None
@@ -1699,8 +1766,8 @@
             links, block, own, rows, held[group], fin, deliver, sends, recvs, group, group in (2, 4, 5)
         )
 
-    def down_mine(chip):
-        return part_down.at[part_of(chip, 192), :]
+    def down_mine(chip, units):
+        return part_down.at[pl.ds(pl.multiple_of(chip * 192, 192), units * 192), :]
 
     def halves_to(ref, start, columns):
         def deliver(low, high):
@@ -1743,18 +1810,26 @@
             copy.wait()
 
     plan = Plan(
-        LAST_PLAN, {"d": down, "u": up, "o": out, "m": most, "r": rest_of, "t": tiny}
+        LAST_PLAN,
+        {"d": down, "u": up, "o": out, "m": most, "r": rest_of, "t": tiny, "l": links},
     )
     plan.until("pre")
+    links.hail()
     first_loads = [
         load(d_branch_hbm, d_branch, 0),
         load(grad_down_hbm.at[:, part_of(c, WIDTH // 2)], part_down, 1),
     ]
+    side_loads = [
+        load(segment_ids_hbm, segment_ids, 11),
+        load(grad_proj_hbm, grad_proj, 12),
+        load(part_vectors_hbm, grad_vectors, 13),
+        load(vectors_hbm, vectors, 14),
+        load(scaled_one_hbm, scaled_one, 15),
+    ]
     attn_load = load(attn_hbm, attn_mat, 3)
-    start(first_loads)
+    start(first_loads + side_loads[:2])
     links.greet()
     wait(first_loads[1:])
-    grad_vectors[...] = part_vectors[...]
     ones = jnp.ones((8, count), jnp.bfloat16)
 
     def slope_load(step):
@@ -1782,10 +1857,16 @@
         return attn_mat[:, :, :, start : start + columns].reshape(WIDTH, columns)
 
     def feed_forward(up_mat, down_mat, normed_one):
-        ahead = [load(down_hbm, down_mat, 5)]
-        start(ahead)
+        def down_load(step):
+            rows = part_of(step, WIDTH)
+            return pltpu.make_async_copy(
+                down_hbm.at[rows, :], down_mat.at[rows, :], down_sems.at[step]
+            )
+
         for step in range(quarters):
+            down_load(step).start()
             slope_load(step).start()
+        start(side_loads[2:])
         middle = [
             load(low_one_hbm, low_one, 6),
             load(up_hbm, up_mat, 7),
@@ -1793,10 +1874,23 @@
             load(normed_one_hbm, normed_one, 9),
         ]
         plan.until("ld")
-        wait(first_loads[:1] + ahead)
+        wait(side_loads[:2])
+        for r in range(rows_dev):
+            _, live = segment_forms(segment_ids, row_lengths, r)
+            key_code[r * SEQ : (r + 1) * SEQ, :] = key_codes(live)
+        low = low_head((SEQ, 128))
+        lows[0] = jnp.where(low, 1.0, 0.0).astype(jnp.bfloat16)
+        lows[1] = jnp.where(low, 0.0, 1.0).astype(jnp.bfloat16)
+        lane = lanes_in_head((SEQ, 128))
+        parts = (lane == PARTS) | (lane == PARTS + 1)
+        value_code[...] = jnp.where(parts, 1.0, 0.0).astype(jnp.bfloat16)
+        for i in range(SHARDS):
+            small_all[i % 2, i // 2, 0:24, :] = grad_proj[i * 24 : (i + 1) * 24, :]
+        wait(first_loads[:1])
 
         def widen(step):
             columns = part_of(step, WIDTH)
+            down_load(step).wait()
             slope_load(step).wait()
             grad = dotted(d_branch[...], down_mat[columns, :], 1, 1)
             wide[:, columns] = (grad * wide[:, columns].astype(jnp.float32)).astype(jnp.bfloat16)
@@ -1818,7 +1912,7 @@
         for index in range(4):
             columns = slice(index * WIDTH, (index + 1) * WIDTH)
             grad_up_bias[:, columns] = dotted(ones, wide[:, columns], 1, 0)
-        wait(middle[1:])
+        wait(middle[1:] + side_loads[2:])
 
         def narrow(step):
             rows = part_of(step, HALF)
@@ -1849,15 +1943,6 @@
         start(loads)
         plan.until("misc")
         grad_vectors[2:3, :] = dotted(ones, d_branch[...], 1, 0)[0:1]
-        for r in range(rows_dev):
-            _, live = segment_forms(segment_ids, row_lengths, r)
-            key_code[r * SEQ : (r + 1) * SEQ, :] = key_codes(live)
-        low = low_head((SEQ, 128))
-        lows[0] = jnp.where(low, 1.0, 0.0).astype(jnp.bfloat16)
-        lows[1] = jnp.where(low, 0.0, 1.0).astype(jnp.bfloat16)
-        lane = lanes_in_head((SEQ, 128))
-        parts = (lane == PARTS) | (lane == PARTS + 1)
-        value_code[...] = jnp.where(parts, 1.0, 0.0).astype(jnp.bfloat16)
         attn_load.wait()
 
         plan.until("g0")
@@ -1866,11 +1951,11 @@
 
         wait(loads[:1])
 
-        def gather_dots(item, carry):
-            dot_codes(lax.rem(item, rows_dev), lax.div(item, rows_dev), context, d_context, low_one)
+        def gather_dots(p, carry):
+            dot_codes(p, context, d_context, low_one)
             return carry
 
-        lax.fori_loop(0, rows_dev * PAIRS, gather_dots, 0)
+        lax.fori_loop(0, PAIRS, gather_dots, 0)
         up.settle()
 
         plan.until("wo0")
@@ -1918,7 +2003,6 @@
     tiles = [grad_up_bias[:, i * 128 : (i + 1) * 128] for i in range(HIDDEN // 128)]
     for i, part in enumerate(pick_lanes(tiles, 96, SHARDS)):
         small_all[i % 2, i // 2, 32:40, :] = part
-        small_all[i % 2, i // 2, 0:24, :] = grad_proj[i * 24 : (i + 1) * 24, :]
 
     def back(step):
         rows = part_of(step, HALF)
@@ -1963,7 +2047,7 @@
             array(96, WIDTH),
             array(SMALL, 128),
         ],
-        in_specs=[anywhere] * 13 + [vmem] * 5 + [smem],
+        in_specs=[anywhere] * 18 + [smem],
         out_specs=[anywhere] + [vmem] * 3,
         scratch_shapes=[
             pltpu.VMEM((4, 4, 48, HIDDEN), low),
@@ -1978,13 +2062,18 @@
             pltpu.VMEM((8, HIDDEN), wide),
             pltpu.SemaphoreType.DMA((6, Scatter.SEMS)),
             pltpu.SemaphoreType.DMA((6, Scatter.SEMS)),
-            pltpu.SemaphoreType.DMA((11,)),
+            pltpu.SemaphoreType.DMA((16,)),
+            pltpu.SemaphoreType.DMA((HIDDEN // WIDTH,)),
             pltpu.SemaphoreType.DMA((HIDDEN // WIDTH,)),
             pltpu.SemaphoreType.DMA((count // HALF,)),
             pltpu.SemaphoreType.DMA((count // HALF,)),
             pltpu.VMEM((count, 128), low),
             pltpu.VMEM((SEQ, 128), low),
             pltpu.VMEM((2, SEQ, 128), low),
+            pltpu.VMEM((count, 128), wide),
+            pltpu.VMEM((8, WIDTH), wide),
+            pltpu.VMEM((WIDTH, EMBED), wide),
+            pltpu.VMEM((rows_dev, SEQ), jnp.int32),
         ]
         + buffers,
         compiler_params=pltpu.CompilerParams(
@@ -1995,16 +2084,17 @@
 
 
 def pass_kernel(*refs):
-    sources, losses = refs[:5], refs[5]
-    grad_tokens, embeddings, query, key, value, out, up, down, proj, *vectors = refs[6:23]
-    up_bias, own_losses = refs[23:25]
-    held, (in_sems, out_sems) = refs[25:30], refs[30:]
-    pieces = 4
+    sources, targets = refs[:6], refs[6:25]
+    held, ready = refs[25:31], refs[31:40]
+    in_sems, out_sems = refs[40:]
+    grad_tokens, embeddings, query, key, value, out, up, down, proj = targets[:9]
+    rows, down_in, small_in, losses_in = held[2:]
+    pieces = 8
     through = []
     for src, mid, dst in zip(sources[:2], held[:2], (grad_tokens, embeddings)):
-        rows = src.shape[0] // pieces
+        size = src.shape[0] // pieces
         for piece in range(pieces):
-            part = pl.ds(piece * rows, rows)
+            part = pl.ds(piece * size, size)
             index = len(through)
             through.append(
                 (
@@ -2022,44 +2112,49 @@
         here.start()
     for copy in small:
         copy.wait()
-    rows, down_in, small_in = held[2:]
-    for index, ref in enumerate((query, key, value, out)):
-        ref[...] = rows[:, index * WIDTH : (index + 1) * WIDTH]
-    up[...] = rows[:, HIDDEN:]
-    down[...] = down_in[...]
-    proj[...] = small_in[0:24, :]
-    for index, ref in enumerate(vectors):
+    for index, ref in enumerate(ready[:8]):
         ref[...] = small_in[24 + index : 25 + index, 0:24].reshape(24)
-    up_bias[...] = small_in[32:33, 0:96].reshape(96)
-    for index in range(losses.shape[0]):
-        own_losses[index] = losses[index]
+    ready[8][...] = small_in[32:33, 0:96].reshape(96)
+    made = [
+        (rows.at[:, index * WIDTH : (index + 1) * WIDTH], ref)
+        for index, ref in enumerate((query, key, value, out))
+    ]
+    made += [(rows.at[:, HIDDEN:], up), (down_in, down), (small_in.at[0:24, :], proj)]
+    made += list(zip(ready, targets[9:18])) + [(losses_in, targets[18])]
+    outs = [
+        pltpu.make_async_copy(mid, dst, out_sems.at[2 * pieces + index])
+        for index, (mid, dst) in enumerate(made)
+    ]
+    for copy in outs:
+        copy.start()
     for here, there in through:
         here.wait()
         there.start()
+    for copy in outs:
+        copy.wait()
     for _, there in through:
         there.wait()
 
 
 def run_pass(*arrays):
-    vmem = pl.BlockSpec(memory_space=pltpu.VMEM)
-    smem = pl.BlockSpec(memory_space=pltpu.SMEM)
     anywhere = pl.BlockSpec(memory_space=pl.ANY)
 
     def array(*shape):
         return jax.ShapeDtypeStruct(shape, jnp.float32)
 
     whole = [array(*a.shape) for a in arrays]
+    vectors = [array(24)] * 8 + [array(96)]
     return pl.pallas_call(
         pass_kernel,
         out_shape=whole[:2]
         + [array(24, WIDTH)] * 4
         + [array(24, HIDDEN), array(96, WIDTH), array(24, EMBED)]
-        + [array(24)] * 8
-        + [array(96), whole[-1]],
-        in_specs=[anywhere] * 5 + [smem],
-        out_specs=[anywhere] * 2 + [vmem] * 16 + [smem],
-        scratch_shapes=[pltpu.VMEM(a.shape, a.dtype) for a in arrays[:5]]
-        + [pltpu.SemaphoreType.DMA((11,)), pltpu.SemaphoreType.DMA((8,))],
+        + vectors
+        + [whole[-1]],
+        in_specs=[anywhere] * 6,
+        out_specs=[anywhere] * 19,
+        scratch_shapes=[pltpu.VMEM(a.shape, a.dtype) for a in (*arrays, *vectors)]
+        + [pltpu.SemaphoreType.DMA((20,)), pltpu.SemaphoreType.DMA((33,))],
         compiler_params=pltpu.CompilerParams(vmem_limit_bytes=62 * 2**20),
         name="hand_over",
     )(*arrays)

time: 179 us -> 175 us (0.978)
  Pallas kernels: 178 us -> 174 us
    pallas_call x1, Pallas kernels: 93.9 us -> 90.2 us  [run_first(): pl.pallas_call(first_kernel, out_shape=[array(wide, rows_dev), array(wide...]
where the time goes in v4:
time: 175 us
  Pallas kernels  174 us (99%)
    pallas_call x1, Pallas kernels, run_first(): pl.pallas_call(first_kernel, out_shape=[array(wide, rows_dev), array(wide...  90.2 us
    pallas_call x1, Pallas kernels, run_last(): pl.pallas_call(last_kernel, out_shape=[array(count, WIDTH), array(24, 2 *...  79.9 us
    pallas_call x1, Pallas kernels, run_pass(): pl.pallas_call(pass_kernel, out_shape=whole[:2] + [array(24, WIDTH)] * 4...  3.89 us

profile of v4, /device:TPU:0, one launch (start us, length us, event | category | flops | bytes accessed | tf_op | source)
XLA Modules:
  0.0 174.8 jit_solution(532835096512579666)
XLA Ops:
  0.7 90.2 %forward_gather.1 = (f32[2]{0:T(128)}, f32[2,512,128]{2,1,0:T(8,128)}, bf16[4,4,48,3072]{3,2,1,0:T(8,128)(2,1)}, bf16[768,3072]{1,0:T(8,128)(2,1)}, bf16[3072,76...) custom-call(bf16[1024,768]{1,0:T(8,128)(2,1)} %bitcast.4, ...), custom_call_target="tpu_custom_call" | custom-call | tf_op jit(solution)/shard_map/forward_gather/pallas_call | solution.py:1625
  90.8 79.9 %backward_scatter.1 = (f32[1024,768]{1,0:T(8,128)}, f32[24,6144]{1,0:T(8,128)}, f32[96,768]{1,0:T(8,128)}, f32[40,128]{1,0:T(8,128)}) custom-call(bf16[4,4,48,3072]{3,2,1,0:T(8,128)(2,1)} %get-tuple-element.61.refs_0_, bf16[768,3072]{1,0:T(8,128)(2,1)} %get-tuple-element.62.refs_1_, bf16[3072,768]{1,0:T(8,128)(2,1)} %get-tuple-element.63.refs_2_, ...), custom_call_target="tpu_custom_call" | custom-call | tf_op jit(solution)/shard_map/backward_scatter/pallas_call | solution.py:2042
  170.7 3.9 %hand_over.1 = (f32[1024,768]{1,0:T(8,128)}, f32[1024,128]{1,0:T(8,128)}, f32[24,768]{1,0:T(8,128)}, f32[24,768]{1,0:T(8,128)}, f32[24,768]{1,0:T(8,128)}, /*ind...) custom-call(f32[1024,768]{1,0:T(8,128)} %get-tuple-element.78.refs_0, ...), custom_call_target="tpu_custom_call" | custom-call | tf_op jit(solution)/shard_map/hand_over/pallas_call | solution.py:2147

commit v5 on v4

--- a/solution.py
+++ b/solution.py
@@ -713,6 +713,7 @@
         self.group = group
         n = links
         self.sent = []
+        self.gone = []
         self.once = whole
         self.span = 4 if whole else 2
         self.columns = (n.chip_d, n.chip_x, n.chip_y, n.chip_own)
@@ -728,6 +729,14 @@
 
     def ship(self, ends, index, target, there=None):
         self.links.send(ends, lambda: self.sems(index, there), target)
+        self.gone.append(self.links.started[-1])
+
+    def done(self):
+        for wait in self.gone:
+            if wait in self.links.started:
+                wait()
+                self.links.started.remove(wait)
+        self.gone = []
 
     def ship_part(self, start, count, ref, there, index, target):
         self.ship(
@@ -979,8 +988,6 @@
     "m0",
     "d.onward1",
     "m1",
-    "m2",
-    "m3",
     "u.last",
     "widen",
     "w0",
@@ -1005,89 +1012,92 @@
 LAST_PLAN = (
     "pre",
     "d.first",
-    "d.second0",
     "ld",
     "w0",
+    "d.second0",
     "w1",
     "d.second1",
     "w2",
     "w3",
     "wu0",
+    "wu1",
     "d.second2",
-    "wu1",
     "wu2",
     "d.third0",
     "u.first",
     "bc",
     "d.third1",
+    "d.second3",
     "n0",
+    "u.second0",
     "n1",
     "misc",
+    "u.second1",
     "g0",
-    "u.second0",
-    "u.second1",
+    "u.second2",
     "rd",
-    "u.second2",
     "u.second3",
     "wo0",
-    "d.second3",
+    "a0",
+    "a1",
+    "d.fourth",
+    "a2",
     "o.first",
-    "a0",
-    "d.fourth",
-    "a1",
-    "a2",
+    "u.third0",
     "a3",
     "u.third1",
-    "u.third0",
     "a4",
-    "o.second0",
     "a5",
     "a6",
     "a7",
     "wm0",
     "wm1",
+    "o.second0",
     "u.fourth",
     "wm2",
     "m.first",
+    "a8",
+    "o.third0",
     "o.third1",
-    "o.third0",
-    "a8",
+    "a9",
     "m.second0",
-    "a9",
     "a10",
     "m.second1",
     "m.second2",
     "a11",
     "wr0",
-    "o.fourth",
+    "m.third0",
     "m.third1",
     "m.second3",
-    "m.third0",
     "wr1",
+    "o.fourth",
     "wr2",
     "r.first",
     "vec",
+    "t.first",
+    "r.second0",
     "d.trade",
-    "r.second0",
     "m.fourth",
+    "r.third1",
+    "r.third0",
+    "t.second0",
+    "o.trade",
+    "r.fourth",
+    "u.trade",
+    "t.third0",
+    "t.third1",
     "b0",
-    "t.first",
-    "r.third0",
-    "r.third1",
-    "t.second0",
-    "u.trade",
-    "r.fourth",
+    "t.fourth",
+    "b1",
+    "d.done",
+    "o.done",
+    "u.done",
+    "r.trade",
+    "m.trade",
+    "t.trade",
+    "u.whole",
+    "r.whole",
     "d.whole",
-    "t.third1",
-    "o.trade",
-    "t.third0",
-    "u.whole",
-    "b1",
-    "m.trade",
-    "t.fourth",
-    "r.trade",
-    "t.trade",
-    "r.whole",
     "m.whole",
     "o.whole",
     "t.whole",
@@ -1504,15 +1514,15 @@
     keep(attn_mat, attn_hbm)
 
     def mix(step):
-        rows = part_of(step, CHUNK)
+        rows = part_of(step, HALF)
         weights = attn_mat[:, :, :, 3 * WIDTH :].reshape(WIDTH, WIDTH)
         mixed = dotted(context[rows, :], weights, 1, 0) + vectors[2:3, :]
         normed, scaled = norm_parts(tokens[rows, :].astype(jnp.float32) + mixed)
         normed_one[rows, :] = normed
-        scaled_one[rows, :] = jnp.broadcast_to(scaled, (CHUNK, 128))
+        scaled_one[rows, :] = jnp.broadcast_to(scaled, (HALF, 128))
         low_one[rows, :] = (normed * vectors[3:4, :] + vectors[4:5, :]).astype(jnp.bfloat16)
 
-    plan.loop("m", 0, count // CHUNK, mix)
+    plan.loop("m", 0, count // HALF, mix)
     keep(normed_one, normed_one_hbm)
     keep(scaled_one, scaled_one_hbm)
     keep(low_one, low_one_hbm)
@@ -1604,9 +1614,9 @@
 
     steps = HIDDEN // WIDTH
     lax.fori_loop(0, steps, weigh, 0)
+    links.finish()
     for step in (steps - 2, steps - 1):
         grad_copy(step, step % 2).wait()
-    links.finish()
     for copy in kept:
         copy.wait()
 
@@ -1718,9 +1728,9 @@
     ) = refs[:19]
     (
         grad_tokens_hbm,
-        own_rows,
-        own_down,
-        own_small,
+        own_rows_hbm,
+        own_down_hbm,
+        own_small_hbm,
     ) = refs[19:23]
     (
         attn_mat,
@@ -1747,6 +1757,9 @@
         vectors,
         grad_proj,
         segment_ids,
+        own_rows,
+        own_down,
+        own_small,
         *rest,
     ) = refs[23:]
     held = [rest[6 * i : 6 * i + 6] for i in range(6)]
@@ -2012,15 +2025,21 @@
 
     plan.loop("b", 0, steps, back)
     plan.until("end")
+    stores = [
+        load(own_rows, own_rows_hbm, 16),
+        load(own_down, own_down_hbm, 17),
+        load(own_small, own_small_hbm, 18),
+    ]
+    start(stores)
+    links.finish()
     for step in range(steps):
         grad_store(step).wait()
-    links.finish()
+    wait(stores)
 
 
 def run_last(kept, segment_ids, row_lengths):
     count = kept[9].shape[0]
     rows_dev = count // SEQ
-    vmem = pl.BlockSpec(memory_space=pltpu.VMEM)
     smem = pl.BlockSpec(memory_space=pltpu.SMEM)
     anywhere = pl.BlockSpec(memory_space=pl.ANY)
     low = jnp.bfloat16
@@ -2048,7 +2067,7 @@
             array(SMALL, 128),
         ],
         in_specs=[anywhere] * 18 + [smem],
-        out_specs=[anywhere] + [vmem] * 3,
+        out_specs=[anywhere] * 4,
         scratch_shapes=[
             pltpu.VMEM((4, 4, 48, HIDDEN), low),
             pltpu.VMEM((WIDTH, HIDDEN), low),
@@ -2062,7 +2081,7 @@
             pltpu.VMEM((8, HIDDEN), wide),
             pltpu.SemaphoreType.DMA((6, Scatter.SEMS)),
             pltpu.SemaphoreType.DMA((6, Scatter.SEMS)),
-            pltpu.SemaphoreType.DMA((16,)),
+            pltpu.SemaphoreType.DMA((19,)),
             pltpu.SemaphoreType.DMA((HIDDEN // WIDTH,)),
             pltpu.SemaphoreType.DMA((HIDDEN // WIDTH,)),
             pltpu.SemaphoreType.DMA((count // HALF,)),
@@ -2074,6 +2093,9 @@
             pltpu.VMEM((8, WIDTH), wide),
             pltpu.VMEM((WIDTH, EMBED), wide),
             pltpu.VMEM((rows_dev, SEQ), jnp.int32),
+            pltpu.VMEM((24, 2 * HIDDEN), wide),
+            pltpu.VMEM((96, WIDTH), wide),
+            pltpu.VMEM((SMALL, 128), wide),
         ]
         + buffers,
         compiler_params=pltpu.CompilerParams(

time: 175 us -> 174 us (level)
  no operation moved by 1% of the time
where the time goes in v5:
time: 174 us
  Pallas kernels  173 us (99%)
    pallas_call x1, Pallas kernels, run_first(): pl.pallas_call(first_kernel, out_shape=[array(wide, rows_dev), array(wide...  89.9 us
    pallas_call x1, Pallas kernels, run_last(): pl.pallas_call(last_kernel, out_shape=[array(count, WIDTH), array(24, 2 *...  78.9 us
    pallas_call x1, Pallas kernels, run_pass(): pl.pallas_call(pass_kernel, out_shape=whole[:2] + [array(24, WIDTH)] * 4...  3.89 us

profile of v5, /device:TPU:0, one launch (start us, length us, event | category | flops | bytes accessed | tf_op | source)
XLA Modules:
  0.0 173.5 jit_solution(1932849501403450791)
XLA Ops:
  0.7 89.9 %forward_gather.1 = (f32[2]{0:T(128)}, f32[2,512,128]{2,1,0:T(8,128)}, bf16[4,4,48,3072]{3,2,1,0:T(8,128)(2,1)}, bf16[768,3072]{1,0:T(8,128)(2,1)}, bf16[3072,76...) custom-call(bf16[1024,768]{1,0:T(8,128)(2,1)} %bitcast.4, ...), custom_call_target="tpu_custom_call" | custom-call | tf_op jit(solution)/shard_map/forward_gather/pallas_call | solution.py:1635
  90.6 78.9 %backward_scatter.1 = (f32[1024,768]{1,0:T(8,128)}, f32[24,6144]{1,0:T(8,128)}, f32[96,768]{1,0:T(8,128)}, f32[40,128]{1,0:T(8,128)}) custom-call(bf16[4,4,48,3072]{3,2,1,0:T(8,128)(2,1)} %get-tuple-element.61.refs_0_, bf16[768,3072]{1,0:T(8,128)(2,1)} %get-tuple-element.62.refs_1_, bf16[3072,768]{1,0:T(8,128)(2,1)} %get-tuple-element.63.refs_2_, ...), custom_call_target="tpu_custom_call" | custom-call | tf_op jit(solution)/shard_map/backward_scatter/pallas_call | solution.py:2061
  169.4 3.9 %hand_over.1 = (f32[1024,768]{1,0:T(8,128)}, f32[1024,128]{1,0:T(8,128)}, f32[24,768]{1,0:T(8,128)}, f32[24,768]{1,0:T(8,128)}, f32[24,768]{1,0:T(8,128)}, /*ind...) custom-call(f32[1024,768]{1,0:T(8,128)} %get-tuple-element.78.refs_0, ...), custom_call_target="tpu_custom_call" | custom-call | tf_op jit(solution)/shard_map/hand_over/pallas_call | solution.py:2169

commit v6 on v5

--- a/solution.py
+++ b/solution.py
@@ -912,10 +912,6 @@
 
 def upright(row):
     return jnp.broadcast_to(row, (128, SEQ)).T[:, 0:1]
-
-
-def mask_of(rows_form, columns_form):
-    return jnp.where(upright(rows_form) == columns_form, 0.0, MASK_FILL)
 
 
 FIRST_PLAN = (
@@ -1185,28 +1181,32 @@
     return jnp.where(lane <= NPASS, hidden, parts).astype(jnp.bfloat16)
 
 
-def attend_pair(r, p, qkv, context, codes, bias, segments):
+def attend_pair(r, p, qkv, context, codes, segments, keys):
     rows = part_of(r, SEQ)
     columns = pl.multiple_of(p * 128, 128)
     query = qkv[rows, pl.ds(columns, 128)]
     key = qkv[rows, pl.ds(columns + WIDTH, 128)]
     value = qkv[rows, pl.ds(columns + 2 * WIDTH, 128)]
+    query_c, key_c = segments[rows, :], keys[rows, :]
     low = low_head((SEQ, 128))
-    zero = jnp.zeros_like(key)
-    outs, sums = [], []
+    one = jnp.ones_like(value)
+    outs, peaks = [], []
     for j in range(2):
-        key_j = jnp.where(low, key, zero) if j == 0 else jnp.where(low, zero, key)
-        scores = dotted(query, key_j, 1, 1) * EXP2_SCALE + bias[rows, 0:SEQ]
+        mine = low if j == 0 else ~low
+        scores = dotted(jnp.where(mine, query, query_c), jnp.where(mine, key, key_c), 1, 1)
         peak = jnp.max(scores, -1, keepdims=True)
-        shifted = jnp.exp2(scores - peak)
-        total = jnp.sum(shifted, -1, keepdims=True)
-        out = dotted(shifted.astype(jnp.bfloat16), value, 1, 0)
-        outs.append(out * (1.0 / total))
-        sums.append(peak + jnp.log2(total))
-    context[rows, pl.ds(columns, 128)] = jnp.where(low, outs[0], outs[1]).astype(jnp.bfloat16)
-    first, second, third = three_parts(jnp.where(low, sums[1], sums[0]) * (-1.0 / EXP2_SCALE))
+        shifted = jnp.exp2((scores - peak) * EXP2_SCALE).astype(jnp.bfloat16)
+        outs.append(dotted(shifted, jnp.where(mine, value, one), 1, 0))
+        peaks.append(peak)
+    total = jnp.where(low, outs[1], outs[0])
+    own = pltpu.roll(total, HEAD, 1)
+    context[rows, pl.ds(columns, 128)] = (
+        jnp.where(low, outs[0], outs[1]) * (1.0 / own)
+    ).astype(jnp.bfloat16)
+    logsum = jnp.where(low, peaks[1], peaks[0]) + jnp.log2(total) * (1.0 / EXP2_SCALE)
+    first, second, third = three_parts(-logsum)
     lane = lanes_in_head((SEQ, 128))
-    code = jnp.where(lane == PARTS + 2, third, segments[rows, :].astype(jnp.float32))
+    code = jnp.where(lane == PARTS + 2, third, query_c.astype(jnp.float32))
     code = jnp.where(lane == PARTS + 1, second, code)
     code = jnp.where(lane == PARTS, first, code)
     codes[rows, pl.ds(columns, 128)] = code.astype(jnp.bfloat16)
@@ -1388,6 +1388,7 @@
         d_raw,
         codes,
         segments,
+        keys,
         sends,
         recvs,
         half_sends,
@@ -1473,7 +1474,7 @@
     for r in range(rows_dev):
         segment, live = segment_forms(segment_ids, row_lengths, r)
         live_rows.append(live)
-        d_mid[r * SEQ : (r + 1) * SEQ, 0:SEQ] = mask_of(segment, live)
+        keys[r * SEQ : (r + 1) * SEQ, :] = key_codes(live)
         segments[r * SEQ : (r + 1) * SEQ, :] = query_codes(segment)
     plan.until("turn")
     turned[...] = tokens[...].T
@@ -1505,7 +1506,7 @@
 
     def attend(item):
         r, p = lax.div(item, PAIRS), lax.rem(item, PAIRS)
-        attend_pair(r, p, qkv, context, codes, d_mid, segments)
+        attend_pair(r, p, qkv, context, codes, segments, keys)
 
     plan.loop("a", 0, rows_dev * PAIRS, attend)
     keep(context, context_hbm)
@@ -1682,6 +1683,7 @@
             pltpu.VMEM((count, 128), wide),
             pltpu.VMEM((count, EMBED), low),
             pltpu.VMEM((count, WIDTH), low),
+            pltpu.VMEM((count, 128), low),
             pltpu.VMEM((count, 128), low),
             pltpu.SemaphoreType.DMA((5, Gather.SEMS)),
             pltpu.SemaphoreType.DMA((5, Gather.SEMS)),

time: 174 us -> 173 us (level)
  no operation moved by 1% of the time
where the time goes in v6:
time: 173 us
  Pallas kernels  172 us (99%)
    pallas_call x1, Pallas kernels, run_first(): pl.pallas_call(first_kernel, out_shape=[array(wide, rows_dev), array(wide...  89.5 us
    pallas_call x1, Pallas kernels, run_last(): pl.pallas_call(last_kernel, out_shape=[array(count, WIDTH), array(24, 2 *...  79 us
    pallas_call x1, Pallas kernels, run_pass(): pl.pallas_call(pass_kernel, out_shape=whole[:2] + [array(24, WIDTH)] * 4...  3.89 us

profile of v6, /device:TPU:0, one launch (start us, length us, event | category | flops | bytes accessed | tf_op | source)
XLA Modules:
  0.0 173.3 jit_solution(9409903010331010212)
XLA Ops:
  0.7 89.5 %forward_gather.1 = (f32[2]{0:T(128)}, f32[2,512,128]{2,1,0:T(8,128)}, bf16[4,4,48,3072]{3,2,1,0:T(8,128)(2,1)}, bf16[768,3072]{1,0:T(8,128)(2,1)}, bf16[3072,76...) custom-call(bf16[1024,768]{1,0:T(8,128)(2,1)} %bitcast.4, ...), custom_call_target="tpu_custom_call" | custom-call | tf_op jit(solution)/shard_map/forward_gather/pallas_call | solution.py:1636
  90.2 79.0 %backward_scatter.1 = (f32[1024,768]{1,0:T(8,128)}, f32[24,6144]{1,0:T(8,128)}, f32[96,768]{1,0:T(8,128)}, f32[40,128]{1,0:T(8,128)}) custom-call(bf16[4,4,48,3072]{3,2,1,0:T(8,128)(2,1)} %get-tuple-element.61.refs_0_, bf16[768,3072]{1,0:T(8,128)(2,1)} %get-tuple-element.62.refs_1_, bf16[3072,768]{1,0:T(8,128)(2,1)} %get-tuple-element.63.refs_2_, ...), custom_call_target="tpu_custom_call" | custom-call | tf_op jit(solution)/shard_map/backward_scatter/pallas_call | solution.py:2063
  169.2 3.9 %hand_over.1 = (f32[1024,768]{1,0:T(8,128)}, f32[1024,128]{1,0:T(8,128)}, f32[24,768]{1,0:T(8,128)}, f32[24,768]{1,0:T(8,128)}, f32[24,768]{1,0:T(8,128)}, /*ind...) custom-call(f32[1024,768]{1,0:T(8,128)} %get-tuple-element.78.refs_0, ...), custom_call_target="tpu_custom_call" | custom-call | tf_op jit(solution)/shard_map/hand_over/pallas_call | solution.py:2171
